TPU v7x, 32 devices: a whole 2x2x4 slice. The times are simulated.
32 devices in a mesh: groups: 2 (over x), ctx: 16 (over z, y, core).
Axes of the slice: x: 2, y: 2, z: 4, core: 2. Of those that a mesh axis runs over, the one named last changes fastest.
Arguments:
- queries: bfloat16 [4096, 36864], P(('groups', 'ctx')), parts along dimension 0, may hold values from -6 to 40
- prefix_latent: bfloat16 [32, 36864], P(('groups', 'ctx')), parts along dimension 0, may hold values from -6 to 6
- window_latent: bfloat16 [64, 36864], P(('groups', 'ctx')), parts along dimension 0, may hold values from -6 to 120
- index_queries: bfloat16 [4096, 8192], P(('groups', 'ctx')), parts along dimension 0, may hold values from -6 to 6
- index_weights: float32 [4096, 64], P(('groups', 'ctx')), parts along dimension 0, may hold values from -0.75 to 0.75
- prefix_index_keys: bfloat16 [2048, 128], P(('groups', 'ctx')), parts along dimension 0, may hold values from -6 to 6
- window_index_keys: bfloat16 [4096, 128], P(('groups', 'ctx')), parts along dimension 0, may hold values from -6 to 6
- picks: int32 [64, 12], P(('groups', 'ctx')), parts along dimension 0, may hold values from 0 to 47, as said below
Outputs:
- attention: bfloat16 [4096, 32768], P(('groups', 'ctx')), parts along dimension 0
- prefix_index: float32 [4096, 1024], P(('groups', 'ctx')), parts along dimension 0
- window_index: float32 [4096, 2048], P(('groups', 'ctx')), parts along dimension 0
There are 2 independent parts, one for each index of `groups`. A program takes and returns all parts, laid end to end along the dimension named above; each array names one. Nothing has to cross between parts.
Inputs may be any that keep to these rules, and one draw needn't show every extreme that they name: `picks`: each row names 12 distinct key blocks, never one after its own query block, and always its own. The query blocks that lie on one index of ctx name together at most one key block held by any other index of ctx (a prefix block and window blocks lie where their rows are placed).
All inputs are finite; a program needn't handle non-finite values.
Results may differ from a plain program's by a relative error of at most 0.008.
Values may be sent and summed in bfloat16 or wider, within the bound.
No kernel may reach another device: no remote copies, remote signals or barrier semaphores. Data moves between devices by JAX's collectives and lax.ppermute only.
A program may use at most 192 MiB of HBM per device.

v0:
```python
import jax
import jax.numpy as jnp
from jax import lax
from jax.sharding import PartitionSpec as P

H = 64
LAT = 512
ROPE = 64
IH = 64
IDX = 128
BLK = 64


score_scale = 192.0 ** (-0.5)
masked_low = -1e30


def attend(query_rows, kv_rows, own_mask):
    rows_each = query_rows.shape[0]
    scores = (
        jnp.einsum("qhd,kd->qhk", query_rows, kv_rows, preferred_element_type=jnp.float32)
        * score_scale
    )
    query_place = jnp.arange(rows_each, dtype=jnp.int32)
    key_place = jnp.arange(BLK, dtype=jnp.int32)
    allowed = jnp.logical_or(
        jnp.logical_not(own_mask)[None, :, None],
        key_place[None, None, :] <= query_place[:, None, None],
    )
    allowed = allowed.reshape(rows_each, 1, kv_rows.shape[0])
    scores = jnp.where(allowed, scores, masked_low)
    peak = jnp.max(scores, axis=-1, keepdims=True)
    weights = jnp.exp(scores - peak)
    total = jnp.sum(weights, axis=-1, keepdims=True)
    probs = (weights / total).astype(jnp.bfloat16)
    return jnp.einsum(
        "qhk,kd->qhd", probs, kv_rows[:, :LAT], preferred_element_type=jnp.float32
    ).astype(jnp.bfloat16)


def body(
    queries,
    prefix_latent,
    window_latent,
    index_queries,
    index_weights,
    prefix_index_keys,
    window_index_keys,
    picks,
):
    row_width = LAT + ROPE
    own_index = lax.axis_index("ctx")
    devices = lax.axis_size("ctx")
    tok_rows = queries.shape[0]
    per_device = tok_rows // BLK
    span = BLK + tok_rows
    local_keys = jnp.concatenate([prefix_index_keys, window_index_keys], 0)
    index_rows = index_queries.reshape(tok_rows, IH, IDX)
    query_place = own_index * tok_rows + jnp.arange(tok_rows, dtype=jnp.int32)
    start_pair = (
        jnp.zeros((tok_rows, devices * BLK), jnp.float32),
        jnp.zeros((tok_rows, devices * tok_rows), jnp.float32),
    )
    piece = lax.all_gather(local_keys, "ctx", axis=0, tiled=True)
    count = piece.shape[0] // span
    shards = piece.reshape(count, span, IDX)

    def one_shard(inner_carry, item):
        offset, shard_keys = item
        products = jnp.einsum(
            "qjd,kd->qjk", index_rows, shard_keys, preferred_element_type=jnp.float32
        ) * IDX ** (-0.5)
        value = jnp.sum(jax.nn.relu(products) * index_weights[:, :, None], axis=1)
        key_place = offset * tok_rows + jnp.arange(tok_rows, dtype=jnp.int32)
        window_part = jnp.where(key_place[None, :] <= query_place[:, None], value[:, BLK:], 0.0)
        zero_index = jnp.zeros((), jnp.int32)
        prefix_scores = lax.dynamic_update_slice(
            inner_carry[0], value[:, :BLK], (zero_index, offset * BLK)
        )
        window_scores = lax.dynamic_update_slice(
            inner_carry[1], window_part, (zero_index, offset * tok_rows)
        )
        return ((prefix_scores, window_scores), None)

    result_pair, unused = lax.scan(
        one_shard, start_pair, (jnp.arange(count, dtype=jnp.int32), shards)
    )
    prefix_index, window_index = result_pair
    every_prefix, every_window = (
        lax.all_gather(prefix_latent, "ctx", axis=0, tiled=True),
        lax.all_gather(window_latent, "ctx", axis=0, tiled=True),
    )
    table = jnp.concatenate([every_prefix, every_window], 0)
    query_rows = queries.reshape(per_device, BLK, H, row_width)
    pick_count = picks.shape[1]

    def one_block(item):
        rows_here, slot_row, pick_row, offset = item
        kv_rows = jnp.take(table, slot_row, axis=0).reshape(pick_count * BLK, row_width)
        own_mask = pick_row == devices + own_index * per_device + offset
        return attend(rows_here, kv_rows, own_mask)

    outputs = lax.map(
        one_block, (query_rows, picks, picks, jnp.arange(per_device, dtype=jnp.int32))
    )
    attention = outputs.reshape(tok_rows, H * LAT)
    return (attention, prefix_index, window_index)


def solution(mesh):
    placed = (
        P(("groups", "ctx"), None),
        P(("groups", "ctx"), None),
        P(("groups", "ctx"), None),
        P(("groups", "ctx"), None),
        P(("groups", "ctx"), None),
        P(("groups", "ctx"), None),
        P(("groups", "ctx"), None),
        P(("groups", "ctx"), None),
    )
    return jax.shard_map(
        body,
        mesh=mesh,
        in_specs=placed,
        out_specs=(
            P(("groups", "ctx"), None),
            P(("groups", "ctx"), None),
            P(("groups", "ctx"), None),
        ),
        check_vma=False,
    )
```

profile of v0, /device:TPU:0, one launch (start us, length us, event | category | flops | bytes accessed | tf_op | source)
XLA Modules:
  0.0 272.3 jit_solution(7436600398126679906)
XLA Ops:
  9.4 25.9 %all_gather.11 = bf16[3072,128]{1,0:T(8,128)(2,1)S(1)} all-gather(bf16[192,128]{1,0:T(8,128)(2,1)S(1)} %pad_maximum_fusion.1), channel_id=1, replica_groups=mesh['groups'=2,'ctx'=16] {'ctx'}, dimensions={0}, use_global_device_ids=true | all-gather | bytes 835584 | tf_op jit(solution)/shard_map/all_gather | solution.py:64
  35.4 3.2 %copy.21 = bf16[128,8192]{0,1:T(8,128)(2,1)S(1)} copy(bf16[128,8192]{1,0:T(8,128)(2,1)} %param.15) | data formatting | bytes 4194304 | tf_op args[3]
  38.6 2.9 %copy.22 = bf16[128,64,128]{2,0,1:T(8,128)(2,1)} copy(bf16[128,64,128]{0,2,1:T(8,128)(2,1)S(1)} %bitcast.65) | data formatting | bytes 4194304
  41.6 76.0 %while.26 = (s32[]{:T(128)}, f32[128,1024]{0,1:T(8,128)S(1)}, f32[128,2048]{1,0:T(8,128)S(1)}, bf16[16,192,128]{2,1,0:T(8,128)(2,1)S(1)}, bf16[128,64,128]{2,0,1...) while((s32[]{:T(128)}, f32[128,1024]{0,1:T(8,128)S(1)}, ...), condition=%wide.region_6.7_spmd.clone, body=%wide.region_4.6_spmd.clone.sunk | while | flops 408953088 | bytes 2738441 | solution.py:85
  42.9 2.6 multiply_reduce_fusion.2
  47.7 2.6 multiply_reduce_fusion.2
  52.5 2.6 multiply_reduce_fusion.2
  62.0 2.6 multiply_reduce_fusion.2
  66.7 2.6 multiply_reduce_fusion.2
  71.5 2.6 multiply_reduce_fusion.2
  76.2 2.6 multiply_reduce_fusion.2
  81.0 2.6 multiply_reduce_fusion.2
  85.7 2.6 multiply_reduce_fusion.2
  95.2 2.6 multiply_reduce_fusion.2
  99.9 2.6 multiply_reduce_fusion.2
  109.4 2.6 multiply_reduce_fusion.2
  114.2 2.6 multiply_reduce_fusion.2
  117.7 18.8 %reshape.142 = bf16[2,64,64,576]{3,2,1,0:T(8,128)(2,1)} reshape(bf16[128,36864]{1,0:T(8,128)(2,1)} %param.12) | data formatting | bytes 18874368 | tf_op jit(solution)/shard_map/reshape | solution.py:94
  137.5 4.0 %copy.32 = bf16[16,1,36864]{2,0,1:T(8,128)(2,1)} copy(bf16[16,1,36864]{2,1,0:T(2,128)(2,1)} %all-gather.5.cloned.1.call-done) | data formatting | bytes 2359296
  141.5 4.3 %reshape.157 = bf16[32,36864]{1,0:T(8,128)(2,1)} reshape(bf16[16,2,36864]{2,1,0:T(2,128)(2,1)} %all-gather.7.cloned.1.call-done) | data formatting | bytes 4718592
  148.5 104.3 %while.25 = (s32[]{:T(128)}, bf16[2,64,64,512]{3,2,1,0:T(8,128)(2,1)}, s32[2,12]{1,0:T(2,128)S(1)}, s32[2]{0:T(128)}, s32[]{:T(128)}, /*index=5*/bf16[2,64,64,57...) while((s32[]{:T(128)}, bf16[2,64,64,512]{3,2,1,0:T(8,128)(2,1)}, s32[2,12]{1,0:T(2,128)S(1)}, ...), condition=%wide.region_3.4_spmd, body=%wide.region_0.3_spmd.sunk | while | flops 6873257984 | bytes 68979128 | solution.py:103
  155.2 3.0 %select_n.93 = bf16[768,576]{1,0:T(8,128)(2,1)} reshape(bf16[12,36864]{1,0:T(8,128)(2,1)} %broadcast_select_fusion.2) | data formatting | bytes 1769472 | tf_op jit(solution)/shard_map/while/body/eval_jaxpr/jit(_take)/select_n | solution.py:99
  158.2 9.9 %fusion.38 = f32[64,64,768]{2,1,0:T(8,128)} fusion(bf16[2,64,64,576]{3,2,1,0:T(8,128)(2,1)} %get-tuple-element.343, s32[]{:T(128)S(6)} %copy.40, bf16[768,576]{1,0:T(8,128)(2,1)} %select_n.93), kind=kOutput, calls=%fused_computation.11.clone.1 | convolution fusion | flops 3623878656 | bytes 18808836 | tf_op jit(solution)/shard_map/while/body/eval_jaxpr/qhd,kd->qhk/dot_general | solution.py:21
  171.5 15.8 %fusion.39 = (f32[64,64]{1,0:T(8,128)}, f32[64,64,768]{2,1,0:T(8,128)}) fusion(f32[64,64,768]{2,1,0:T(8,128)} %fusion.38, pred[64,768]{1,0:T(8,128)(4,1)S(1)} %broadcast_or_fusion.2), kind=kOutput, calls=%fused_computation.46.clone.1 | output fusion | flops 18875136 | bytes 25231360 | tf_op jit(solution)/shard_map/while/body/eval_jaxpr/sub | solution.py:33
  187.3 3.0 %gather.13 = bf16[768,576]{1,0:T(8,128)(2,1)} reshape(bf16[12,36864]{1,0:T(8,128)(2,1)} %gather_fusion) | data formatting | bytes 1769472 | tf_op jit(solution)/shard_map/while/body/eval_jaxpr/jit(_take)/gather | solution.py:99
  190.5 10.2 %bitcast_dynamic-update-slice_fusion.2 = bf16[2,64,64,512]{3,2,1,0:T(8,128)(2,1)} fusion(bf16[2,64,64,512]{3,2,1,0:T(8,128)(2,1)} %get-tuple-element.331, s32[]{:T(128)S(6)} %copy.40, f32[64,64,768]{2,1,0:T(8,128)} %get-tuple-element.310, f32[64,64]{1,0:T(8,128)} %get-tuple-element.311, bf16[768,576]{1,0:T(8,128)(2,1)} %gather.13, ...), kind=kOutput, calls=%fused_computation.14.clone.1 | convolution fusion | flops 3230007296 | bytes 17597188 | tf_op jit(solution)/shard_map/while/body/eval_jaxpr/qhk,kd->qhd/dot_general | solution.py:36
  207.3 3.0 %select_n.93 = bf16[768,576]{1,0:T(8,128)(2,1)} reshape(bf16[12,36864]{1,0:T(8,128)(2,1)} %broadcast_select_fusion.2) | data formatting | bytes 1769472 | tf_op jit(solution)/shard_map/while/body/eval_jaxpr/jit(_take)/select_n | solution.py:99
  210.3 9.9 %fusion.38 = f32[64,64,768]{2,1,0:T(8,128)} fusion(bf16[2,64,64,576]{3,2,1,0:T(8,128)(2,1)} %get-tuple-element.343, s32[]{:T(128)S(6)} %copy.40, bf16[768,576]{1,0:T(8,128)(2,1)} %select_n.93), kind=kOutput, calls=%fused_computation.11.clone.1 | convolution fusion | flops 3623878656 | bytes 18808836 | tf_op jit(solution)/shard_map/while/body/eval_jaxpr/qhd,kd->qhk/dot_general | solution.py:21
  223.6 15.8 %fusion.39 = (f32[64,64]{1,0:T(8,128)}, f32[64,64,768]{2,1,0:T(8,128)}) fusion(f32[64,64,768]{2,1,0:T(8,128)} %fusion.38, pred[64,768]{1,0:T(8,128)(4,1)S(1)} %broadcast_or_fusion.2), kind=kOutput, calls=%fused_computation.46.clone.1 | output fusion | flops 18875136 | bytes 25231360 | tf_op jit(solution)/shard_map/while/body/eval_jaxpr/sub | solution.py:33
  239.4 3.0 %gather.13 = bf16[768,576]{1,0:T(8,128)(2,1)} reshape(bf16[12,36864]{1,0:T(8,128)(2,1)} %gather_fusion) | data formatting | bytes 1769472 | tf_op jit(solution)/shard_map/while/body/eval_jaxpr/jit(_take)/gather | solution.py:99
  242.6 10.2 %bitcast_dynamic-update-slice_fusion.2 = bf16[2,64,64,512]{3,2,1,0:T(8,128)(2,1)} fusion(bf16[2,64,64,512]{3,2,1,0:T(8,128)(2,1)} %get-tuple-element.331, s32[]{:T(128)S(6)} %copy.40, f32[64,64,768]{2,1,0:T(8,128)} %get-tuple-element.310, f32[64,64]{1,0:T(8,128)} %get-tuple-element.311, bf16[768,576]{1,0:T(8,128)(2,1)} %gather.13, ...), kind=kOutput, calls=%fused_computation.14.clone.1 | convolution fusion | flops 3230007296 | bytes 17597188 | tf_op jit(solution)/shard_map/while/body/eval_jaxpr/qhk,kd->qhd/dot_general | solution.py:36
  252.8 12.6 %copy.30 = bf16[16,8,64,512]{3,1,2,0:T(8,128)(2,1)} copy(bf16[16,8,64,512]{3,2,1,0:T(8,128)(2,1)} %bitcast.63) | data formatting | bytes 16777216
  (147 shorter events, 45.7 us)
Async XLA Ops:
  7.2 34.5 %copy-start.2 = (f32[128,64]{0,1:T(8,128)S(1)}, f32[128,64]{0,1:T(8,128)}, u32[]{:S(2)}) copy-start(f32[128,64]{0,1:T(8,128)} %param.16) | copy-start | bytes 98308
  7.2 130.3 %all-gather.5.cloned.1.call-start = ((), (), s32[]{:S(2)}) async-start(), calls=%async_computation | async-start | bytes 2506752 | tf_op jit(solution)/shard_map/all_gather | solution.py:90
  7.9 133.6 %all-gather.7.cloned.1.call-start = ((), (), s32[]{:S(2)}) async-start(), calls=%async_computation.1 | async-start | bytes 2506752 | tf_op jit(solution)/shard_map/all_gather | solution.py:91
  117.7 18.8 %copy-start = (f32[128,2048]{1,0:T(8,128)}, f32[128,2048]{1,0:T(8,128)S(1)}, u32[]{:S(2)}) copy-start(f32[128,2048]{1,0:T(8,128)S(1)} %get-tuple-element.181) | copy-start | bytes 3145732
  141.5 7.0 %copy-start.1 = (s32[2,12]{1,0:T(2,128)S(1)}, s32[2,12]{1,0:T(2,128)}, u32[]{:S(2)}) copy-start(s32[2,12]{1,0:T(2,128)} %param.19) | copy-start | bytes 292
Sparse Core Ops, SparseCore 0:
  10.3 45.9 all-gather.4
  58.6 41.1 all-gather.6
where the time goes:
time: 274 us; the launch traced here: 272 us
  local copies, waits for them, and re-layouts  83.4 us (30%)
  matrix products  81.8 us (30%)
  other arithmetic  42.6 us (16%)
  blocking collectives  25.9 us (9%)
  loops' own time  23 us (8%)
  between operations  14.1 us (5%)
    dot_general x16, matrix products, one_shard(): jnp.einsum('qjd,kd->qjk', index_rows, shard_keys, preferred_element_type=...  41.5 us
    sub x2, other arithmetic, attend(): weights = jnp.exp(scores - peak)  31.5 us
    unnamed x12, local copies, waits for them, and re-layouts  28 us
    all_gather x1, blocking collectives, body(): piece = lax.all_gather(local_keys, 'ctx', axis=0, tiled=True)  25.9 us
    another operation x1, loops' own time, body(): lax.scan(one_shard, start_pair, (jnp.arange(count, dtype=jnp.int32), shar...  21.6 us
    dot_general x2, matrix products, attend(): jnp.einsum('qhk,kd->qhd', probs, kv_rows[:, :LAT], preferred_element_type...  20.5 us
    dot_general x2, matrix products, attend(): jnp.einsum('qhd,kd->qhk', query_rows, kv_rows, preferred_element_type=jnp...  19.8 us
    reshape x1, local copies, waits for them, and re-layouts, body(): query_rows = queries.reshape(per_device, BLK, H, row_width)  18.8 us
  transfers between devices with their start and end apart: 2, of which 0 were waited for; matrix products, arithmetic and copies ran while one was open for 31% of the time, Pallas kernels for 0%

commit v1 on v0

v1 whole, which is shorter than its diff:
```python
import functools

import jax
import jax.numpy as jnp
from jax import lax
from jax.experimental import pallas as pl
from jax.experimental.pallas import tpu as pltpu
from jax.sharding import PartitionSpec as P

H = 64
LAT = 512
ROPE = 64
ROW = LAT + ROPE
WIDE = 640
IH = 64
IDX = 128
BLK = 64
LANES = 128
TILE = 256
TOK_TILE = 32
HEAD_STEP = 16
PAIRS = 8
GROUP = 8
LOW = -1.0e30
EXP2_SCALE = 192.0**-0.5 * 1.4426950408889634
VMEM = 48 * 2**20


def index_tile(iq_ref, wide_ref, keys):
    keys_t = keys.T
    rows = iq_ref.shape[0]
    parts = []
    for t0 in range(0, rows, TOK_TILE):
        acc = jnp.zeros((TOK_TILE, TILE), jnp.float32)
        for j0 in range(0, IH, HEAD_STEP):
            lhs = jnp.concatenate(
                [
                    iq_ref[t0 : t0 + TOK_TILE, j * IDX : (j + 1) * IDX]
                    for j in range(j0, j0 + HEAD_STEP)
                ],
                0,
            )
            prod = jnp.dot(lhs, keys_t, preferred_element_type=jnp.float32)
            for j in range(HEAD_STEP):
                weight = wide_ref[j0 + j, t0 : t0 + TOK_TILE, :]
                weight = jnp.concatenate([weight] * (TILE // LANES), 1)
                acc = acc + jnp.maximum(prod[j * TOK_TILE : (j + 1) * TOK_TILE], 0.0) * weight
        parts.append(acc)
    return jnp.concatenate(parts, 0)


def spread_weights(w_ref, wide_ref):
    for j in range(IH):
        wide_ref[j] = jnp.broadcast_to(w_ref[:, j : j + 1] * IDX**-0.5, wide_ref.shape[1:])


def index_near_kernel(rels, own_ref, iq_ref, w_ref, keys_ref, out_ref, wide_ref):
    own = own_ref[0]
    tok = iq_ref.shape[0]
    span = BLK + tok
    spread_weights(w_ref, wide_ref)

    @pl.loop(0, len(rels) // 2)
    def _(pair):
        first = keys_ref[pl.ds(pl.multiple_of(2 * pair * span + BLK, BLK), tok), :]
        second = keys_ref[pl.ds(pl.multiple_of((2 * pair + 1) * span + BLK, BLK), tok), :]
        value = index_tile(iq_ref, wide_ref, jnp.concatenate([first, second], 0))
        out_ref[2 * pair] = value[:, :LANES]
        out_ref[2 * pair + 1] = value[:, LANES:]


def index_far_kernel(
    near, far, own_ref, iq_ref, w_ref, near_ref, far_ref, done_ref, prefix_ref, window_ref,
    wide_ref, keys_ref, res_ref,
):
    own = own_ref[0]
    tok = iq_ref.shape[0]
    span = BLK + tok
    devices = len(near) + len(far)
    spread_weights(w_ref, wide_ref)
    for ref, rels in ((near_ref, near), (far_ref, far)):
        for n, rel in enumerate(rels):
            at = pl.multiple_of((own ^ rel) * BLK, BLK)
            keys_ref[pl.ds(at, BLK), :] = ref[n * span : n * span + BLK, :]
    base = devices * BLK
    for n in range(len(far)):
        keys_ref[base + n * tok : base + (n + 1) * tok, :] = far_ref[
            n * span + BLK : (n + 1) * span, :
        ]

    @pl.loop(0, keys_ref.shape[0] // TILE)
    def _(tile):
        keys = keys_ref[pl.ds(pl.multiple_of(tile * TILE, TILE), TILE), :]
        value = index_tile(iq_ref, wide_ref, keys)
        res_ref[2 * tile] = value[:, :LANES]
        res_ref[2 * tile + 1] = value[:, LANES:]

    for n in range(base // LANES):
        prefix_ref[:, n * LANES : (n + 1) * LANES] = res_ref[n]
    row = lax.broadcasted_iota(jnp.int32, (tok, LANES), 0)
    lane = lax.broadcasted_iota(jnp.int32, (tok, LANES), 1)
    for rels, ref, start in ((near, done_ref, 0), (far, res_ref, base // LANES)):
        for n, rel in enumerate(rels):
            other = own ^ rel
            seen = other * tok + lane <= own * tok + row
            window_ref[:, pl.ds(pl.multiple_of(other * tok, LANES), LANES)] = jnp.where(
                seen, ref[start + n], 0.0
            )


def attention_kernel(devices, own_ref, pick_ref, q_ref, *refs):
    shards = refs[:devices]
    out_ref, cache, raw, even_t, odd_t, need, sem = refs[devices:]
    block = pl.program_id(0)
    own = own_ref[0]
    picks = pick_ref.shape[1]

    def split(pick):
        window = pick - devices
        holder = jnp.where(window < 0, pick, window // 2)
        return holder ^ own, jnp.where(window < 0, 0, 1 + window % 2)

    def fetch(rel, inner, slot):
        return pltpu.make_async_copy(
            shards[rel].at[pl.ds(pl.multiple_of(inner * BLK, BLK), BLK)],
            cache.at[slot],
            sem.at[slot],
        )

    @pl.when((block == 0) & (pl.program_id(1) == 0))
    def _():
        for rel in range(devices):
            need[rel] = 0
        for b in range(pick_ref.shape[0]):
            for s in range(picks):
                rel, inner = split(pick_ref[b, s])
                need[rel] = inner
        for n in range(3):
            fetch(0, n, 0 if n == 0 else devices - 1 + n).start()
        for rel in range(1, devices):
            fetch(rel, need[rel], rel).start()
        for n in range(3):
            fetch(0, n, 0 if n == 0 else devices - 1 + n).wait()
        for rel in range(1, devices):
            fetch(rel, need[rel], rel).wait()

    @pl.when(pl.program_id(1) == 0)
    def _():
        own_pick = devices + own * 2 + block
        own_slot = jnp.int32(0)
        for s in range(picks):
            own_slot = jnp.where(pick_ref[block, s] == own_pick, s, own_slot)
        for s in range(picks):
            place = jnp.where(own_slot == s, picks - 1, own_slot if s == picks - 1 else s)
            rel, inner = split(pick_ref[block, s])
            slot = jnp.where((rel == 0) & (inner > 0), devices - 1 + inner, rel)
            raw[pl.ds(pl.multiple_of(place * BLK, BLK), BLK), :] = cache[slot]
        turned = raw[...].T
        even_t[...] = turned
        odd_t[0:ROPE] = turned[ROW:WIDE]
        odd_t[ROPE:WIDE] = turned[0:ROW]

    count = picks * BLK
    row = lax.broadcasted_iota(jnp.int32, (BLK, LANES), 0)
    lane = lax.broadcasted_iota(jnp.int32, (BLK, LANES), 1)
    allowed = jnp.concatenate([lane - BLK <= row] * GROUP, 0)

    def score(unit):
        odd, first = unit % 2, unit // 2 * GROUP
        lhs = jnp.concatenate(
            [
                q_ref[:, (first + g) * 2 * ROW + odd * LAT : (first + g) * 2 * ROW + odd * LAT + WIDE]
                for g in range(GROUP)
            ],
            0,
        )
        return jnp.dot(lhs, (odd_t if odd else even_t)[...], preferred_element_type=jnp.float32)

    def finish(unit, scores):
        odd, first = unit % 2, unit // 2 * GROUP
        last = jnp.where(allowed, scores[:, count - LANES :], LOW)
        scores = jnp.concatenate([scores[:, : count - LANES], last], 1)
        peak = jnp.max(scores, axis=1, keepdims=True)
        weights = jnp.exp2((scores - peak) * EXP2_SCALE)
        total = jnp.sum(weights, axis=1, keepdims=True)
        result = jnp.dot(
            weights.astype(jnp.bfloat16), raw[:, :LAT], preferred_element_type=jnp.float32
        )
        result = (result * (1.0 / total)).astype(jnp.bfloat16)
        for g in range(GROUP):
            at = (first + g) * 2 * LAT + odd * LAT
            out_ref[:, at : at + LAT] = result[g * BLK : (g + 1) * BLK]

    units = PAIRS // GROUP * 2
    scores = score(0)
    for unit in range(units):
        following = score(unit + 1) if unit + 1 < units else None
        finish(unit, scores)
        scores = following


def body(
    queries,
    prefix_latent,
    window_latent,
    index_queries,
    index_weights,
    prefix_index_keys,
    window_index_keys,
    picks,
):
    devices = lax.axis_size("ctx")
    own = lax.axis_index("ctx").astype(jnp.int32).reshape(1)
    tok = queries.shape[0]
    per_device = tok // BLK
    span = BLK + tok

    def swap(array, rel):
        return lax.ppermute(array, "ctx", [(i, i ^ rel) for i in range(devices)])

    line = list(range(0, devices, 4))
    keys = jnp.concatenate([prefix_index_keys, window_index_keys], 0)
    key_line = jnp.concatenate([keys] + [swap(keys, rel) for rel in line[1:]], 0)
    near_keys = jnp.concatenate([key_line, swap(key_line, 2)], 0)
    near = line + [rel + 2 for rel in line]
    far_keys = swap(near_keys, 1)
    far = [rel + 1 for rel in near]

    rows = jnp.concatenate([prefix_latent, window_latent], 0).reshape(3 * BLK, ROW)
    rows = jnp.pad(rows, ((0, 0), (0, WIDE - ROW)))
    shards = [None] * devices
    shards[0] = rows
    for rel in line[1:]:
        shards[rel] = swap(rows, rel)
    for rel in line:
        shards[rel + 2] = swap(shards[rel], 2)
    for rel in near:
        shards[rel + 1] = swap(shards[rel], 1)

    smem = pl.BlockSpec(memory_space=pltpu.SMEM)
    vmem = pl.BlockSpec(memory_space=pltpu.VMEM)
    hbm = pl.BlockSpec(memory_space=pl.ANY)
    params = pltpu.CompilerParams(vmem_limit_bytes=VMEM)
    done = pl.pallas_call(
        functools.partial(index_near_kernel, near),
        out_shape=jax.ShapeDtypeStruct((len(near), tok, LANES), jnp.float32),
        in_specs=[smem, vmem, vmem, vmem],
        out_specs=vmem,
        scratch_shapes=[pltpu.VMEM((IH, tok, LANES), jnp.float32)],
        compiler_params=params,
        cost_estimate=pl.CostEstimate(
            flops=2 * tok * IH * IDX * len(near) * tok * 4, bytes_accessed=2**22, transcendentals=0
        ),
    )(own, index_queries, index_weights, near_keys)
    total_keys = devices * BLK + len(far) * tok
    prefix_index, window_index = pl.pallas_call(
        functools.partial(index_far_kernel, near, far),
        out_shape=(
            jax.ShapeDtypeStruct((tok, devices * BLK), jnp.float32),
            jax.ShapeDtypeStruct((tok, devices * tok), jnp.float32),
        ),
        in_specs=[smem, vmem, vmem, vmem, vmem, vmem],
        out_specs=(vmem, vmem),
        scratch_shapes=[
            pltpu.VMEM((IH, tok, LANES), jnp.float32),
            pltpu.VMEM((total_keys, IDX), jnp.bfloat16),
            pltpu.VMEM((total_keys // LANES, tok, LANES), jnp.float32),
        ],
        compiler_params=params,
        cost_estimate=pl.CostEstimate(
            flops=2 * tok * IH * IDX * total_keys * 4, bytes_accessed=2**22, transcendentals=0
        ),
    )(own, index_queries, index_weights, near_keys, far_keys, done)

    count = picks.shape[1] * BLK
    attention = pl.pallas_call(
        functools.partial(attention_kernel, devices),
        grid_spec=pltpu.PrefetchScalarGridSpec(
            num_scalar_prefetch=2,
            grid=(per_device, H // 2 // PAIRS),
            in_specs=[pl.BlockSpec((BLK, PAIRS * 2 * ROW), lambda b, h, *_: (b, h))]
            + [hbm] * devices,
            out_specs=pl.BlockSpec((BLK, PAIRS * 2 * LAT), lambda b, h, *_: (b, h)),
            scratch_shapes=[
                pltpu.VMEM((devices + 2, BLK, WIDE), jnp.bfloat16),
                pltpu.VMEM((count, WIDE), jnp.bfloat16),
                pltpu.VMEM((WIDE, count), jnp.bfloat16),
                pltpu.VMEM((WIDE, count), jnp.bfloat16),
                pltpu.SMEM((devices,), jnp.int32),
                pltpu.SemaphoreType.DMA((devices + 2,)),
            ],
        ),
        out_shape=jax.ShapeDtypeStruct((tok, H * LAT), jnp.bfloat16),
        compiler_params=params,
        cost_estimate=pl.CostEstimate(
            flops=2 * tok * H * count * (WIDE + LAT), bytes_accessed=2**24, transcendentals=0
        ),
    )(own, picks, queries, *shards)
    return (attention, prefix_index, window_index)


def solution(mesh):
    placed = P(("groups", "ctx"), None)
    return jax.shard_map(
        body,
        mesh=mesh,
        in_specs=(placed,) * 8,
        out_specs=(placed,) * 3,
        check_vma=False,
    )
```

time: 274 us -> 92.5 us (0.34)
  matrix products: 81.8 us -> 0 us
  local copies, waits for them, and re-layouts: 83.4 us -> 4.36 us
  Pallas kernels: 0 us -> 45 us
  other arithmetic: 42.6 us -> 1.29 us
  blocking collectives: 25.9 us -> 0 us
  loops' own time: 23 us -> 0 us
  waiting for transfers between devices: 1.38 us -> 22.2 us
  starting transfers between devices: 0.08 us -> 18.4 us
  between operations: 14.1 us -> 0.77 us
    dot_general x20 -> x0, matrix products: 81.8 us -> none  [the longest x16 41.5 us: one_shard(): jnp.einsum('qjd,kd->qjk', index_rows, shard_keys, preferred_element_type=...]
    pallas_call x0 -> x3, Pallas kernels: none -> 45 us  [the longest x1 24.8 us: body(): pl.pallas_call(functools.partial(attention_kernel, devices), grid_spec=pl...]
    sub x2 -> x0, other arithmetic: 31.5 us -> none  [attend(): weights = jnp.exp(scores - peak)]
    all_gather x1 -> x0, blocking collectives: 25.9 us -> none  [body(): piece = lax.all_gather(local_keys, 'ctx', axis=0, tiled=True)]
    unnamed x12 -> x9, local copies, waits for them, and re-layouts: 28 us -> 3.99 us
    another operation x2 -> x0, loops' own time: 23 us -> none  [the longest x1 21.6 us: body(): lax.scan(one_shard, start_pair, (jnp.arange(count, dtype=jnp.int32), shar...]
    ppermute x0 -> x20, waiting for transfers between devices: none -> 22.2 us  [swap(): return lax.ppermute(array, 'ctx', [(i, i ^ rel) for i in range(devices)])]
    reshape x1, local copies, waits for them, and re-layouts: 18.8 us -> 0.3 us  [body(): jnp.concatenate([prefix_latent, window_latent], 0).reshape(3 * BLK, ROW)]
  transfers between devices with their start and end apart: 2 -> 20, of which waited for: 0 -> 6; matrix products, arithmetic and copies ran while one was open for 31% -> 3% of each run, Pallas kernels for 0% -> 22%
where the time goes in v1:
time: 92.5 us; the launch traced here: 92.1 us
  Pallas kernels  45 us (49%)
  waiting for transfers between devices  22.2 us (24%)
  starting transfers between devices  18.4 us (20%)
  local copies, waits for them, and re-layouts  4.36 us (5%)
  other arithmetic  1.29 us (1%)
    pallas_call x1, Pallas kernels, body(): pl.pallas_call(functools.partial(attention_kernel, devices), grid_spec=pl...  24.8 us
    ppermute x20, waiting for transfers between devices, swap(): return lax.ppermute(array, 'ctx', [(i, i ^ rel) for i in range(devices)])  22.2 us
    ppermute x20, starting transfers between devices, swap(): return lax.ppermute(array, 'ctx', [(i, i ^ rel) for i in range(devices)])  18.4 us
    pallas_call x1, Pallas kernels, body(): pl.pallas_call(functools.partial(index_far_kernel, near, far), out_shape=...  13.5 us
    pallas_call x1, Pallas kernels, body(): pl.pallas_call(functools.partial(index_near_kernel, near), out_shape=jax....  6.77 us
    unnamed x9, local copies, waits for them, and re-layouts  3.99 us
  transfers between devices with their start and end apart: 20, of which 6 were waited for; matrix products, arithmetic and copies ran while one was open for 3% of the time, Pallas kernels for 22%

profile of v1, /device:TPU:0, one launch (start us, length us, event | category | flops | bytes accessed | tf_op | source)
XLA Modules:
  0.0 92.1 jit_solution(13086158640868494300)
XLA Ops:
  0.6 0.7 constant_dynamic-update-slice_fusion.6
  1.4 0.8 constant_dynamic-update-slice_fusion.5
  2.1 3.1 %collective-permute-start.15 = (bf16[192,128]{1,0:T(8,128)(2,1)S(1)}, bf16[192,128]{1,0:T(8,128)(2,1)S(1)}, u32[]{:S(2)}, u32[]{:S(2)}) collective-permute-start(bf16[192,128]{1,0:T(8,128)(2,1)S(1)} %get-tuple-element.14), channel_id=1, source_target_pairs={{0,4},{1,5},{2,6},{3,7},{4,0},{5,1},{6,2},{7,3},{8,12},{9,13},{10,... | collective-permute-start | bytes 147464 | tf_op jit(solution)/shard_map/ppermute | solution.py:219
  5.2 2.6 %collective-permute-start.16 = (bf16[192,128]{1,0:T(8,128)(2,1)S(1)}, bf16[192,128]{1,0:T(8,128)(2,1)S(1)}, u32[]{:S(2)}, u32[]{:S(2)}) collective-permute-start(bf16[192,128]{1,0:T(8,128)(2,1)S(1)} %get-tuple-element.14), channel_id=1, source_target_pairs={{0,8},{1,9},{2,10},{3,11},{4,12},{5,13},{6,14},{7,15},{8,0},{9,1},... | collective-permute-start | bytes 147464 | tf_op jit(solution)/shard_map/ppermute | solution.py:219
  7.8 0.0 collective-permute-start.17
  7.8 1.3 %pad_maximum_fusion = bf16[3,36864]{1,0:T(4,128)(2,1)S(1)} fusion(bf16[2,36864]{1,0:T(2,128)(2,1)} %param.10, bf16[1,36864]{1,0:T(2,128)(2,1)} %param.9), kind=kLoop, calls=%fused_computation | loop fusion | flops 442368 | bytes 442368 | tf_op jit(solution)/shard_map/concatenate | solution.py:229
  9.1 0.3 reshape.13
  9.5 1.8 %collective-permute-start.1 = (bf16[192,640]{1,0:T(8,128)(2,1)S(1)}, bf16[192,640]{1,0:T(8,128)(2,1)S(1)}, u32[]{:S(2)}, u32[]{:S(2)}) collective-permute-start(bf16[192,640]{1,0:T(8,128)(2,1)S(1)} %pad.4.refs_0_), channel_id=1, source_target_pairs={{0,2},{1,3},{2,0},{3,1},{4,6},{5,7},{6,4},{7,5},{8,10},{9,11},{10,... | collective-permute-start | bytes 737288 | tf_op jit(solution)/shard_map/ppermute | solution.py:219
  11.3 2.4 %collective-permute-done.17 = bf16[192,128]{1,0:T(8,128)(2,1)S(1)} collective-permute-done((bf16[192,128]{1,0:T(8,128)(2,1)S(1)}, bf16[192,128]{1,0:T(8,128)(2,1)S(1)}, u32[]{:S(2)}, u32[]{:S(2)}) %collective-permute-start.17) | collective-permute-done | bytes 49184 | tf_op jit(solution)/shard_map/ppermute | solution.py:219
  13.7 1.6 %collective-permute-start.18 = (bf16[768,128]{1,0:T(8,128)(2,1)S(1)}, bf16[768,128]{1,0:T(8,128)(2,1)S(1)}, u32[]{:S(2)}, u32[]{:S(2)}) collective-permute-start(bf16[768,128]{1,0:T(8,128)(2,1)S(1)} %get-tuple-element.7), channel_id=1, source_target_pairs={{0,2},{1,3},{2,0},{3,1},{4,6},{5,7},{6,4},{7,5},{8,10},{9,11},{10,... | collective-permute-start | bytes 589832 | tf_op jit(solution)/shard_map/ppermute | solution.py:219
  15.3 0.0 collective-permute-start
  15.3 0.0 collective-permute-start.3
  15.3 1.3 %collective-permute-start.7 = (bf16[192,640]{1,0:T(8,128)(2,1)S(1)}, bf16[192,640]{1,0:T(8,128)(2,1)S(1)}, u32[]{:S(2)}, u32[]{:S(2)}) collective-permute-start(bf16[192,640]{1,0:T(8,128)(2,1)S(1)} %pad.4.refs_0_), channel_id=1, source_target_pairs={{0,8},{1,9},{2,10},{3,11},{4,12},{5,13},{6,14},{7,15},{8,0},{9,1},... | collective-permute-start | bytes 737288 | tf_op jit(solution)/shard_map/ppermute | solution.py:219
  16.6 1.8 %collective-permute-done.1.refs_2_ = bf16[192,640]{1,0:T(8,128)(2,1)S(1)} collective-permute-done((bf16[192,640]{1,0:T(8,128)(2,1)S(1)}, bf16[192,640]{1,0:T(8,128)(2,1)S(1)}, u32[]{:S(2)}, u32[]{:S(2)}) %collective-permute-start.1) | collective-permute-done | bytes 245792 | tf_op jit(solution)/shard_map/ppermute | solution.py:219
  18.4 3.8 %collective-permute-start.11 = (bf16[192,640]{1,0:T(8,128)(2,1)S(1)}, bf16[192,640]{1,0:T(8,128)(2,1)S(1)}, u32[]{:S(2)}, u32[]{:S(2)}) collective-permute-start(bf16[192,640]{1,0:T(8,128)(2,1)S(1)} %pad.4.refs_0_), channel_id=1, source_target_pairs={{0,12},{1,13},{2,14},{3,15},{4,8},{5,9},{6,10},{7,11},{8,4},{9,5},... | collective-permute-start | bytes 737288 | tf_op jit(solution)/shard_map/ppermute | solution.py:219
  22.3 0.8 copy.12.w_ref
  23.2 0.6 collective-permute-start.19
  23.7 4.1 %collective-permute-done.3.refs_4_ = bf16[192,640]{1,0:T(8,128)(2,1)S(1)} collective-permute-done((bf16[192,640]{1,0:T(8,128)(2,1)S(1)}, bf16[192,640]{1,0:T(8,128)(2,1)S(1)}, u32[]{:S(2)}, u32[]{:S(2)}) %collective-permute-start.3) | collective-permute-done | bytes 245792 | tf_op jit(solution)/shard_map/ppermute | solution.py:219
  27.9 7.6 %collective-permute-done.7.refs_8_ = bf16[192,640]{1,0:T(8,128)(2,1)S(1)} collective-permute-done((bf16[192,640]{1,0:T(8,128)(2,1)S(1)}, bf16[192,640]{1,0:T(8,128)(2,1)S(1)}, u32[]{:S(2)}, u32[]{:S(2)}) %collective-permute-start.7) | collective-permute-done | bytes 245792 | tf_op jit(solution)/shard_map/ppermute | solution.py:219
  35.5 0.5 collective-permute-start.5
  36.1 1.5 %collective-permute-start.9 = (bf16[192,640]{1,0:T(8,128)(2,1)S(1)}, bf16[192,640]{1,0:T(8,128)(2,1)S(1)}, u32[]{:S(2)}, u32[]{:S(2)}) collective-permute-start(bf16[192,640]{1,0:T(8,128)(2,1)S(1)} %collective-permute-done.7.refs_8_), channel_id=1, source_target_pairs={{0,2},{1,3},{2,0},{3,1},{4,6},{5,7},{6,4},{7,5},{8,10},{9,11},{10,... | collective-permute-start | bytes 737288 | tf_op jit(solution)/shard_map/ppermute | solution.py:219
  37.6 0.5 collective-permute-start.13
  38.1 1.6 %copy-done = bf16[128,8192]{1,0:T(8,128)(2,1)S(1)} copy-done((bf16[128,8192]{1,0:T(8,128)(2,1)S(1)}, bf16[128,8192]{1,0:T(8,128)(2,1)}, u32[]{:S(2)}) %copy-start) | copy-done | bytes 2097176
  39.7 6.8 %shard_map.104.done_ref = f32[8,128,128]{2,1,0:T(8,128)S(1)} custom-call(s32[1]{0:T(128)} %bitcast.own_ref, bf16[128,8192]{1,0:T(8,128)(2,1)S(1)} %copy-done, f32[128,64]{1,0:T(8,128)S(1)} %copy.12.w_ref, bf16[1536,128]{1,0:T(8,128)(2,1)S(1)} %constant_dynamic-update-slice_fusion.7.keys_ref.near_ref), custom_call_target="tpu_custom_call" | custom-call | flops 8589934592 | bytes 4194304 | tf_op jit(solution)/shard_map/pallas_call | solution.py:244
  46.5 0.0 copy-start.1
  46.5 0.1 collective-permute-start.8
  46.6 0.5 collective-permute-start.12
  47.1 2.6 %collective-permute-done.9.refs_10_ = bf16[192,640]{1,0:T(8,128)(2,1)S(1)} collective-permute-done((bf16[192,640]{1,0:T(8,128)(2,1)S(1)}, bf16[192,640]{1,0:T(8,128)(2,1)S(1)}, u32[]{:S(2)}, u32[]{:S(2)}) %collective-permute-start.9) | collective-permute-done | bytes 245792 | tf_op jit(solution)/shard_map/ppermute | solution.py:219
  49.7 3.6 %collective-permute-done.13.refs_14_ = bf16[192,640]{1,0:T(8,128)(2,1)S(1)} collective-permute-done((bf16[192,640]{1,0:T(8,128)(2,1)S(1)}, bf16[192,640]{1,0:T(8,128)(2,1)S(1)}, u32[]{:S(2)}, u32[]{:S(2)}) %collective-permute-start.13) | collective-permute-done | bytes 245792 | tf_op jit(solution)/shard_map/ppermute | solution.py:219
  53.3 0.5 collective-permute-start.14
  53.8 13.5 %shard_map.105 = (f32[128,1024]{1,0:T(8,128)}, f32[128,2048]{1,0:T(8,128)}) custom-call(s32[1]{0:T(128)} %bitcast.own_ref, bf16[128,8192]{1,0:T(8,128)(2,1)S(1)} %copy-done, f32[128,64]{1,0:T(8,128)S(1)} %copy.12.w_ref, bf16[1536,128]{1,0:T(8,128)(2,1)S(1)} %constant_dynamic-update-slice_fusion.7.keys_ref.near_ref, ...), custom_call_target="tpu_custom_call" | custom-call | flops 17179869184 | bytes 4194304 | tf_op jit(solution)/shard_map/pallas_call | solution.py:256
  67.3 24.8 %shard_map.103 = bf16[128,32768]{1,0:T(8,128)(2,1)} custom-call(s32[1]{0:T(128)} %bitcast.own_ref, s32[2,12]{1,0:T(2,128)S(1)} %copy-done.1, bf16[128,36864]{1,0:T(8,128)(2,1)} %q_ref.1, bf16[192,640]{1,0:T(8,128)(2,1)S(1)} %pad.4.refs_0_, bf16[192,640]{1,0:T(8,128)(2,1)S(1)} %collective-permute-done.refs_1_, ...), custom_call_target="tpu_custom_call" | custom-call | flops 14495514624 | bytes 16777216 | tf_op jit(solution)/shard_map/pallas_call | solution.py:276
  (25 shorter events, 0.2 us)
Async XLA Ops:
  2.1 9.1 %collective-permute-start.15 = (bf16[192,128]{1,0:T(8,128)(2,1)S(1)}, bf16[192,128]{1,0:T(8,128)(2,1)S(1)}, u32[]{:S(2)}, u32[]{:S(2)}) collective-permute-start(bf16[192,128]{1,0:T(8,128)(2,1)S(1)} %get-tuple-element.14), channel_id=1, source_target_pairs={{0,4},{1,5},{2,6},{3,7},{4,0},{5,1},{6,2},{7,3},{8,12},{9,13},{10,... | collective-permute-start | bytes 147464 | tf_op jit(solution)/shard_map/ppermute | solution.py:219
  5.2 6.1 %collective-permute-start.16 = (bf16[192,128]{1,0:T(8,128)(2,1)S(1)}, bf16[192,128]{1,0:T(8,128)(2,1)S(1)}, u32[]{:S(2)}, u32[]{:S(2)}) collective-permute-start(bf16[192,128]{1,0:T(8,128)(2,1)S(1)} %get-tuple-element.14), channel_id=1, source_target_pairs={{0,8},{1,9},{2,10},{3,11},{4,12},{5,13},{6,14},{7,15},{8,0},{9,1},... | collective-permute-start | bytes 147464 | tf_op jit(solution)/shard_map/ppermute | solution.py:219
  7.8 5.9 %collective-permute-start.17 = (bf16[192,128]{1,0:T(8,128)(2,1)S(1)}, bf16[192,128]{1,0:T(8,128)(2,1)S(1)}, u32[]{:S(2)}, u32[]{:S(2)}) collective-permute-start(bf16[192,128]{1,0:T(8,128)(2,1)S(1)} %get-tuple-element.14), channel_id=1, source_target_pairs={{0,12},{1,13},{2,14},{3,15},{4,8},{5,9},{6,10},{7,11},{8,4},{9,5},... | collective-permute-start | bytes 147464 | tf_op jit(solution)/shard_map/ppermute | solution.py:219
  9.5 9.0 %collective-permute-start.1 = (bf16[192,640]{1,0:T(8,128)(2,1)S(1)}, bf16[192,640]{1,0:T(8,128)(2,1)S(1)}, u32[]{:S(2)}, u32[]{:S(2)}) collective-permute-start(bf16[192,640]{1,0:T(8,128)(2,1)S(1)} %pad.4.refs_0_), channel_id=1, source_target_pairs={{0,2},{1,3},{2,0},{3,1},{4,6},{5,7},{6,4},{7,5},{8,10},{9,11},{10,... | collective-permute-start | bytes 737288 | tf_op jit(solution)/shard_map/ppermute | solution.py:219
  13.7 8.5 %collective-permute-start.18 = (bf16[768,128]{1,0:T(8,128)(2,1)S(1)}, bf16[768,128]{1,0:T(8,128)(2,1)S(1)}, u32[]{:S(2)}, u32[]{:S(2)}) collective-permute-start(bf16[768,128]{1,0:T(8,128)(2,1)S(1)} %get-tuple-element.7), channel_id=1, source_target_pairs={{0,2},{1,3},{2,0},{3,1},{4,6},{5,7},{6,4},{7,5},{8,10},{9,11},{10,... | collective-permute-start | bytes 589832 | tf_op jit(solution)/shard_map/ppermute | solution.py:219
  15.3 7.9 %collective-permute-start = (bf16[192,640]{1,0:T(8,128)(2,1)S(1)}, bf16[192,640]{1,0:T(8,128)(2,1)S(1)}, u32[]{:S(2)}, u32[]{:S(2)}) collective-permute-start(bf16[192,640]{1,0:T(8,128)(2,1)S(1)} %pad.4.refs_0_), channel_id=1, source_target_pairs={{0,1},{1,0},{2,3},{3,2},{4,5},{5,4},{6,7},{7,6},{8,9},{9,8},{10,11... | collective-permute-start | bytes 737288 | tf_op jit(solution)/shard_map/ppermute | solution.py:219
  15.3 12.6 %collective-permute-start.3 = (bf16[192,640]{1,0:T(8,128)(2,1)S(1)}, bf16[192,640]{1,0:T(8,128)(2,1)S(1)}, u32[]{:S(2)}, u32[]{:S(2)}) collective-permute-start(bf16[192,640]{1,0:T(8,128)(2,1)S(1)} %pad.4.refs_0_), channel_id=1, source_target_pairs={{0,4},{1,5},{2,6},{3,7},{4,0},{5,1},{6,2},{7,3},{8,12},{9,13},{10,... | collective-permute-start | bytes 737288 | tf_op jit(solution)/shard_map/ppermute | solution.py:219
  15.3 20.2 %collective-permute-start.7 = (bf16[192,640]{1,0:T(8,128)(2,1)S(1)}, bf16[192,640]{1,0:T(8,128)(2,1)S(1)}, u32[]{:S(2)}, u32[]{:S(2)}) collective-permute-start(bf16[192,640]{1,0:T(8,128)(2,1)S(1)} %pad.4.refs_0_), channel_id=1, source_target_pairs={{0,8},{1,9},{2,10},{3,11},{4,12},{5,13},{6,14},{7,15},{8,0},{9,1},... | collective-permute-start | bytes 737288 | tf_op jit(solution)/shard_map/ppermute | solution.py:219
  18.4 17.6 %collective-permute-start.11 = (bf16[192,640]{1,0:T(8,128)(2,1)S(1)}, bf16[192,640]{1,0:T(8,128)(2,1)S(1)}, u32[]{:S(2)}, u32[]{:S(2)}) collective-permute-start(bf16[192,640]{1,0:T(8,128)(2,1)S(1)} %pad.4.refs_0_), channel_id=1, source_target_pairs={{0,12},{1,13},{2,14},{3,15},{4,8},{5,9},{6,10},{7,11},{8,4},{9,5},... | collective-permute-start | bytes 737288 | tf_op jit(solution)/shard_map/ppermute | solution.py:219
  22.3 15.3 %collective-permute-start.2 = (bf16[192,640]{1,0:T(8,128)(2,1)S(1)}, bf16[192,640]{1,0:T(8,128)(2,1)S(1)}, u32[]{:S(2)}, u32[]{:S(2)}) collective-permute-start(bf16[192,640]{1,0:T(8,128)(2,1)S(1)} %collective-permute-done.1.refs_2_), channel_id=1, source_target_pairs={{0,1},{1,0},{2,3},{3,2},{4,5},{5,4},{6,7},{7,6},{8,9},{9,8},{10,11... | collective-permute-start | bytes 737288 | tf_op jit(solution)/shard_map/ppermute | solution.py:219
  23.2 30.1 %collective-permute-start.19 = (bf16[1536,128]{1,0:T(8,128)(2,1)S(1)}, bf16[1536,128]{1,0:T(8,128)(2,1)S(1)}, u32[]{:S(2)}, u32[]{:S(2)}) collective-permute-start(bf16[1536,128]{1,0:T(8,128)(2,1)S(1)} %constant_dynamic-update-slice_fusion.7.keys_ref.near_ref), channel_id=1, source_target_pairs={{0,1},{1,0},{2,3},{3,2},{4,5},{5,4},{6,7},{7,6},{8,9},{9,8},{10,11... | collective-permute-start | bytes 1179656 | tf_op jit(solution)/shard_map/ppermute | solution.py:219
  27.9 18.6 %collective-permute-start.4 = (bf16[192,640]{1,0:T(8,128)(2,1)S(1)}, bf16[192,640]{1,0:T(8,128)(2,1)S(1)}, u32[]{:S(2)}, u32[]{:S(2)}) collective-permute-start(bf16[192,640]{1,0:T(8,128)(2,1)S(1)} %collective-permute-done.3.refs_4_), channel_id=1, source_target_pairs={{0,1},{1,0},{2,3},{3,2},{4,5},{5,4},{6,7},{7,6},{8,9},{9,8},{10,11... | collective-permute-start | bytes 737288 | tf_op jit(solution)/shard_map/ppermute | solution.py:219
  35.5 11.0 %collective-permute-start.5 = (bf16[192,640]{1,0:T(8,128)(2,1)S(1)}, bf16[192,640]{1,0:T(8,128)(2,1)S(1)}, u32[]{:S(2)}, u32[]{:S(2)}) collective-permute-start(bf16[192,640]{1,0:T(8,128)(2,1)S(1)} %collective-permute-done.3.refs_4_), channel_id=1, source_target_pairs={{0,2},{1,3},{2,0},{3,1},{4,6},{5,7},{6,4},{7,5},{8,10},{9,11},{10,... | collective-permute-start | bytes 737288 | tf_op jit(solution)/shard_map/ppermute | solution.py:219
  36.1 13.6 %collective-permute-start.9 = (bf16[192,640]{1,0:T(8,128)(2,1)S(1)}, bf16[192,640]{1,0:T(8,128)(2,1)S(1)}, u32[]{:S(2)}, u32[]{:S(2)}) collective-permute-start(bf16[192,640]{1,0:T(8,128)(2,1)S(1)} %collective-permute-done.7.refs_8_), channel_id=1, source_target_pairs={{0,2},{1,3},{2,0},{3,1},{4,6},{5,7},{6,4},{7,5},{8,10},{9,11},{10,... | collective-permute-start | bytes 737288 | tf_op jit(solution)/shard_map/ppermute | solution.py:219
  37.6 15.7 %collective-permute-start.13 = (bf16[192,640]{1,0:T(8,128)(2,1)S(1)}, bf16[192,640]{1,0:T(8,128)(2,1)S(1)}, u32[]{:S(2)}, u32[]{:S(2)}) collective-permute-start(bf16[192,640]{1,0:T(8,128)(2,1)S(1)} %collective-permute-done.11.refs_12_), channel_id=1, source_target_pairs={{0,2},{1,3},{2,0},{3,1},{4,6},{5,7},{6,4},{7,5},{8,10},{9,11},{10,... | collective-permute-start | bytes 737288 | tf_op jit(solution)/shard_map/ppermute | solution.py:219
  38.1 1.6 %copy-start = (bf16[128,8192]{1,0:T(8,128)(2,1)S(1)}, bf16[128,8192]{1,0:T(8,128)(2,1)}, u32[]{:S(2)}) copy-start(bf16[128,8192]{1,0:T(8,128)(2,1)} %iq_ref.3) | copy-start | bytes 6291460
  46.5 20.9 %copy-start.1 = (s32[2,12]{1,0:T(2,128)S(1)}, s32[2,12]{1,0:T(2,128)}, u32[]{:S(2)}) copy-start(s32[2,12]{1,0:T(2,128)} %pick_ref.1) | copy-start | bytes 292
  46.5 20.8 %collective-permute-start.8 = (bf16[192,640]{1,0:T(8,128)(2,1)S(1)}, bf16[192,640]{1,0:T(8,128)(2,1)S(1)}, u32[]{:S(2)}, u32[]{:S(2)}) collective-permute-start(bf16[192,640]{1,0:T(8,128)(2,1)S(1)} %collective-permute-done.7.refs_8_), channel_id=1, source_target_pairs={{0,1},{1,0},{2,3},{3,2},{4,5},{5,4},{6,7},{7,6},{8,9},{9,8},{10,11... | collective-permute-start | bytes 737288 | tf_op jit(solution)/shard_map/ppermute | solution.py:219
  46.6 20.7 %collective-permute-start.12 = (bf16[192,640]{1,0:T(8,128)(2,1)S(1)}, bf16[192,640]{1,0:T(8,128)(2,1)S(1)}, u32[]{:S(2)}, u32[]{:S(2)}) collective-permute-start(bf16[192,640]{1,0:T(8,128)(2,1)S(1)} %collective-permute-done.11.refs_12_), channel_id=1, source_target_pairs={{0,1},{1,0},{2,3},{3,2},{4,5},{5,4},{6,7},{7,6},{8,9},{9,8},{10,11... | collective-permute-start | bytes 737288 | tf_op jit(solution)/shard_map/ppermute | solution.py:219
  49.7 17.6 %collective-permute-start.6 = (bf16[192,640]{1,0:T(8,128)(2,1)S(1)}, bf16[192,640]{1,0:T(8,128)(2,1)S(1)}, u32[]{:S(2)}, u32[]{:S(2)}) collective-permute-start(bf16[192,640]{1,0:T(8,128)(2,1)S(1)} %collective-permute-done.5.refs_6_), channel_id=1, source_target_pairs={{0,1},{1,0},{2,3},{3,2},{4,5},{5,4},{6,7},{7,6},{8,9},{9,8},{10,11... | collective-permute-start | bytes 737288 | tf_op jit(solution)/shard_map/ppermute | solution.py:219
  53.3 14.0 %collective-permute-start.10 = (bf16[192,640]{1,0:T(8,128)(2,1)S(1)}, bf16[192,640]{1,0:T(8,128)(2,1)S(1)}, u32[]{:S(2)}, u32[]{:S(2)}) collective-permute-start(bf16[192,640]{1,0:T(8,128)(2,1)S(1)} %collective-permute-done.9.refs_10_), channel_id=1, source_target_pairs={{0,1},{1,0},{2,3},{3,2},{4,5},{5,4},{6,7},{7,6},{8,9},{9,8},{10,11... | collective-permute-start | bytes 737288 | tf_op jit(solution)/shard_map/ppermute | solution.py:219
  53.3 14.0 %collective-permute-start.14 = (bf16[192,640]{1,0:T(8,128)(2,1)S(1)}, bf16[192,640]{1,0:T(8,128)(2,1)S(1)}, u32[]{:S(2)}, u32[]{:S(2)}) collective-permute-start(bf16[192,640]{1,0:T(8,128)(2,1)S(1)} %collective-permute-done.13.refs_14_), channel_id=1, source_target_pairs={{0,1},{1,0},{2,3},{3,2},{4,5},{5,4},{6,7},{7,6},{8,9},{9,8},{10,11... | collective-permute-start | bytes 737288 | tf_op jit(solution)/shard_map/ppermute | solution.py:219

commit v2 on v1

--- a/solution.py
+++ b/solution.py
@@ -54,8 +54,7 @@
         wide_ref[j] = jnp.broadcast_to(w_ref[:, j : j + 1] * IDX**-0.5, wide_ref.shape[1:])
 
 
-def index_near_kernel(rels, own_ref, iq_ref, w_ref, keys_ref, out_ref, wide_ref):
-    own = own_ref[0]
+def index_window_kernel(rels, iq_ref, w_ref, keys_ref, out_ref, wide_ref):
     tok = iq_ref.shape[0]
     span = BLK + tok
     spread_weights(w_ref, wide_ref)
@@ -69,24 +68,18 @@
         out_ref[2 * pair + 1] = value[:, LANES:]
 
 
-def index_far_kernel(
-    near, far, own_ref, iq_ref, w_ref, near_ref, far_ref, done_ref, prefix_ref, window_ref,
-    wide_ref, keys_ref, res_ref,
+def index_prefix_kernel(
+    near, far, own_ref, iq_ref, w_ref, near_ref, far_ref, near_done, far_done, prefix_ref,
+    window_ref, wide_ref, keys_ref, res_ref,
 ):
     own = own_ref[0]
     tok = iq_ref.shape[0]
     span = BLK + tok
-    devices = len(near) + len(far)
     spread_weights(w_ref, wide_ref)
     for ref, rels in ((near_ref, near), (far_ref, far)):
         for n, rel in enumerate(rels):
             at = pl.multiple_of((own ^ rel) * BLK, BLK)
             keys_ref[pl.ds(at, BLK), :] = ref[n * span : n * span + BLK, :]
-    base = devices * BLK
-    for n in range(len(far)):
-        keys_ref[base + n * tok : base + (n + 1) * tok, :] = far_ref[
-            n * span + BLK : (n + 1) * span, :
-        ]
 
     @pl.loop(0, keys_ref.shape[0] // TILE)
     def _(tile):
@@ -95,16 +88,16 @@
         res_ref[2 * tile] = value[:, :LANES]
         res_ref[2 * tile + 1] = value[:, LANES:]
 
-    for n in range(base // LANES):
+    for n in range(keys_ref.shape[0] // LANES):
         prefix_ref[:, n * LANES : (n + 1) * LANES] = res_ref[n]
     row = lax.broadcasted_iota(jnp.int32, (tok, LANES), 0)
     lane = lax.broadcasted_iota(jnp.int32, (tok, LANES), 1)
-    for rels, ref, start in ((near, done_ref, 0), (far, res_ref, base // LANES)):
+    for rels, ref in ((near, near_done), (far, far_done)):
         for n, rel in enumerate(rels):
             other = own ^ rel
             seen = other * tok + lane <= own * tok + row
             window_ref[:, pl.ds(pl.multiple_of(other * tok, LANES), LANES)] = jnp.where(
-                seen, ref[start + n], 0.0
+                seen, ref[n], 0.0
             )
 
 
@@ -218,6 +211,30 @@
     def swap(array, rel):
         return lax.ppermute(array, "ctx", [(i, i ^ rel) for i in range(devices)])
 
+    smem = pl.BlockSpec(memory_space=pltpu.SMEM)
+    vmem = pl.BlockSpec(memory_space=pltpu.VMEM)
+    hbm = pl.BlockSpec(memory_space=pl.ANY)
+    params = pltpu.CompilerParams(vmem_limit_bytes=VMEM)
+
+    def index_cost(keys):
+        return pl.CostEstimate(
+            flops=2 * tok * IH * IDX * keys * 4, bytes_accessed=2**22, transcendentals=0
+        )
+
+    def index_window(rels, shard_keys):
+        return pl.pallas_call(
+            functools.partial(index_window_kernel, rels),
+            out_shape=jax.ShapeDtypeStruct((len(rels), tok, LANES), jnp.float32),
+            in_specs=[vmem, vmem, vmem],
+            out_specs=vmem,
+            scratch_shapes=[pltpu.VMEM((IH, tok, LANES), jnp.float32)],
+            compiler_params=params,
+            cost_estimate=index_cost(len(rels) * tok),
+        )(index_queries, index_weights, shard_keys)
+
+    def after(done, *arrays):
+        return lax.optimization_barrier((done, *arrays))[1:]
+
     line = list(range(0, devices, 4))
     keys = jnp.concatenate([prefix_index_keys, window_index_keys], 0)
     key_line = jnp.concatenate([keys] + [swap(keys, rel) for rel in line[1:]], 0)
@@ -232,45 +249,41 @@
     shards[0] = rows
     for rel in line[1:]:
         shards[rel] = swap(rows, rel)
-    for rel in line:
-        shards[rel + 2] = swap(shards[rel], 2)
-    for rel in near:
-        shards[rel + 1] = swap(shards[rel], 1)
-
-    smem = pl.BlockSpec(memory_space=pltpu.SMEM)
-    vmem = pl.BlockSpec(memory_space=pltpu.VMEM)
-    hbm = pl.BlockSpec(memory_space=pl.ANY)
-    params = pltpu.CompilerParams(vmem_limit_bytes=VMEM)
-    done = pl.pallas_call(
-        functools.partial(index_near_kernel, near),
-        out_shape=jax.ShapeDtypeStruct((len(near), tok, LANES), jnp.float32),
-        in_specs=[smem, vmem, vmem, vmem],
-        out_specs=vmem,
-        scratch_shapes=[pltpu.VMEM((IH, tok, LANES), jnp.float32)],
-        compiler_params=params,
-        cost_estimate=pl.CostEstimate(
-            flops=2 * tok * IH * IDX * len(near) * tok * 4, bytes_accessed=2**22, transcendentals=0
-        ),
-    )(own, index_queries, index_weights, near_keys)
-    total_keys = devices * BLK + len(far) * tok
+    shards[2] = swap(rows, 2)
+
+    near_done = index_window(near, near_keys)
+    first, rest = line[1], line[2:]
+    held = [0, 2, first]
+    for rel, array in zip(held, after(near_done, *[shards[rel] for rel in held])):
+        shards[rel + 1] = swap(array, 1)
+        if rel == first:
+            shards[rel + 2] = swap(array, 2)
+    far_done = index_window(far, far_keys)
+    held = rest + [first + 2]
+    for rel, array in zip(held, after(far_done, *[shards[rel] for rel in held])):
+        shards[rel + 1] = swap(array, 1)
+        if rel in rest:
+            shards[rel + 2] = swap(array, 2)
+
     prefix_index, window_index = pl.pallas_call(
-        functools.partial(index_far_kernel, near, far),
+        functools.partial(index_prefix_kernel, near, far),
         out_shape=(
             jax.ShapeDtypeStruct((tok, devices * BLK), jnp.float32),
             jax.ShapeDtypeStruct((tok, devices * tok), jnp.float32),
         ),
-        in_specs=[smem, vmem, vmem, vmem, vmem, vmem],
+        in_specs=[smem] + [vmem] * 6,
         out_specs=(vmem, vmem),
         scratch_shapes=[
             pltpu.VMEM((IH, tok, LANES), jnp.float32),
-            pltpu.VMEM((total_keys, IDX), jnp.bfloat16),
-            pltpu.VMEM((total_keys // LANES, tok, LANES), jnp.float32),
+            pltpu.VMEM((devices * BLK, IDX), jnp.bfloat16),
+            pltpu.VMEM((devices * BLK // LANES, tok, LANES), jnp.float32),
         ],
         compiler_params=params,
-        cost_estimate=pl.CostEstimate(
-            flops=2 * tok * IH * IDX * total_keys * 4, bytes_accessed=2**22, transcendentals=0
-        ),
-    )(own, index_queries, index_weights, near_keys, far_keys, done)
+        cost_estimate=index_cost(devices * BLK),
+    )(own, index_queries, index_weights, near_keys, far_keys, near_done, far_done)
+    held = [rel + 2 for rel in rest]
+    for rel, array in zip(held, after(prefix_index, *[shards[rel] for rel in held])):
+        shards[rel + 1] = swap(array, 1)
 
     count = picks.shape[1] * BLK
     attention = pl.pallas_call(

time: 92.5 us -> 82.7 us (0.89)
  waiting for transfers between devices: 22.2 us -> 13.4 us
  starting transfers between devices: 18.4 us -> 16.5 us
    ppermute x20, waiting for transfers between devices: 22.2 us -> 13.4 us  [swap(): return lax.ppermute(array, 'ctx', [(i, i ^ rel) for i in range(devices)])]
    ppermute x20, starting transfers between devices: 18.4 us -> 16.5 us  [swap(): return lax.ppermute(array, 'ctx', [(i, i ^ rel) for i in range(devices)])]
    pallas_call x2 -> x3, Pallas kernels: 20.3 us -> 21.1 us  [the longest x2 13 us: index_window(): pl.pallas_call(functools.partial(index_window_kernel, rels), out_shape=ja...]
    unnamed x9 -> x11, local copies, waits for them, and re-layouts: 3.99 us -> 3.98 us
  transfers between devices with their start and end apart: 20 -> 20, of which waited for: 6 -> 6; matrix products, arithmetic and copies ran while one was open for 3% -> 3% of each run, Pallas kernels for 22% -> 26%
where the time goes in v2:
time: 82.7 us; the launch traced here: 82.3 us
  Pallas kernels  45.8 us (55%)
  starting transfers between devices  16.5 us (20%)
  waiting for transfers between devices  13.4 us (16%)
  local copies, waits for them, and re-layouts  4.36 us (5%)
  other arithmetic  1.29 us (2%)
  between operations  0.94 us (1%)
    pallas_call x1, Pallas kernels, body(): pl.pallas_call(functools.partial(attention_kernel, devices), grid_spec=pl...  24.7 us
    ppermute x20, starting transfers between devices, swap(): return lax.ppermute(array, 'ctx', [(i, i ^ rel) for i in range(devices)])  16.5 us
    ppermute x20, waiting for transfers between devices, swap(): return lax.ppermute(array, 'ctx', [(i, i ^ rel) for i in range(devices)])  13.4 us
    pallas_call x2, Pallas kernels, index_window(): pl.pallas_call(functools.partial(index_window_kernel, rels), out_shape=ja...  13 us
    pallas_call x1, Pallas kernels, body(): pl.pallas_call(functools.partial(index_prefix_kernel, near, far), out_sha...  8.05 us
    unnamed x11, local copies, waits for them, and re-layouts  3.98 us
  transfers between devices with their start and end apart: 20, of which 6 were waited for; matrix products, arithmetic and copies ran while one was open for 3% of the time, Pallas kernels for 26%

profile of v2, /device:TPU:0, one launch (start us, length us, event | category | flops | bytes accessed | tf_op | source)
XLA Modules:
  0.0 82.3 jit_solution(10599652840569977831)
XLA Ops:
  0.6 0.7 constant_dynamic-update-slice_fusion.6
  1.4 0.8 constant_dynamic-update-slice_fusion.5
  2.1 3.1 %collective-permute-start = (bf16[192,128]{1,0:T(8,128)(2,1)S(1)}, bf16[192,128]{1,0:T(8,128)(2,1)S(1)}, u32[]{:S(2)}, u32[]{:S(2)}) collective-permute-start(bf16[192,128]{1,0:T(8,128)(2,1)S(1)} %get-tuple-element.30), channel_id=1, source_target_pairs={{0,4},{1,5},{2,6},{3,7},{4,0},{5,1},{6,2},{7,3},{8,12},{9,13},{10,... | collective-permute-start | bytes 147464 | tf_op jit(solution)/shard_map/ppermute | solution.py:212
  5.2 2.5 %collective-permute-start.2 = (bf16[192,128]{1,0:T(8,128)(2,1)S(1)}, bf16[192,128]{1,0:T(8,128)(2,1)S(1)}, u32[]{:S(2)}, u32[]{:S(2)}) collective-permute-start(bf16[192,128]{1,0:T(8,128)(2,1)S(1)} %get-tuple-element.30), channel_id=1, source_target_pairs={{0,12},{1,13},{2,14},{3,15},{4,8},{5,9},{6,10},{7,11},{8,4},{9,5},... | collective-permute-start | bytes 147464 | tf_op jit(solution)/shard_map/ppermute | solution.py:212
  7.7 0.1 collective-permute-start.1
  7.8 5.4 %collective-permute-done.1 = bf16[192,128]{1,0:T(8,128)(2,1)S(1)} collective-permute-done((bf16[192,128]{1,0:T(8,128)(2,1)S(1)}, bf16[192,128]{1,0:T(8,128)(2,1)S(1)}, u32[]{:S(2)}, u32[]{:S(2)}) %collective-permute-start.1) | collective-permute-done | bytes 49184 | tf_op jit(solution)/shard_map/ppermute | solution.py:212
  13.3 1.6 %collective-permute-start.3 = (bf16[768,128]{1,0:T(8,128)(2,1)S(1)}, bf16[768,128]{1,0:T(8,128)(2,1)S(1)}, u32[]{:S(2)}, u32[]{:S(2)}) collective-permute-start(bf16[768,128]{1,0:T(8,128)(2,1)S(1)} %get-tuple-element.23), channel_id=1, source_target_pairs={{0,2},{1,3},{2,0},{3,1},{4,6},{5,7},{6,4},{7,5},{8,10},{9,11},{10,... | collective-permute-start | bytes 589832 | tf_op jit(solution)/shard_map/ppermute | solution.py:212
  14.9 1.3 %pad_maximum_fusion = bf16[3,36864]{1,0:T(4,128)(2,1)S(1)} fusion(bf16[2,36864]{1,0:T(2,128)(2,1)} %param.10, bf16[1,36864]{1,0:T(2,128)(2,1)} %param.9), kind=kLoop, calls=%fused_computation | loop fusion | flops 442368 | bytes 442368 | tf_op jit(solution)/shard_map/concatenate | solution.py:246
  16.1 0.3 reshape.13
  16.5 2.2 %collective-permute-start.12 = (bf16[192,640]{1,0:T(8,128)(2,1)S(1)}, bf16[192,640]{1,0:T(8,128)(2,1)S(1)}, u32[]{:S(2)}, u32[]{:S(2)}) collective-permute-start(bf16[192,640]{1,0:T(8,128)(2,1)S(1)} %pad.4.refs_0_), channel_id=1, source_target_pairs={{0,12},{1,13},{2,14},{3,15},{4,8},{5,9},{6,10},{7,11},{8,4},{9,5},... | collective-permute-start | bytes 737288 | tf_op jit(solution)/shard_map/ppermute | solution.py:212
  18.7 2.3 %collective-permute-start.5 = (bf16[192,640]{1,0:T(8,128)(2,1)S(1)}, bf16[192,640]{1,0:T(8,128)(2,1)S(1)}, u32[]{:S(2)}, u32[]{:S(2)}) collective-permute-start(bf16[192,640]{1,0:T(8,128)(2,1)S(1)} %pad.4.refs_0_), channel_id=1, source_target_pairs={{0,4},{1,5},{2,6},{3,7},{4,0},{5,1},{6,2},{7,3},{8,12},{9,13},{10,... | collective-permute-start | bytes 737288 | tf_op jit(solution)/shard_map/ppermute | solution.py:212
  20.9 0.5 collective-permute-start.4
  21.5 0.8 %copy.11.w_ref = f32[128,64]{1,0:T(8,128)S(1)} copy(f32[128,64]{0,1:T(8,128)} %param.12) | data formatting | bytes 65536 | tf_op args[4]
  22.3 0.1 collective-permute-start.10
  22.4 1.6 %copy-done = bf16[128,8192]{1,0:T(8,128)(2,1)S(1)} copy-done((bf16[128,8192]{1,0:T(8,128)(2,1)S(1)}, bf16[128,8192]{1,0:T(8,128)(2,1)}, u32[]{:S(2)}) %copy-start) | copy-done | bytes 2097176
  24.0 6.6 %shard_map.103.near_done = f32[8,128,128]{2,1,0:T(8,128)S(1)} custom-call(bf16[128,8192]{1,0:T(8,128)(2,1)S(1)} %copy-done, f32[128,64]{1,0:T(8,128)S(1)} %copy.11.w_ref, bf16[1536,128]{1,0:T(8,128)(2,1)S(1)} %constant_dynamic-update-slice_fusion.7.keys_ref.near_ref), custom_call_target="tpu_custom_call" | custom-call | flops 8589934592 | bytes 4194304 | tf_op jit(solution)/shard_map/pallas_call | solution.py:225
  30.6 3.0 %collective-permute-done.5.refs_4_ = bf16[192,640]{1,0:T(8,128)(2,1)S(1)} collective-permute-done((bf16[192,640]{1,0:T(8,128)(2,1)S(1)}, bf16[192,640]{1,0:T(8,128)(2,1)S(1)}, u32[]{:S(2)}, u32[]{:S(2)}) %collective-permute-start.5) | collective-permute-done | bytes 245792 | tf_op jit(solution)/shard_map/ppermute | solution.py:212
  33.6 0.5 collective-permute-start.9
  34.2 0.5 collective-permute-start.6
  34.7 6.4 %shard_map.104.far_done = f32[8,128,128]{2,1,0:T(8,128)S(1)} custom-call(bf16[128,8192]{1,0:T(8,128)(2,1)S(1)} %copy-done, f32[128,64]{1,0:T(8,128)S(1)} %copy.11.w_ref, bf16[1536,128]{1,0:T(8,128)(2,1)S(1)} %collective-permute-done.10.keys_ref.far_ref), custom_call_target="tpu_custom_call" | custom-call | flops 8589934592 | bytes 4194304 | tf_op jit(solution)/shard_map/pallas_call | solution.py:225
  41.1 0.1 collective-permute-start.7
  41.2 1.6 %collective-permute-start.15 = (bf16[192,640]{1,0:T(8,128)(2,1)S(1)}, bf16[192,640]{1,0:T(8,128)(2,1)S(1)}, u32[]{:S(2)}, u32[]{:S(2)}) collective-permute-start(bf16[192,640]{1,0:T(8,128)(2,1)S(1)} %collective-permute-done.11.refs_8_), channel_id=1, source_target_pairs={{0,2},{1,3},{2,0},{3,1},{4,6},{5,7},{6,4},{7,5},{8,10},{9,11},{10,... | collective-permute-start | bytes 737288 | tf_op jit(solution)/shard_map/ppermute | solution.py:212
  42.8 0.5 collective-permute-start.16
  43.3 8.0 %shard_map.105 = (f32[128,1024]{1,0:T(8,128)}, f32[128,2048]{1,0:T(8,128)}) custom-call(s32[1]{0:T(128)} %bitcast.own_ref, bf16[128,8192]{1,0:T(8,128)(2,1)S(1)} %copy-done.1, f32[128,64]{1,0:T(8,128)S(1)} %copy.11.w_ref, bf16[1536,128]{1,0:T(8,128)(2,1)S(1)} %constant_dynamic-update-slice_fusion.7.keys_ref.near_ref, ...), custom_call_target="tpu_custom_call" | custom-call | flops 8589934592 | bytes 4194304 | tf_op jit(solution)/shard_map/pallas_call | solution.py:268
  51.4 3.5 %collective-permute-done.16.refs_14_ = bf16[192,640]{1,0:T(8,128)(2,1)S(1)} collective-permute-done((bf16[192,640]{1,0:T(8,128)(2,1)S(1)}, bf16[192,640]{1,0:T(8,128)(2,1)S(1)}, u32[]{:S(2)}, u32[]{:S(2)}) %collective-permute-start.16) | collective-permute-done | bytes 245792 | tf_op jit(solution)/shard_map/ppermute | solution.py:212
  54.9 0.5 collective-permute-start.13
  55.4 0.1 collective-permute-start.17
  55.4 0.4 collective-permute-start.19
  55.9 0.8 %collective-permute-done.13.refs_7_ = bf16[192,640]{1,0:T(8,128)(2,1)S(1)} collective-permute-done((bf16[192,640]{1,0:T(8,128)(2,1)S(1)}, bf16[192,640]{1,0:T(8,128)(2,1)S(1)}, u32[]{:S(2)}, u32[]{:S(2)}) %collective-permute-start.13) | collective-permute-done | bytes 245792 | tf_op jit(solution)/shard_map/ppermute | solution.py:212
  56.7 0.3 collective-permute-done.17.refs_11_
  57.1 0.4 collective-permute-done.19.refs_15_
  57.4 24.7 %shard_map.106 = bf16[128,32768]{1,0:T(8,128)(2,1)} custom-call(s32[1]{0:T(128)} %bitcast.own_ref, s32[2,12]{1,0:T(2,128)S(1)} %copy-done.2, bf16[128,36864]{1,0:T(8,128)(2,1)} %q_ref.1, bf16[192,640]{1,0:T(8,128)(2,1)S(1)} %pad.4.refs_0_, bf16[192,640]{1,0:T(8,128)(2,1)S(1)} %collective-permute-done.6.refs_1_, ...), custom_call_target="tpu_custom_call" | custom-call | flops 14495514624 | bytes 16777216 | tf_op jit(solution)/shard_map/pallas_call | solution.py:289
  (28 shorter events, 0.2 us)
Async XLA Ops:
  2.1 5.7 %collective-permute-start = (bf16[192,128]{1,0:T(8,128)(2,1)S(1)}, bf16[192,128]{1,0:T(8,128)(2,1)S(1)}, u32[]{:S(2)}, u32[]{:S(2)}) collective-permute-start(bf16[192,128]{1,0:T(8,128)(2,1)S(1)} %get-tuple-element.30), channel_id=1, source_target_pairs={{0,4},{1,5},{2,6},{3,7},{4,0},{5,1},{6,2},{7,3},{8,12},{9,13},{10,... | collective-permute-start | bytes 147464 | tf_op jit(solution)/shard_map/ppermute | solution.py:212
  5.2 8.0 %collective-permute-start.2 = (bf16[192,128]{1,0:T(8,128)(2,1)S(1)}, bf16[192,128]{1,0:T(8,128)(2,1)S(1)}, u32[]{:S(2)}, u32[]{:S(2)}) collective-permute-start(bf16[192,128]{1,0:T(8,128)(2,1)S(1)} %get-tuple-element.30), channel_id=1, source_target_pairs={{0,12},{1,13},{2,14},{3,15},{4,8},{5,9},{6,10},{7,11},{8,4},{9,5},... | collective-permute-start | bytes 147464 | tf_op jit(solution)/shard_map/ppermute | solution.py:212
  7.7 5.5 %collective-permute-start.1 = (bf16[192,128]{1,0:T(8,128)(2,1)S(1)}, bf16[192,128]{1,0:T(8,128)(2,1)S(1)}, u32[]{:S(2)}, u32[]{:S(2)}) collective-permute-start(bf16[192,128]{1,0:T(8,128)(2,1)S(1)} %get-tuple-element.30), channel_id=1, source_target_pairs={{0,8},{1,9},{2,10},{3,11},{4,12},{5,13},{6,14},{7,15},{8,0},{9,1},... | collective-permute-start | bytes 147464 | tf_op jit(solution)/shard_map/ppermute | solution.py:212
  13.3 9.0 %collective-permute-start.3 = (bf16[768,128]{1,0:T(8,128)(2,1)S(1)}, bf16[768,128]{1,0:T(8,128)(2,1)S(1)}, u32[]{:S(2)}, u32[]{:S(2)}) collective-permute-start(bf16[768,128]{1,0:T(8,128)(2,1)S(1)} %get-tuple-element.23), channel_id=1, source_target_pairs={{0,2},{1,3},{2,0},{3,1},{4,6},{5,7},{6,4},{7,5},{8,10},{9,11},{10,... | collective-permute-start | bytes 589832 | tf_op jit(solution)/shard_map/ppermute | solution.py:212
  16.5 24.6 %collective-permute-start.12 = (bf16[192,640]{1,0:T(8,128)(2,1)S(1)}, bf16[192,640]{1,0:T(8,128)(2,1)S(1)}, u32[]{:S(2)}, u32[]{:S(2)}) collective-permute-start(bf16[192,640]{1,0:T(8,128)(2,1)S(1)} %pad.4.refs_0_), channel_id=1, source_target_pairs={{0,12},{1,13},{2,14},{3,15},{4,8},{5,9},{6,10},{7,11},{8,4},{9,5},... | collective-permute-start | bytes 737288 | tf_op jit(solution)/shard_map/ppermute | solution.py:212
  18.7 22.5 %collective-permute-start.11 = (bf16[192,640]{1,0:T(8,128)(2,1)S(1)}, bf16[192,640]{1,0:T(8,128)(2,1)S(1)}, u32[]{:S(2)}, u32[]{:S(2)}) collective-permute-start(bf16[192,640]{1,0:T(8,128)(2,1)S(1)} %pad.4.refs_0_), channel_id=1, source_target_pairs={{0,8},{1,9},{2,10},{3,11},{4,12},{5,13},{6,14},{7,15},{8,0},{9,1},... | collective-permute-start | bytes 737288 | tf_op jit(solution)/shard_map/ppermute | solution.py:212
  18.7 15.0 %collective-permute-start.5 = (bf16[192,640]{1,0:T(8,128)(2,1)S(1)}, bf16[192,640]{1,0:T(8,128)(2,1)S(1)}, u32[]{:S(2)}, u32[]{:S(2)}) collective-permute-start(bf16[192,640]{1,0:T(8,128)(2,1)S(1)} %pad.4.refs_0_), channel_id=1, source_target_pairs={{0,4},{1,5},{2,6},{3,7},{4,0},{5,1},{6,2},{7,3},{8,12},{9,13},{10,... | collective-permute-start | bytes 737288 | tf_op jit(solution)/shard_map/ppermute | solution.py:212
  20.9 12.7 %collective-permute-start.4 = (bf16[192,640]{1,0:T(8,128)(2,1)S(1)}, bf16[192,640]{1,0:T(8,128)(2,1)S(1)}, u32[]{:S(2)}, u32[]{:S(2)}) collective-permute-start(bf16[192,640]{1,0:T(8,128)(2,1)S(1)} %pad.4.refs_0_), channel_id=1, source_target_pairs={{0,2},{1,3},{2,0},{3,1},{4,6},{5,7},{6,4},{7,5},{8,10},{9,11},{10,... | collective-permute-start | bytes 737288 | tf_op jit(solution)/shard_map/ppermute | solution.py:212
  22.3 11.8 %collective-permute-start.10 = (bf16[1536,128]{1,0:T(8,128)(2,1)S(1)}, bf16[1536,128]{1,0:T(8,128)(2,1)S(1)}, u32[]{:S(2)}, u32[]{:S(2)}) collective-permute-start(bf16[1536,128]{1,0:T(8,128)(2,1)S(1)} %constant_dynamic-update-slice_fusion.7.keys_ref.near_ref), channel_id=1, source_target_pairs={{0,1},{1,0},{2,3},{3,2},{4,5},{5,4},{6,7},{7,6},{8,9},{9,8},{10,11... | collective-permute-start | bytes 1179656 | tf_op jit(solution)/shard_map/ppermute | solution.py:212
  22.4 1.6 %copy-start = (bf16[128,8192]{1,0:T(8,128)(2,1)S(1)}, bf16[128,8192]{1,0:T(8,128)(2,1)}, u32[]{:S(2)}) copy-start(bf16[128,8192]{1,0:T(8,128)(2,1)} %iq_ref.5) | copy-start | bytes 6291460
  30.6 12.7 %copy-start.1 = (bf16[128,8192]{1,0:T(8,128)(2,1)S(1)}, bf16[128,8192]{1,0:T(8,128)(2,1)}, u32[]{:S(2)}) copy-start(bf16[128,8192]{1,0:T(8,128)(2,1)} %iq_ref.5) | copy-start | bytes 6291460
  33.6 7.6 %collective-permute-start.9 = (bf16[192,640]{1,0:T(8,128)(2,1)S(1)}, bf16[192,640]{1,0:T(8,128)(2,1)S(1)}, u32[]{:S(2)}, u32[]{:S(2)}) collective-permute-start(bf16[192,640]{1,0:T(8,128)(2,1)S(1)} %collective-permute-done.5.refs_4_), channel_id=1, source_target_pairs={{0,2},{1,3},{2,0},{3,1},{4,6},{5,7},{6,4},{7,5},{8,10},{9,11},{10,... | collective-permute-start | bytes 737288 | tf_op jit(solution)/shard_map/ppermute | solution.py:212
  34.2 21.3 %collective-permute-start.8 = (bf16[192,640]{1,0:T(8,128)(2,1)S(1)}, bf16[192,640]{1,0:T(8,128)(2,1)S(1)}, u32[]{:S(2)}, u32[]{:S(2)}) collective-permute-start(bf16[192,640]{1,0:T(8,128)(2,1)S(1)} %collective-permute-done.5.refs_4_), channel_id=1, source_target_pairs={{0,1},{1,0},{2,3},{3,2},{4,5},{5,4},{6,7},{7,6},{8,9},{9,8},{10,11... | collective-permute-start | bytes 737288 | tf_op jit(solution)/shard_map/ppermute | solution.py:212
  34.2 20.7 %collective-permute-start.6 = (bf16[192,640]{1,0:T(8,128)(2,1)S(1)}, bf16[192,640]{1,0:T(8,128)(2,1)S(1)}, u32[]{:S(2)}, u32[]{:S(2)}) collective-permute-start(bf16[192,640]{1,0:T(8,128)(2,1)S(1)} %pad.4.refs_0_), channel_id=1, source_target_pairs={{0,1},{1,0},{2,3},{3,2},{4,5},{5,4},{6,7},{7,6},{8,9},{9,8},{10,11... | collective-permute-start | bytes 737288 | tf_op jit(solution)/shard_map/ppermute | solution.py:212
  41.1 14.2 %collective-permute-start.7 = (bf16[192,640]{1,0:T(8,128)(2,1)S(1)}, bf16[192,640]{1,0:T(8,128)(2,1)S(1)}, u32[]{:S(2)}, u32[]{:S(2)}) collective-permute-start(bf16[192,640]{1,0:T(8,128)(2,1)S(1)} %collective-permute-done.4.refs_2_), channel_id=1, source_target_pairs={{0,1},{1,0},{2,3},{3,2},{4,5},{5,4},{6,7},{7,6},{8,9},{9,8},{10,11... | collective-permute-start | bytes 737288 | tf_op jit(solution)/shard_map/ppermute | solution.py:212
  41.2 10.1 %collective-permute-start.15 = (bf16[192,640]{1,0:T(8,128)(2,1)S(1)}, bf16[192,640]{1,0:T(8,128)(2,1)S(1)}, u32[]{:S(2)}, u32[]{:S(2)}) collective-permute-start(bf16[192,640]{1,0:T(8,128)(2,1)S(1)} %collective-permute-done.11.refs_8_), channel_id=1, source_target_pairs={{0,2},{1,3},{2,0},{3,1},{4,6},{5,7},{6,4},{7,5},{8,10},{9,11},{10,... | collective-permute-start | bytes 737288 | tf_op jit(solution)/shard_map/ppermute | solution.py:212
  42.8 12.1 %collective-permute-start.16 = (bf16[192,640]{1,0:T(8,128)(2,1)S(1)}, bf16[192,640]{1,0:T(8,128)(2,1)S(1)}, u32[]{:S(2)}, u32[]{:S(2)}) collective-permute-start(bf16[192,640]{1,0:T(8,128)(2,1)S(1)} %collective-permute-done.12.refs_12_), channel_id=1, source_target_pairs={{0,2},{1,3},{2,0},{3,1},{4,6},{5,7},{6,4},{7,5},{8,10},{9,11},{10,... | collective-permute-start | bytes 737288 | tf_op jit(solution)/shard_map/ppermute | solution.py:212
  43.3 14.1 %copy-start.2 = (s32[2,12]{1,0:T(2,128)S(1)}, s32[2,12]{1,0:T(2,128)}, u32[]{:S(2)}) copy-start(s32[2,12]{1,0:T(2,128)} %pick_ref.1) | copy-start | bytes 292
  51.4 5.3 %collective-permute-start.14 = (bf16[192,640]{1,0:T(8,128)(2,1)S(1)}, bf16[192,640]{1,0:T(8,128)(2,1)S(1)}, u32[]{:S(2)}, u32[]{:S(2)}) collective-permute-start(bf16[192,640]{1,0:T(8,128)(2,1)S(1)} %collective-permute-done.11.refs_8_), channel_id=1, source_target_pairs={{0,1},{1,0},{2,3},{3,2},{4,5},{5,4},{6,7},{7,6},{8,9},{9,8},{10,11... | collective-permute-start | bytes 737288 | tf_op jit(solution)/shard_map/ppermute | solution.py:212
  54.9 1.9 %collective-permute-start.18 = (bf16[192,640]{1,0:T(8,128)(2,1)S(1)}, bf16[192,640]{1,0:T(8,128)(2,1)S(1)}, u32[]{:S(2)}, u32[]{:S(2)}) collective-permute-start(bf16[192,640]{1,0:T(8,128)(2,1)S(1)} %collective-permute-done.12.refs_12_), channel_id=1, source_target_pairs={{0,1},{1,0},{2,3},{3,2},{4,5},{5,4},{6,7},{7,6},{8,9},{9,8},{10,11... | collective-permute-start | bytes 737288 | tf_op jit(solution)/shard_map/ppermute | solution.py:212
  54.9 1.9 %collective-permute-start.13 = (bf16[192,640]{1,0:T(8,128)(2,1)S(1)}, bf16[192,640]{1,0:T(8,128)(2,1)S(1)}, u32[]{:S(2)}, u32[]{:S(2)}) collective-permute-start(bf16[192,640]{1,0:T(8,128)(2,1)S(1)} %collective-permute-done.9.refs_6_), channel_id=1, source_target_pairs={{0,1},{1,0},{2,3},{3,2},{4,5},{5,4},{6,7},{7,6},{8,9},{9,8},{10,11... | collective-permute-start | bytes 737288 | tf_op jit(solution)/shard_map/ppermute | solution.py:212
  55.4 1.7 %collective-permute-start.17 = (bf16[192,640]{1,0:T(8,128)(2,1)S(1)}, bf16[192,640]{1,0:T(8,128)(2,1)S(1)}, u32[]{:S(2)}, u32[]{:S(2)}) collective-permute-start(bf16[192,640]{1,0:T(8,128)(2,1)S(1)} %collective-permute-done.15.refs_10_), channel_id=1, source_target_pairs={{0,1},{1,0},{2,3},{3,2},{4,5},{5,4},{6,7},{7,6},{8,9},{9,8},{10,11... | collective-permute-start | bytes 737288 | tf_op jit(solution)/shard_map/ppermute | solution.py:212
  55.4 2.0 %collective-permute-start.19 = (bf16[192,640]{1,0:T(8,128)(2,1)S(1)}, bf16[192,640]{1,0:T(8,128)(2,1)S(1)}, u32[]{:S(2)}, u32[]{:S(2)}) collective-permute-start(bf16[192,640]{1,0:T(8,128)(2,1)S(1)} %collective-permute-done.16.refs_14_), channel_id=1, source_target_pairs={{0,1},{1,0},{2,3},{3,2},{4,5},{5,4},{6,7},{7,6},{8,9},{9,8},{10,11... | collective-permute-start | bytes 737288 | tf_op jit(solution)/shard_map/ppermute | solution.py:212

commit v3 on v2

--- a/solution.py
+++ b/solution.py
@@ -16,7 +16,7 @@
 IDX = 128
 BLK = 64
 LANES = 128
-TILE = 256
+TILE = 512
 TOK_TILE = 32
 HEAD_STEP = 16
 PAIRS = 8
@@ -26,12 +26,12 @@
 VMEM = 48 * 2**20
 
 
-def index_tile(iq_ref, wide_ref, keys):
+def index_tile(iq_ref, weights, keys):
     keys_t = keys.T
-    rows = iq_ref.shape[0]
+    rows, width = iq_ref.shape[0], keys.shape[0]
     parts = []
     for t0 in range(0, rows, TOK_TILE):
-        acc = jnp.zeros((TOK_TILE, TILE), jnp.float32)
+        acc = jnp.zeros((TOK_TILE, width), jnp.float32)
         for j0 in range(0, IH, HEAD_STEP):
             lhs = jnp.concatenate(
                 [
@@ -42,63 +42,59 @@
             )
             prod = jnp.dot(lhs, keys_t, preferred_element_type=jnp.float32)
             for j in range(HEAD_STEP):
-                weight = wide_ref[j0 + j, t0 : t0 + TOK_TILE, :]
-                weight = jnp.concatenate([weight] * (TILE // LANES), 1)
+                weight = jnp.broadcast_to(
+                    weights[t0 : t0 + TOK_TILE, j0 + j : j0 + j + 1], (TOK_TILE, LANES)
+                )
+                weight = jnp.concatenate([weight] * (width // LANES), 1)
                 acc = acc + jnp.maximum(prod[j * TOK_TILE : (j + 1) * TOK_TILE], 0.0) * weight
         parts.append(acc)
     return jnp.concatenate(parts, 0)
 
 
-def spread_weights(w_ref, wide_ref):
-    for j in range(IH):
-        wide_ref[j] = jnp.broadcast_to(w_ref[:, j : j + 1] * IDX**-0.5, wide_ref.shape[1:])
-
-
-def index_window_kernel(rels, iq_ref, w_ref, keys_ref, out_ref, wide_ref):
+def index_window_kernel(shards, iq_ref, w_ref, keys_ref, out_ref):
     tok = iq_ref.shape[0]
     span = BLK + tok
-    spread_weights(w_ref, wide_ref)
-
-    @pl.loop(0, len(rels) // 2)
-    def _(pair):
-        first = keys_ref[pl.ds(pl.multiple_of(2 * pair * span + BLK, BLK), tok), :]
-        second = keys_ref[pl.ds(pl.multiple_of((2 * pair + 1) * span + BLK, BLK), tok), :]
-        value = index_tile(iq_ref, wide_ref, jnp.concatenate([first, second], 0))
-        out_ref[2 * pair] = value[:, :LANES]
-        out_ref[2 * pair + 1] = value[:, LANES:]
-
-
-def index_prefix_kernel(
-    near, far, own_ref, iq_ref, w_ref, near_ref, far_ref, near_done, far_done, prefix_ref,
-    window_ref, wide_ref, keys_ref, res_ref,
-):
+    each = TILE // tok
+    weights = w_ref[...].T * IDX**-0.5
+
+    @pl.loop(0, shards // each)
+    def _(step):
+        keys = [
+            keys_ref[pl.ds(pl.multiple_of((step * each + n) * span + BLK, BLK), tok), :]
+            for n in range(each)
+        ]
+        value = index_tile(iq_ref, weights, jnp.concatenate(keys, 0))
+        for n in range(each):
+            out_ref[step * each + n] = value[:, n * tok : (n + 1) * tok]
+
+
+def index_prefix_kernel(places, *refs):
+    count = len(places)
+    own_ref, iq_ref, w_ref = refs[:3]
+    key_refs, done_refs = refs[3 : 3 + count], refs[3 + count : 3 + 2 * count]
+    prefix_ref, window_ref, keys_ref = refs[3 + 2 * count :]
     own = own_ref[0]
     tok = iq_ref.shape[0]
     span = BLK + tok
-    spread_weights(w_ref, wide_ref)
-    for ref, rels in ((near_ref, near), (far_ref, far)):
+    weights = w_ref[...].T * IDX**-0.5
+    for ref, rels in zip(key_refs, places):
         for n, rel in enumerate(rels):
             at = pl.multiple_of((own ^ rel) * BLK, BLK)
             keys_ref[pl.ds(at, BLK), :] = ref[n * span : n * span + BLK, :]
-
-    @pl.loop(0, keys_ref.shape[0] // TILE)
-    def _(tile):
-        keys = keys_ref[pl.ds(pl.multiple_of(tile * TILE, TILE), TILE), :]
-        value = index_tile(iq_ref, wide_ref, keys)
-        res_ref[2 * tile] = value[:, :LANES]
-        res_ref[2 * tile + 1] = value[:, LANES:]
-
-    for n in range(keys_ref.shape[0] // LANES):
-        prefix_ref[:, n * LANES : (n + 1) * LANES] = res_ref[n]
     row = lax.broadcasted_iota(jnp.int32, (tok, LANES), 0)
     lane = lax.broadcasted_iota(jnp.int32, (tok, LANES), 1)
-    for rels, ref in ((near, near_done), (far, far_done)):
+    for ref, rels in zip(done_refs, places):
         for n, rel in enumerate(rels):
             other = own ^ rel
             seen = other * tok + lane <= own * tok + row
             window_ref[:, pl.ds(pl.multiple_of(other * tok, LANES), LANES)] = jnp.where(
                 seen, ref[n], 0.0
             )
+
+    @pl.loop(0, keys_ref.shape[0] // TILE)
+    def _(step):
+        at = pl.multiple_of(step * TILE, TILE)
+        prefix_ref[:, pl.ds(at, TILE)] = index_tile(iq_ref, weights, keys_ref[pl.ds(at, TILE), :])
 
 
 def attention_kernel(devices, own_ref, pick_ref, q_ref, *refs):
@@ -221,69 +217,100 @@
             flops=2 * tok * IH * IDX * keys * 4, bytes_accessed=2**22, transcendentals=0
         )
 
-    def index_window(rels, shard_keys):
+    weights = index_weights.T
+
+    def index_window(shard_keys):
+        count = shard_keys.shape[0] // span
         return pl.pallas_call(
-            functools.partial(index_window_kernel, rels),
-            out_shape=jax.ShapeDtypeStruct((len(rels), tok, LANES), jnp.float32),
+            functools.partial(index_window_kernel, count),
+            out_shape=jax.ShapeDtypeStruct((count, tok, LANES), jnp.float32),
             in_specs=[vmem, vmem, vmem],
             out_specs=vmem,
-            scratch_shapes=[pltpu.VMEM((IH, tok, LANES), jnp.float32)],
             compiler_params=params,
-            cost_estimate=index_cost(len(rels) * tok),
-        )(index_queries, index_weights, shard_keys)
+            cost_estimate=index_cost(count * tok),
+        )(index_queries, weights, shard_keys)
 
     def after(done, *arrays):
         return lax.optimization_barrier((done, *arrays))[1:]
 
-    line = list(range(0, devices, 4))
-    keys = jnp.concatenate([prefix_index_keys, window_index_keys], 0)
-    key_line = jnp.concatenate([keys] + [swap(keys, rel) for rel in line[1:]], 0)
-    near_keys = jnp.concatenate([key_line, swap(key_line, 2)], 0)
-    near = line + [rel + 2 for rel in line]
-    far_keys = swap(near_keys, 1)
-    far = [rel + 1 for rel in near]
+    bits = []
+    bit = devices // 2
+    while bit >= 4:
+        bits.append(bit)
+        bit //= 2
 
     rows = jnp.concatenate([prefix_latent, window_latent], 0).reshape(3 * BLK, ROW)
     rows = jnp.pad(rows, ((0, 0), (0, WIDE - ROW)))
-    shards = [None] * devices
-    shards[0] = rows
-    for rel in line[1:]:
-        shards[rel] = swap(rows, rel)
-    shards[2] = swap(rows, 2)
-
-    near_done = index_window(near, near_keys)
-    first, rest = line[1], line[2:]
-    held = [0, 2, first]
-    for rel, array in zip(held, after(near_done, *[shards[rel] for rel in held])):
-        shards[rel + 1] = swap(array, 1)
-        if rel == first:
-            shards[rel + 2] = swap(array, 2)
-    far_done = index_window(far, far_keys)
-    held = rest + [first + 2]
-    for rel, array in zip(held, after(far_done, *[shards[rel] for rel in held])):
-        shards[rel + 1] = swap(array, 1)
-        if rel in rest:
-            shards[rel + 2] = swap(array, 2)
+    shards = {0: rows}
+    for bit in bits + [2]:
+        shards[bit] = swap(rows, bit)
+
+    line, key_line = [0], jnp.concatenate([prefix_index_keys, window_index_keys], 0)
+    (key_line,) = after(rows, key_line)
+    for bit in bits:
+        key_line = jnp.concatenate([key_line, swap(key_line, bit)], 0)
+        line = line + [rel ^ bit for rel in line]
+    key_side = swap(key_line, 2)
+    side = [rel ^ 2 for rel in line]
+    key_far = swap(jnp.concatenate([key_line, key_side], 0), 1)
+    far = [rel ^ 1 for rel in line + side]
+
+    low, high = bits[-1], bits[:-1]
+
+    def send(done, *moves):
+        sources = sorted({rel for rel, _ in moves})
+        held = dict(zip(sources, after(done, *[shards[rel] for rel in sources])))
+        for rel, bit in moves:
+            shards[rel ^ bit] = swap(held[rel], bit)
+
+    line_done = index_window(key_line)
+    send(line_done, (0, 1), (2, 1), (low, 2), (low, 1))
+    side_done = index_window(key_side)
+    reach = list(high)
+    moves = []
+    for n, bit in enumerate(high):
+        moves += [(bit, 2), (bit, 1)]
+    send(side_done, *moves)
+    rest = []
+    for n, bit in enumerate(high):
+        for other in bits[n + 1 :]:
+            for rel in [r for r in [bit] + rest if not r & (2 * other - 1) and r & -r > other]:
+                (held,) = after(side_done, shards[rel])
+                shards[rel ^ other] = swap(held, other)
+                rest.append(rel ^ other)
+    far_done = index_window(key_far)
+    send(
+        far_done,
+        (low | 2, 1),
+        *[(bit | 2, 1) for bit in high],
+        *[(rel, 2) for rel in rest],
+        *[(rel, 1) for rel in rest],
+    )
 
     prefix_index, window_index = pl.pallas_call(
-        functools.partial(index_prefix_kernel, near, far),
+        functools.partial(index_prefix_kernel, [line, side, far]),
         out_shape=(
             jax.ShapeDtypeStruct((tok, devices * BLK), jnp.float32),
             jax.ShapeDtypeStruct((tok, devices * tok), jnp.float32),
         ),
-        in_specs=[smem] + [vmem] * 6,
+        in_specs=[smem] + [vmem] * 8,
         out_specs=(vmem, vmem),
-        scratch_shapes=[
-            pltpu.VMEM((IH, tok, LANES), jnp.float32),
-            pltpu.VMEM((devices * BLK, IDX), jnp.bfloat16),
-            pltpu.VMEM((devices * BLK // LANES, tok, LANES), jnp.float32),
-        ],
+        scratch_shapes=[pltpu.VMEM((devices * BLK, IDX), jnp.bfloat16)],
         compiler_params=params,
         cost_estimate=index_cost(devices * BLK),
-    )(own, index_queries, index_weights, near_keys, far_keys, near_done, far_done)
-    held = [rel + 2 for rel in rest]
-    for rel, array in zip(held, after(prefix_index, *[shards[rel] for rel in held])):
-        shards[rel + 1] = swap(array, 1)
+    )(
+        own,
+        index_queries,
+        weights,
+        key_line,
+        key_side,
+        key_far,
+        line_done,
+        side_done,
+        far_done,
+    )
+    send(prefix_index, *[(rel | 2, 1) for rel in rest])
+    shards = [shards[rel] for rel in range(devices)]
 
     count = picks.shape[1] * BLK
     attention = pl.pallas_call(

time: 82.7 us -> 79.1 us (0.956)
  Pallas kernels: 45.8 us -> 41.2 us
  local copies, waits for them, and re-layouts: 4.36 us -> 2.71 us
  waiting for transfers between devices: 13.4 us -> 14.8 us
    pallas_call x3 -> x4, Pallas kernels: 21.1 us -> 16.4 us  [the longest x3 10.2 us: index_window(): pl.pallas_call(functools.partial(index_window_kernel, count), out_shape=j...]
    unnamed x11 -> x10, local copies, waits for them, and re-layouts: 3.98 us -> 2.37 us
    ppermute x20 -> x19, waiting for transfers between devices: 13.4 us -> 14.8 us  [swap(): return lax.ppermute(array, 'ctx', [(i, i ^ rel) for i in range(devices)])]
    ppermute x20 -> x19, starting transfers between devices: 16.5 us -> 17.1 us  [swap(): return lax.ppermute(array, 'ctx', [(i, i ^ rel) for i in range(devices)])]
  transfers between devices with their start and end apart: 20 -> 19, of which waited for: 6 -> 7; matrix products, arithmetic and copies ran while one was open for 3% -> 1% of each run, Pallas kernels for 26% -> 21%
where the time goes in v3:
time: 79.1 us; the launch traced here: 78.8 us
  Pallas kernels  41.2 us (52%)
  starting transfers between devices  17.1 us (22%)
  waiting for transfers between devices  14.8 us (19%)
  local copies, waits for them, and re-layouts  2.71 us (3%)
  other arithmetic  2.09 us (3%)
  between operations  0.93 us (1%)
    pallas_call x1, Pallas kernels, body(): pl.pallas_call(functools.partial(attention_kernel, devices), grid_spec=pl...  24.8 us
    ppermute x19, starting transfers between devices, swap(): return lax.ppermute(array, 'ctx', [(i, i ^ rel) for i in range(devices)])  17.1 us
    ppermute x19, waiting for transfers between devices, swap(): return lax.ppermute(array, 'ctx', [(i, i ^ rel) for i in range(devices)])  14.8 us
    pallas_call x3, Pallas kernels, index_window(): pl.pallas_call(functools.partial(index_window_kernel, count), out_shape=j...  10.2 us
    pallas_call x1, Pallas kernels, body(): pl.pallas_call(functools.partial(index_prefix_kernel, [line, side, far]),...  6.24 us
    unnamed x10, local copies, waits for them, and re-layouts  2.37 us
  transfers between devices with their start and end apart: 19, of which 7 were waited for; matrix products, arithmetic and copies ran while one was open for 1% of the time, Pallas kernels for 21%

profile of v3, /device:TPU:0, one launch (start us, length us, event | category | flops | bytes accessed | tf_op | source)
XLA Modules:
  0.0 78.8 jit_solution(6974431843094581653)
XLA Ops:
  0.6 1.3 %pad_maximum_fusion.1 = bf16[3,36864]{1,0:T(4,128)(2,1)S(1)} fusion(bf16[2,36864]{1,0:T(2,128)(2,1)} %param.10, bf16[1,36864]{1,0:T(2,128)(2,1)} %param.9), kind=kLoop, calls=%fused_computation.1 | loop fusion | flops 442368 | bytes 442368 | tf_op jit(solution)/shard_map/concatenate | solution.py:242
  1.9 0.3 reshape.13
  2.3 4.1 %collective-permute-start.10 = (bf16[192,640]{1,0:T(8,128)(2,1)S(1)}, bf16[192,640]{1,0:T(8,128)(2,1)S(1)}, u32[]{:S(2)}, u32[]{:S(2)}) collective-permute-start(bf16[192,640]{1,0:T(8,128)(2,1)S(1)} %pad.4.refs_0_), channel_id=1, source_target_pairs={{0,8},{1,9},{2,10},{3,11},{4,12},{5,13},{6,14},{7,15},{8,0},{9,1},... | collective-permute-start | bytes 737288 | tf_op jit(solution)/shard_map/ppermute | solution.py:208
  6.4 1.6 %collective-permute-start.3 = (bf16[192,640]{1,0:T(8,128)(2,1)S(1)}, bf16[192,640]{1,0:T(8,128)(2,1)S(1)}, u32[]{:S(2)}, u32[]{:S(2)}) collective-permute-start(bf16[192,640]{1,0:T(8,128)(2,1)S(1)} %pad.4.refs_0_), channel_id=1, source_target_pairs={{0,4},{1,5},{2,6},{3,7},{4,0},{5,1},{6,2},{7,3},{8,12},{9,13},{10,... | collective-permute-start | bytes 737288 | tf_op jit(solution)/shard_map/ppermute | solution.py:208
  7.9 1.5 %collective-permute-start.2 = (bf16[192,640]{1,0:T(8,128)(2,1)S(1)}, bf16[192,640]{1,0:T(8,128)(2,1)S(1)}, u32[]{:S(2)}, u32[]{:S(2)}) collective-permute-start(bf16[192,640]{1,0:T(8,128)(2,1)S(1)} %pad.4.refs_0_), channel_id=1, source_target_pairs={{0,2},{1,3},{2,0},{3,1},{4,6},{5,7},{6,4},{7,5},{8,10},{9,11},{10,... | collective-permute-start | bytes 737288 | tf_op jit(solution)/shard_map/ppermute | solution.py:208
  9.5 0.8 pad_maximum_fusion.3
  10.2 0.3 collective-permute-start
  10.6 8.6 %collective-permute-done = bf16[192,128]{1,0:T(8,128)(2,1)S(1)} collective-permute-done((bf16[192,128]{1,0:T(8,128)(2,1)S(1)}, bf16[192,128]{1,0:T(8,128)(2,1)S(1)}, u32[]{:S(2)}, u32[]{:S(2)}) %collective-permute-start) | collective-permute-done | bytes 49184 | tf_op jit(solution)/shard_map/ppermute | solution.py:208
  19.2 1.2 %collective-permute-start.1 = (bf16[384,128]{1,0:T(8,128)(2,1)S(1)}, bf16[384,128]{1,0:T(8,128)(2,1)S(1)}, u32[]{:S(2)}, u32[]{:S(2)}) collective-permute-start(bf16[384,128]{1,0:T(8,128)(2,1)S(1)} %pad_maximum_fusion.2), channel_id=1, source_target_pairs={{0,4},{1,5},{2,6},{3,7},{4,0},{5,1},{6,2},{7,3},{8,12},{9,13},{10,... | collective-permute-start | bytes 294920 | tf_op jit(solution)/shard_map/ppermute | solution.py:208
  20.5 3.4 %collective-permute-done.1 = bf16[384,128]{1,0:T(8,128)(2,1)S(1)} collective-permute-done((bf16[384,128]{1,0:T(8,128)(2,1)S(1)}, bf16[384,128]{1,0:T(8,128)(2,1)S(1)}, u32[]{:S(2)}, u32[]{:S(2)}) %collective-permute-start.1) | collective-permute-done | bytes 98336 | tf_op jit(solution)/shard_map/ppermute | solution.py:208
  23.9 1.6 %collective-permute-start.8 = (bf16[768,128]{1,0:T(8,128)(2,1)S(1)}, bf16[768,128]{1,0:T(8,128)(2,1)S(1)}, u32[]{:S(2)}, u32[]{:S(2)}) collective-permute-start(bf16[768,128]{1,0:T(8,128)(2,1)S(1)} %constant_dynamic-update-slice_fusion.keys_ref.refs_3_), channel_id=1, source_target_pairs={{0,2},{1,3},{2,0},{3,1},{4,6},{5,7},{6,4},{7,5},{8,10},{9,11},{10,... | collective-permute-start | bytes 589832 | tf_op jit(solution)/shard_map/ppermute | solution.py:208
  25.6 1.6 %copy-done = bf16[128,8192]{1,0:T(8,128)(2,1)S(1)} copy-done((bf16[128,8192]{1,0:T(8,128)(2,1)S(1)}, bf16[128,8192]{1,0:T(8,128)(2,1)}, u32[]{:S(2)}) %copy-start) | copy-done | bytes 2097176
  27.2 0.8 copy-done.2
  27.9 2.5 %shard_map.103.refs_6_ = f32[4,128,128]{2,1,0:T(8,128)S(1)} custom-call(bf16[128,8192]{1,0:T(8,128)(2,1)S(1)} %copy-done, f32[64,128]{1,0:T(8,128)S(1)} %bitcast.2, bf16[768,128]{1,0:T(8,128)(2,1)S(1)} %constant_dynamic-update-slice_fusion.keys_ref.refs_3_), custom_call_target="tpu_custom_call" | custom-call | flops 4294967296 | bytes 4194304 | tf_op jit(solution)/shard_map/pallas_call | solution.py:224
  30.4 0.5 collective-permute-start.7
  31.0 0.5 collective-permute-start.4
  31.6 2.5 %shard_map.105.refs_7_ = f32[4,128,128]{2,1,0:T(8,128)S(1)} custom-call(bf16[128,8192]{1,0:T(8,128)(2,1)S(1)} %copy-done, f32[64,128]{1,0:T(8,128)S(1)} %bitcast.3, bf16[768,128]{1,0:T(8,128)(2,1)S(1)} %collective-permute-done.8.keys_ref.refs_4_), custom_call_target="tpu_custom_call" | custom-call | flops 4294967296 | bytes 4194304 | tf_op jit(solution)/shard_map/pallas_call | solution.py:224
  34.1 1.3 %collective-permute-start.12 = (bf16[192,640]{1,0:T(8,128)(2,1)S(1)}, bf16[192,640]{1,0:T(8,128)(2,1)S(1)}, u32[]{:S(2)}, u32[]{:S(2)}) collective-permute-start(bf16[192,640]{1,0:T(8,128)(2,1)S(1)} %collective-permute-done.10.refs_8_), channel_id=1, source_target_pairs={{0,4},{1,5},{2,6},{3,7},{4,0},{5,1},{6,2},{7,3},{8,12},{9,13},{10,... | collective-permute-start | bytes 737288 | tf_op jit(solution)/shard_map/ppermute | solution.py:208
  35.4 1.5 %collective-permute-start.11 = (bf16[192,640]{1,0:T(8,128)(2,1)S(1)}, bf16[192,640]{1,0:T(8,128)(2,1)S(1)}, u32[]{:S(2)}, u32[]{:S(2)}) collective-permute-start(bf16[192,640]{1,0:T(8,128)(2,1)S(1)} %collective-permute-done.10.refs_8_), channel_id=1, source_target_pairs={{0,2},{1,3},{2,0},{3,1},{4,6},{5,7},{6,4},{7,5},{8,10},{9,11},{10,... | collective-permute-start | bytes 737288 | tf_op jit(solution)/shard_map/ppermute | solution.py:208
  36.9 5.2 %shard_map.104.refs_8_ = f32[8,128,128]{2,1,0:T(8,128)S(1)} custom-call(bf16[128,8192]{1,0:T(8,128)(2,1)S(1)} %copy-done, f32[64,128]{1,0:T(8,128)S(1)} %bitcast.4, bf16[1536,128]{1,0:T(8,128)(2,1)S(1)} %collective-permute-done.9.keys_ref.refs_5_), custom_call_target="tpu_custom_call" | custom-call | flops 8589934592 | bytes 4194304 | tf_op jit(solution)/shard_map/pallas_call | solution.py:224
  42.1 0.1 collective-permute-start.5
  42.2 0.3 collective-permute-done.12.refs_12_
  42.5 0.2 collective-permute-start.14
  42.7 0.8 %collective-permute-done.11.refs_10_ = bf16[192,640]{1,0:T(8,128)(2,1)S(1)} collective-permute-done((bf16[192,640]{1,0:T(8,128)(2,1)S(1)}, bf16[192,640]{1,0:T(8,128)(2,1)S(1)}, u32[]{:S(2)}, u32[]{:S(2)}) %collective-permute-start.11) | collective-permute-done | bytes 245792 | tf_op jit(solution)/shard_map/ppermute | solution.py:208
  43.5 1.5 %collective-permute-start.17 = (bf16[192,640]{1,0:T(8,128)(2,1)S(1)}, bf16[192,640]{1,0:T(8,128)(2,1)S(1)}, u32[]{:S(2)}, u32[]{:S(2)}) collective-permute-start(bf16[192,640]{1,0:T(8,128)(2,1)S(1)} %collective-permute-done.12.refs_12_), channel_id=1, source_target_pairs={{0,2},{1,3},{2,0},{3,1},{4,6},{5,7},{6,4},{7,5},{8,10},{9,11},{10,... | collective-permute-start | bytes 737288 | tf_op jit(solution)/shard_map/ppermute | solution.py:208
  45.0 6.2 %shard_map.106 = (f32[128,1024]{1,0:T(8,128)}, f32[128,2048]{1,0:T(8,128)}) custom-call(s32[1]{0:T(128)} %bitcast.refs_0_.own_ref, bf16[128,8192]{1,0:T(8,128)(2,1)S(1)} %copy-done.1, f32[64,128]{1,0:T(8,128)S(1)} %bitcast.5, bf16[768,128]{1,0:T(8,128)(2,1)S(1)} %constant_dynamic-update-slice_fusion.keys_ref.refs_3_, ...), custom_call_target="tpu_custom_call" | custom-call | flops 8589934592 | bytes 4194304 | tf_op jit(solution)/shard_map/pallas_call | solution.py:290
  51.3 0.5 collective-permute-start.13
  51.9 0.4 collective-permute-start.18
  52.3 0.8 %collective-permute-done.13.refs_7_ = bf16[192,640]{1,0:T(8,128)(2,1)S(1)} collective-permute-done((bf16[192,640]{1,0:T(8,128)(2,1)S(1)}, bf16[192,640]{1,0:T(8,128)(2,1)S(1)}, u32[]{:S(2)}, u32[]{:S(2)}) %collective-permute-start.13) | collective-permute-done | bytes 245792 | tf_op jit(solution)/shard_map/ppermute | solution.py:208
  53.1 0.4 collective-permute-done.15.refs_11_
  53.5 0.3 collective-permute-done.18.refs_15_
  53.8 24.8 %shard_map.107 = bf16[128,32768]{1,0:T(8,128)(2,1)} custom-call(s32[1]{0:T(128)} %bitcast.refs_0_.own_ref, s32[2,12]{1,0:T(2,128)S(1)} %copy-done.3, bf16[128,36864]{1,0:T(8,128)(2,1)} %q_ref.1, bf16[192,640]{1,0:T(8,128)(2,1)S(1)} %pad.4.refs_0_, bf16[192,640]{1,0:T(8,128)(2,1)S(1)} %collective-permute-done.4.refs_1_, ...), custom_call_target="tpu_custom_call" | custom-call | flops 14495514624 | bytes 16777216 | tf_op jit(solution)/shard_map/pallas_call | solution.py:316
  (28 shorter events, 0.3 us)
Async XLA Ops:
  2.3 31.9 %collective-permute-start.10 = (bf16[192,640]{1,0:T(8,128)(2,1)S(1)}, bf16[192,640]{1,0:T(8,128)(2,1)S(1)}, u32[]{:S(2)}, u32[]{:S(2)}) collective-permute-start(bf16[192,640]{1,0:T(8,128)(2,1)S(1)} %pad.4.refs_0_), channel_id=1, source_target_pairs={{0,8},{1,9},{2,10},{3,11},{4,12},{5,13},{6,14},{7,15},{8,0},{9,1},... | collective-permute-start | bytes 737288 | tf_op jit(solution)/shard_map/ppermute | solution.py:208
  6.4 24.0 %collective-permute-start.3 = (bf16[192,640]{1,0:T(8,128)(2,1)S(1)}, bf16[192,640]{1,0:T(8,128)(2,1)S(1)}, u32[]{:S(2)}, u32[]{:S(2)}) collective-permute-start(bf16[192,640]{1,0:T(8,128)(2,1)S(1)} %pad.4.refs_0_), channel_id=1, source_target_pairs={{0,4},{1,5},{2,6},{3,7},{4,0},{5,1},{6,2},{7,3},{8,12},{9,13},{10,... | collective-permute-start | bytes 737288 | tf_op jit(solution)/shard_map/ppermute | solution.py:208
  7.9 22.5 %collective-permute-start.2 = (bf16[192,640]{1,0:T(8,128)(2,1)S(1)}, bf16[192,640]{1,0:T(8,128)(2,1)S(1)}, u32[]{:S(2)}, u32[]{:S(2)}) collective-permute-start(bf16[192,640]{1,0:T(8,128)(2,1)S(1)} %pad.4.refs_0_), channel_id=1, source_target_pairs={{0,2},{1,3},{2,0},{3,1},{4,6},{5,7},{6,4},{7,5},{8,10},{9,11},{10,... | collective-permute-start | bytes 737288 | tf_op jit(solution)/shard_map/ppermute | solution.py:208
  10.2 9.0 %collective-permute-start = (bf16[192,128]{1,0:T(8,128)(2,1)S(1)}, bf16[192,128]{1,0:T(8,128)(2,1)S(1)}, u32[]{:S(2)}, u32[]{:S(2)}) collective-permute-start(bf16[192,128]{1,0:T(8,128)(2,1)S(1)} %pad_maximum_fusion.3), channel_id=1, source_target_pairs={{0,8},{1,9},{2,10},{3,11},{4,12},{5,13},{6,14},{7,15},{8,0},{9,1},... | collective-permute-start | bytes 147464 | tf_op jit(solution)/shard_map/ppermute | solution.py:208
  19.2 4.7 %collective-permute-start.1 = (bf16[384,128]{1,0:T(8,128)(2,1)S(1)}, bf16[384,128]{1,0:T(8,128)(2,1)S(1)}, u32[]{:S(2)}, u32[]{:S(2)}) collective-permute-start(bf16[384,128]{1,0:T(8,128)(2,1)S(1)} %pad_maximum_fusion.2), channel_id=1, source_target_pairs={{0,4},{1,5},{2,6},{3,7},{4,0},{5,1},{6,2},{7,3},{8,12},{9,13},{10,... | collective-permute-start | bytes 294920 | tf_op jit(solution)/shard_map/ppermute | solution.py:208
  23.9 7.6 %collective-permute-start.8 = (bf16[768,128]{1,0:T(8,128)(2,1)S(1)}, bf16[768,128]{1,0:T(8,128)(2,1)S(1)}, u32[]{:S(2)}, u32[]{:S(2)}) collective-permute-start(bf16[768,128]{1,0:T(8,128)(2,1)S(1)} %constant_dynamic-update-slice_fusion.keys_ref.refs_3_), channel_id=1, source_target_pairs={{0,2},{1,3},{2,0},{3,1},{4,6},{5,7},{6,4},{7,5},{8,10},{9,11},{10,... | collective-permute-start | bytes 589832 | tf_op jit(solution)/shard_map/ppermute | solution.py:208
  25.6 1.6 %copy-start = (bf16[128,8192]{1,0:T(8,128)(2,1)S(1)}, bf16[128,8192]{1,0:T(8,128)(2,1)}, u32[]{:S(2)}) copy-start(bf16[128,8192]{1,0:T(8,128)(2,1)} %refs_1_.1) | copy-start | bytes 6291460
  27.2 0.8 copy-start.2
  30.4 11.7 %collective-permute-start.7 = (bf16[192,640]{1,0:T(8,128)(2,1)S(1)}, bf16[192,640]{1,0:T(8,128)(2,1)S(1)}, u32[]{:S(2)}, u32[]{:S(2)}) collective-permute-start(bf16[192,640]{1,0:T(8,128)(2,1)S(1)} %collective-permute-done.3.refs_4_), channel_id=1, source_target_pairs={{0,2},{1,3},{2,0},{3,1},{4,6},{5,7},{6,4},{7,5},{8,10},{9,11},{10,... | collective-permute-start | bytes 737288 | tf_op jit(solution)/shard_map/ppermute | solution.py:208
  31.0 20.9 %collective-permute-start.6 = (bf16[192,640]{1,0:T(8,128)(2,1)S(1)}, bf16[192,640]{1,0:T(8,128)(2,1)S(1)}, u32[]{:S(2)}, u32[]{:S(2)}) collective-permute-start(bf16[192,640]{1,0:T(8,128)(2,1)S(1)} %collective-permute-done.3.refs_4_), channel_id=1, source_target_pairs={{0,1},{1,0},{2,3},{3,2},{4,5},{5,4},{6,7},{7,6},{8,9},{9,8},{10,11... | collective-permute-start | bytes 737288 | tf_op jit(solution)/shard_map/ppermute | solution.py:208
  31.0 20.3 %collective-permute-start.4 = (bf16[192,640]{1,0:T(8,128)(2,1)S(1)}, bf16[192,640]{1,0:T(8,128)(2,1)S(1)}, u32[]{:S(2)}, u32[]{:S(2)}) collective-permute-start(bf16[192,640]{1,0:T(8,128)(2,1)S(1)} %pad.4.refs_0_), channel_id=1, source_target_pairs={{0,1},{1,0},{2,3},{3,2},{4,5},{5,4},{6,7},{7,6},{8,9},{9,8},{10,11... | collective-permute-start | bytes 737288 | tf_op jit(solution)/shard_map/ppermute | solution.py:208
  31.5 3.9 %collective-permute-start.9 = (bf16[1536,128]{1,0:T(8,128)(2,1)S(1)}, bf16[1536,128]{1,0:T(8,128)(2,1)S(1)}, u32[]{:S(2)}, u32[]{:S(2)}) collective-permute-start(bf16[1536,128]{1,0:T(8,128)(2,1)S(1)} %pad_maximum_fusion), channel_id=1, source_target_pairs={{0,1},{1,0},{2,3},{3,2},{4,5},{5,4},{6,7},{7,6},{8,9},{9,8},{10,11... | collective-permute-start | bytes 1179656 | tf_op jit(solution)/shard_map/ppermute | solution.py:208
  34.1 10.9 %copy-start.1 = (bf16[128,8192]{1,0:T(8,128)(2,1)S(1)}, bf16[128,8192]{1,0:T(8,128)(2,1)}, u32[]{:S(2)}) copy-start(bf16[128,8192]{1,0:T(8,128)(2,1)} %refs_1_.1) | copy-start | bytes 6291460
  34.1 8.4 %collective-permute-start.12 = (bf16[192,640]{1,0:T(8,128)(2,1)S(1)}, bf16[192,640]{1,0:T(8,128)(2,1)S(1)}, u32[]{:S(2)}, u32[]{:S(2)}) collective-permute-start(bf16[192,640]{1,0:T(8,128)(2,1)S(1)} %collective-permute-done.10.refs_8_), channel_id=1, source_target_pairs={{0,4},{1,5},{2,6},{3,7},{4,0},{5,1},{6,2},{7,3},{8,12},{9,13},{10,... | collective-permute-start | bytes 737288 | tf_op jit(solution)/shard_map/ppermute | solution.py:208
  35.4 8.1 %collective-permute-start.11 = (bf16[192,640]{1,0:T(8,128)(2,1)S(1)}, bf16[192,640]{1,0:T(8,128)(2,1)S(1)}, u32[]{:S(2)}, u32[]{:S(2)}) collective-permute-start(bf16[192,640]{1,0:T(8,128)(2,1)S(1)} %collective-permute-done.10.refs_8_), channel_id=1, source_target_pairs={{0,2},{1,3},{2,0},{3,1},{4,6},{5,7},{6,4},{7,5},{8,10},{9,11},{10,... | collective-permute-start | bytes 737288 | tf_op jit(solution)/shard_map/ppermute | solution.py:208
  42.1 9.7 %collective-permute-start.5 = (bf16[192,640]{1,0:T(8,128)(2,1)S(1)}, bf16[192,640]{1,0:T(8,128)(2,1)S(1)}, u32[]{:S(2)}, u32[]{:S(2)}) collective-permute-start(bf16[192,640]{1,0:T(8,128)(2,1)S(1)} %collective-permute-done.2.refs_2_), channel_id=1, source_target_pairs={{0,1},{1,0},{2,3},{3,2},{4,5},{5,4},{6,7},{7,6},{8,9},{9,8},{10,11... | collective-permute-start | bytes 737288 | tf_op jit(solution)/shard_map/ppermute | solution.py:208
  42.5 9.8 %collective-permute-start.14 = (bf16[192,640]{1,0:T(8,128)(2,1)S(1)}, bf16[192,640]{1,0:T(8,128)(2,1)S(1)}, u32[]{:S(2)}, u32[]{:S(2)}) collective-permute-start(bf16[192,640]{1,0:T(8,128)(2,1)S(1)} %collective-permute-done.10.refs_8_), channel_id=1, source_target_pairs={{0,1},{1,0},{2,3},{3,2},{4,5},{5,4},{6,7},{7,6},{8,9},{9,8},{10,11... | collective-permute-start | bytes 737288 | tf_op jit(solution)/shard_map/ppermute | solution.py:208
  43.5 7.8 %collective-permute-start.17 = (bf16[192,640]{1,0:T(8,128)(2,1)S(1)}, bf16[192,640]{1,0:T(8,128)(2,1)S(1)}, u32[]{:S(2)}, u32[]{:S(2)}) collective-permute-start(bf16[192,640]{1,0:T(8,128)(2,1)S(1)} %collective-permute-done.12.refs_12_), channel_id=1, source_target_pairs={{0,2},{1,3},{2,0},{3,1},{4,6},{5,7},{6,4},{7,5},{8,10},{9,11},{10,... | collective-permute-start | bytes 737288 | tf_op jit(solution)/shard_map/ppermute | solution.py:208
  45.0 8.8 %copy-start.3 = (s32[2,12]{1,0:T(2,128)S(1)}, s32[2,12]{1,0:T(2,128)}, u32[]{:S(2)}) copy-start(s32[2,12]{1,0:T(2,128)} %pick_ref.1) | copy-start | bytes 292
  51.3 2.2 %collective-permute-start.16 = (bf16[192,640]{1,0:T(8,128)(2,1)S(1)}, bf16[192,640]{1,0:T(8,128)(2,1)S(1)}, u32[]{:S(2)}, u32[]{:S(2)}) collective-permute-start(bf16[192,640]{1,0:T(8,128)(2,1)S(1)} %collective-permute-done.12.refs_12_), channel_id=1, source_target_pairs={{0,1},{1,0},{2,3},{3,2},{4,5},{5,4},{6,7},{7,6},{8,9},{9,8},{10,11... | collective-permute-start | bytes 737288 | tf_op jit(solution)/shard_map/ppermute | solution.py:208
  51.3 1.9 %collective-permute-start.13 = (bf16[192,640]{1,0:T(8,128)(2,1)S(1)}, bf16[192,640]{1,0:T(8,128)(2,1)S(1)}, u32[]{:S(2)}, u32[]{:S(2)}) collective-permute-start(bf16[192,640]{1,0:T(8,128)(2,1)S(1)} %collective-permute-done.7.refs_6_), channel_id=1, source_target_pairs={{0,1},{1,0},{2,3},{3,2},{4,5},{5,4},{6,7},{7,6},{8,9},{9,8},{10,11... | collective-permute-start | bytes 737288 | tf_op jit(solution)/shard_map/ppermute | solution.py:208
  51.8 1.7 %collective-permute-start.15 = (bf16[192,640]{1,0:T(8,128)(2,1)S(1)}, bf16[192,640]{1,0:T(8,128)(2,1)S(1)}, u32[]{:S(2)}, u32[]{:S(2)}) collective-permute-start(bf16[192,640]{1,0:T(8,128)(2,1)S(1)} %collective-permute-done.11.refs_10_), channel_id=1, source_target_pairs={{0,1},{1,0},{2,3},{3,2},{4,5},{5,4},{6,7},{7,6},{8,9},{9,8},{10,11... | collective-permute-start | bytes 737288 | tf_op jit(solution)/shard_map/ppermute | solution.py:208
  51.9 2.0 %collective-permute-start.18 = (bf16[192,640]{1,0:T(8,128)(2,1)S(1)}, bf16[192,640]{1,0:T(8,128)(2,1)S(1)}, u32[]{:S(2)}, u32[]{:S(2)}) collective-permute-start(bf16[192,640]{1,0:T(8,128)(2,1)S(1)} %collective-permute-done.17.refs_14_), channel_id=1, source_target_pairs={{0,1},{1,0},{2,3},{3,2},{4,5},{5,4},{6,7},{7,6},{8,9},{9,8},{10,11... | collective-permute-start | bytes 737288 | tf_op jit(solution)/shard_map/ppermute | solution.py:208

commit v4 on v3

--- a/solution.py
+++ b/solution.py
@@ -26,11 +26,13 @@
 VMEM = 48 * 2**20
 
 
-def index_tile(iq_ref, weights, keys):
+def index_tile(iq_ref, weights, keys, pieces=None):
     keys_t = keys.T
     rows, width = iq_ref.shape[0], keys.shape[0]
     parts = []
     for t0 in range(0, rows, TOK_TILE):
+        if pieces is not None:
+            pieces[t0 // TOK_TILE].wait()
         acc = jnp.zeros((TOK_TILE, width), jnp.float32)
         for j0 in range(0, IH, HEAD_STEP):
             lhs = jnp.concatenate(
@@ -51,19 +53,50 @@
     return jnp.concatenate(parts, 0)
 
 
+def window_keys(keys_ref, tok, each, step):
+    span = BLK + tok
+    return jnp.concatenate(
+        [
+            keys_ref[pl.ds(pl.multiple_of((step * each + n) * span + BLK, BLK), tok), :]
+            for n in range(each)
+        ],
+        0,
+    )
+
+
+def index_line_kernel(shards, iq_hbm, w_hbm, keys_ref, out_ref, iq_ref, w_ref, sem):
+    tok = iq_ref.shape[0]
+    each = TILE // tok
+    w_copy = pltpu.make_async_copy(w_hbm, w_ref, sem.at[tok // TOK_TILE])
+    w_copy.start()
+    pieces = []
+    for n in range(tok // TOK_TILE):
+        part = pl.ds(n * TOK_TILE, TOK_TILE)
+        pieces.append(pltpu.make_async_copy(iq_hbm.at[part], iq_ref.at[part], sem.at[n]))
+        pieces[-1].start()
+    w_copy.wait()
+    weights = w_ref[...].T * IDX**-0.5
+    value = index_tile(iq_ref, weights, window_keys(keys_ref, tok, each, 0), pieces)
+    for n in range(each):
+        out_ref[n] = value[:, n * tok : (n + 1) * tok]
+
+    if shards > each:
+
+        @pl.loop(1, shards // each)
+        def _(step):
+            value = index_tile(iq_ref, weights, window_keys(keys_ref, tok, each, step))
+            for n in range(each):
+                out_ref[step * each + n] = value[:, n * tok : (n + 1) * tok]
+
+
 def index_window_kernel(shards, iq_ref, w_ref, keys_ref, out_ref):
     tok = iq_ref.shape[0]
-    span = BLK + tok
     each = TILE // tok
     weights = w_ref[...].T * IDX**-0.5
 
     @pl.loop(0, shards // each)
     def _(step):
-        keys = [
-            keys_ref[pl.ds(pl.multiple_of((step * each + n) * span + BLK, BLK), tok), :]
-            for n in range(each)
-        ]
-        value = index_tile(iq_ref, weights, jnp.concatenate(keys, 0))
+        value = index_tile(iq_ref, weights, window_keys(keys_ref, tok, each, step))
         for n in range(each):
             out_ref[step * each + n] = value[:, n * tok : (n + 1) * tok]
 
@@ -209,7 +242,7 @@
 
     smem = pl.BlockSpec(memory_space=pltpu.SMEM)
     vmem = pl.BlockSpec(memory_space=pltpu.VMEM)
-    hbm = pl.BlockSpec(memory_space=pl.ANY)
+    hbm = pl.BlockSpec(memory_space=pltpu.HBM)
     params = pltpu.CompilerParams(vmem_limit_bytes=VMEM)
 
     def index_cost(keys):
@@ -218,6 +251,22 @@
         )
 
     weights = index_weights.T
+
+    def index_line(shard_keys):
+        count = shard_keys.shape[0] // span
+        return pl.pallas_call(
+            functools.partial(index_line_kernel, count),
+            out_shape=jax.ShapeDtypeStruct((count, tok, LANES), jnp.float32),
+            in_specs=[hbm, hbm, vmem],
+            out_specs=vmem,
+            scratch_shapes=[
+                pltpu.VMEM((tok, IH * IDX), jnp.bfloat16),
+                pltpu.VMEM((IH, tok), jnp.float32),
+                pltpu.SemaphoreType.DMA((tok // TOK_TILE + 1,)),
+            ],
+            compiler_params=params,
+            cost_estimate=index_cost(count * tok),
+        )(index_queries, weights, shard_keys)
 
     def index_window(shard_keys):
         count = shard_keys.shape[0] // span
@@ -239,23 +288,26 @@
         bits.append(bit)
         bit //= 2
 
+    low, high = bits[-1], bits[:-1]
     rows = jnp.concatenate([prefix_latent, window_latent], 0).reshape(3 * BLK, ROW)
     rows = jnp.pad(rows, ((0, 0), (0, WIDE - ROW)))
     shards = {0: rows}
-    for bit in bits + [2]:
-        shards[bit] = swap(rows, bit)
-
     line, key_line = [0], jnp.concatenate([prefix_index_keys, window_index_keys], 0)
-    (key_line,) = after(rows, key_line)
+    (key_line,) = lax.optimization_barrier((key_line,))
     for bit in bits:
-        key_line = jnp.concatenate([key_line, swap(key_line, bit)], 0)
+        other = swap(key_line, bit)
+        if bit != low:
+            (other, held) = lax.optimization_barrier((other, rows))
+            shards[bit] = swap(held, bit)
+        key_line = jnp.concatenate([key_line, other], 0)
         line = line + [rel ^ bit for rel in line]
+    (held,) = after(key_line, rows)
+    for bit in (low, 2):
+        shards[bit] = swap(held, bit)
     key_side = swap(key_line, 2)
     side = [rel ^ 2 for rel in line]
     key_far = swap(jnp.concatenate([key_line, key_side], 0), 1)
     far = [rel ^ 1 for rel in line + side]
-
-    low, high = bits[-1], bits[:-1]
 
     def send(done, *moves):
         sources = sorted({rel for rel, _ in moves})
@@ -263,14 +315,10 @@
         for rel, bit in moves:
             shards[rel ^ bit] = swap(held[rel], bit)
 
-    line_done = index_window(key_line)
-    send(line_done, (0, 1), (2, 1), (low, 2), (low, 1))
+    line_done = index_line(key_line)
+    send(line_done, (0, 1), (2, 1))
     side_done = index_window(key_side)
-    reach = list(high)
-    moves = []
-    for n, bit in enumerate(high):
-        moves += [(bit, 2), (bit, 1)]
-    send(side_done, *moves)
+    send(side_done, (low, 2), (low, 1), *[(bit, 2) for bit in high], *[(bit, 1) for bit in high])
     rest = []
     for n, bit in enumerate(high):
         for other in bits[n + 1 :]:

time: 79.1 us -> 75.3 us (0.952)
  waiting for transfers between devices: 14.8 us -> 9.33 us
  starting transfers between devices: 17.1 us -> 18.1 us
    ppermute x19, waiting for transfers between devices: 14.8 us -> 9.33 us  [swap(): return lax.ppermute(array, 'ctx', [(i, i ^ rel) for i in range(devices)])]
    pallas_call x0 -> x1, Pallas kernels: none -> 3.2 us  [index_line(): pl.pallas_call(functools.partial(index_line_kernel, count), out_shape=jax...]
    pallas_call x3 -> x2, Pallas kernels: 10.2 us -> 7.5 us  [index_window(): pl.pallas_call(functools.partial(index_window_kernel, count), out_shape=j...]
    ppermute x19, starting transfers between devices: 17.1 us -> 18.1 us  [swap(): return lax.ppermute(array, 'ctx', [(i, i ^ rel) for i in range(devices)])]
    unnamed x10 -> x8, local copies, waits for them, and re-layouts: 2.37 us -> 2.36 us
  transfers between devices with their start and end apart: 19 -> 19, of which waited for: 7 -> 7; matrix products, arithmetic and copies ran while one was open for 1% -> 2% of each run, Pallas kernels for 21% -> 23%
where the time goes in v4:
time: 75.3 us; the launch traced here: 75 us
  Pallas kernels  41.9 us (56%)
  starting transfers between devices  18.1 us (24%)
  waiting for transfers between devices  9.33 us (12%)
  local copies, waits for them, and re-layouts  2.68 us (4%)
  other arithmetic  2.1 us (3%)
  between operations  0.92 us (1%)
    pallas_call x1, Pallas kernels, body(): pl.pallas_call(functools.partial(attention_kernel, devices), grid_spec=pl...  24.9 us
    ppermute x19, starting transfers between devices, swap(): return lax.ppermute(array, 'ctx', [(i, i ^ rel) for i in range(devices)])  18.1 us
    ppermute x19, waiting for transfers between devices, swap(): return lax.ppermute(array, 'ctx', [(i, i ^ rel) for i in range(devices)])  9.33 us
    pallas_call x2, Pallas kernels, index_window(): pl.pallas_call(functools.partial(index_window_kernel, count), out_shape=j...  7.5 us
    pallas_call x1, Pallas kernels, body(): pl.pallas_call(functools.partial(index_prefix_kernel, [line, side, far]),...  6.24 us
    pallas_call x1, Pallas kernels, index_line(): pl.pallas_call(functools.partial(index_line_kernel, count), out_shape=jax...  3.2 us
    unnamed x8, local copies, waits for them, and re-layouts  2.36 us
  transfers between devices with their start and end apart: 19, of which 7 were waited for; matrix products, arithmetic and copies ran while one was open for 2% of the time, Pallas kernels for 23%

profile of v4, /device:TPU:0, one launch (start us, length us, event | category | flops | bytes accessed | tf_op | source)
XLA Modules:
  0.0 75.0 jit_solution(13959426250598980958)
XLA Ops:
  0.6 0.8 %pad_maximum_fusion.4 = bf16[192,128]{1,0:T(8,128)(2,1)S(1)} fusion(bf16[128,128]{1,0:T(8,128)(2,1)} %param.14, bf16[64,128]{1,0:T(8,128)(2,1)} %param.13), kind=kLoop, calls=%fused_computation.4 | loop fusion | flops 98304 | bytes 98304 | tf_op jit(solution)/shard_map/concatenate | solution.py:295
  1.4 4.0 %collective-permute-start = (bf16[192,128]{1,0:T(8,128)(2,1)S(1)}, bf16[192,128]{1,0:T(8,128)(2,1)S(1)}, u32[]{:S(2)}, u32[]{:S(2)}) collective-permute-start(bf16[192,128]{1,0:T(8,128)(2,1)S(1)} %pad_maximum_fusion.4), channel_id=1, source_target_pairs={{0,8},{1,9},{2,10},{3,11},{4,12},{5,13},{6,14},{7,15},{8,0},{9,1},... | collective-permute-start | bytes 147464 | tf_op jit(solution)/shard_map/ppermute | solution.py:241
  5.4 1.3 %pad_maximum_fusion.1 = bf16[3,36864]{1,0:T(4,128)(2,1)S(1)} fusion(bf16[2,36864]{1,0:T(2,128)(2,1)} %param.10, bf16[1,36864]{1,0:T(2,128)(2,1)} %param.9), kind=kLoop, calls=%fused_computation.1 | loop fusion | flops 442368 | bytes 442368 | tf_op jit(solution)/shard_map/concatenate | solution.py:292
  6.7 0.3 reshape.13
  7.1 1.0 %collective-permute-done = bf16[192,128]{1,0:T(8,128)(2,1)S(1)} collective-permute-done((bf16[192,128]{1,0:T(8,128)(2,1)S(1)}, bf16[192,128]{1,0:T(8,128)(2,1)S(1)}, u32[]{:S(2)}, u32[]{:S(2)}) %collective-permute-start) | collective-permute-done | bytes 49184 | tf_op jit(solution)/shard_map/ppermute | solution.py:241
  8.0 1.4 %collective-permute-start.1 = (bf16[384,128]{1,0:T(8,128)(2,1)S(1)}, bf16[384,128]{1,0:T(8,128)(2,1)S(1)}, u32[]{:S(2)}, u32[]{:S(2)}) collective-permute-start(bf16[384,128]{1,0:T(8,128)(2,1)S(1)} %pad_maximum_fusion.3), channel_id=1, source_target_pairs={{0,4},{1,5},{2,6},{3,7},{4,0},{5,1},{6,2},{7,3},{8,12},{9,13},{10,... | collective-permute-start | bytes 294920 | tf_op jit(solution)/shard_map/ppermute | solution.py:241
  9.5 3.0 %collective-permute-start.7 = (bf16[192,640]{1,0:T(8,128)(2,1)S(1)}, bf16[192,640]{1,0:T(8,128)(2,1)S(1)}, u32[]{:S(2)}, u32[]{:S(2)}) collective-permute-start(bf16[192,640]{1,0:T(8,128)(2,1)S(1)} %pad.4.refs_0_), channel_id=1, source_target_pairs={{0,8},{1,9},{2,10},{3,11},{4,12},{5,13},{6,14},{7,15},{8,0},{9,1},... | collective-permute-start | bytes 737288 | tf_op jit(solution)/shard_map/ppermute | solution.py:241
  12.5 1.1 %collective-permute-done.1 = bf16[384,128]{1,0:T(8,128)(2,1)S(1)} collective-permute-done((bf16[384,128]{1,0:T(8,128)(2,1)S(1)}, bf16[384,128]{1,0:T(8,128)(2,1)S(1)}, u32[]{:S(2)}, u32[]{:S(2)}) %collective-permute-start.1) | collective-permute-done | bytes 98336 | tf_op jit(solution)/shard_map/ppermute | solution.py:241
  13.6 1.8 %collective-permute-start.6 = (bf16[768,128]{1,0:T(8,128)(2,1)S(1)}, bf16[768,128]{1,0:T(8,128)(2,1)S(1)}, u32[]{:S(2)}, u32[]{:S(2)}) collective-permute-start(bf16[768,128]{1,0:T(8,128)(2,1)S(1)} %pad_maximum_fusion.2.keys_ref.refs_3_), channel_id=1, source_target_pairs={{0,2},{1,3},{2,0},{3,1},{4,6},{5,7},{6,4},{7,5},{8,10},{9,11},{10,... | collective-permute-start | bytes 589832 | tf_op jit(solution)/shard_map/ppermute | solution.py:241
  15.4 1.0 %collective-permute-start.5 = (bf16[192,640]{1,0:T(8,128)(2,1)S(1)}, bf16[192,640]{1,0:T(8,128)(2,1)S(1)}, u32[]{:S(2)}, u32[]{:S(2)}) collective-permute-start(bf16[192,640]{1,0:T(8,128)(2,1)S(1)} %pad.4.refs_0_), channel_id=1, source_target_pairs={{0,4},{1,5},{2,6},{3,7},{4,0},{5,1},{6,2},{7,3},{8,12},{9,13},{10,... | collective-permute-start | bytes 737288 | tf_op jit(solution)/shard_map/ppermute | solution.py:241
  16.4 0.5 collective-permute-start.2
  16.9 1.6 %copy-done = bf16[128,8192]{1,0:T(8,128)(2,1)S(1)} copy-done((bf16[128,8192]{1,0:T(8,128)(2,1)S(1)}, bf16[128,8192]{1,0:T(8,128)(2,1)}, u32[]{:S(2)}) %copy-start) | copy-done | bytes 2097176
  18.5 0.8 %copy-done.2 = f32[128,64]{0,1:T(8,128)S(1)} copy-done((f32[128,64]{0,1:T(8,128)S(1)}, f32[128,64]{0,1:T(8,128)}, u32[]{:S(2)}) %copy-start.2) | copy-done | bytes 32792
  19.3 3.2 %shard_map.103.refs_6_ = f32[4,128,128]{2,1,0:T(8,128)S(1)} custom-call(bf16[128,8192]{1,0:T(8,128)(2,1)S(1)} %copy-done, f32[64,128]{1,0:T(8,128)S(1)} %bitcast.2, bf16[768,128]{1,0:T(8,128)(2,1)S(1)} %pad_maximum_fusion.2.keys_ref.refs_3_), custom_call_target="tpu_custom_call" | custom-call | flops 4294967296 | bytes 4194304 | tf_op jit(solution)/shard_map/pallas_call | solution.py:257
  22.5 0.1 collective-permute-start.10
  22.6 2.5 %shard_map.104.refs_7_ = f32[4,128,128]{2,1,0:T(8,128)S(1)} custom-call(bf16[128,8192]{1,0:T(8,128)(2,1)S(1)} %copy-done, f32[64,128]{1,0:T(8,128)S(1)} %bitcast.3, bf16[768,128]{1,0:T(8,128)(2,1)S(1)} %collective-permute-done.6.keys_ref.refs_4_), custom_call_target="tpu_custom_call" | custom-call | flops 4294967296 | bytes 4194304 | tf_op jit(solution)/shard_map/pallas_call | solution.py:273
  25.1 0.9 %collective-permute-start.12 = (bf16[192,640]{1,0:T(8,128)(2,1)S(1)}, bf16[192,640]{1,0:T(8,128)(2,1)S(1)}, u32[]{:S(2)}, u32[]{:S(2)}) collective-permute-start(bf16[192,640]{1,0:T(8,128)(2,1)S(1)} %collective-permute-done.7.refs_8_), channel_id=1, source_target_pairs={{0,4},{1,5},{2,6},{3,7},{4,0},{5,1},{6,2},{7,3},{8,12},{9,13},{10,... | collective-permute-start | bytes 737288 | tf_op jit(solution)/shard_map/ppermute | solution.py:241
  26.0 1.7 %collective-permute-start.9 = (bf16[192,640]{1,0:T(8,128)(2,1)S(1)}, bf16[192,640]{1,0:T(8,128)(2,1)S(1)}, u32[]{:S(2)}, u32[]{:S(2)}) collective-permute-start(bf16[192,640]{1,0:T(8,128)(2,1)S(1)} %collective-permute-done.5.refs_4_), channel_id=1, source_target_pairs={{0,2},{1,3},{2,0},{3,1},{4,6},{5,7},{6,4},{7,5},{8,10},{9,11},{10,... | collective-permute-start | bytes 737288 | tf_op jit(solution)/shard_map/ppermute | solution.py:241
  27.7 0.5 collective-permute-start.14
  28.2 0.3 collective-permute-start.11
  28.6 5.0 %shard_map.105.refs_8_ = f32[8,128,128]{2,1,0:T(8,128)S(1)} custom-call(bf16[128,8192]{1,0:T(8,128)(2,1)S(1)} %copy-done, f32[64,128]{1,0:T(8,128)S(1)} %bitcast.4, bf16[1536,128]{1,0:T(8,128)(2,1)S(1)} %collective-permute-done.10.keys_ref.refs_5_), custom_call_target="tpu_custom_call" | custom-call | flops 8589934592 | bytes 4194304 | tf_op jit(solution)/shard_map/pallas_call | solution.py:273
  33.6 0.1 collective-permute-start.3
  33.7 1.1 %collective-permute-done.9.refs_6_ = bf16[192,640]{1,0:T(8,128)(2,1)S(1)} collective-permute-done((bf16[192,640]{1,0:T(8,128)(2,1)S(1)}, bf16[192,640]{1,0:T(8,128)(2,1)S(1)}, u32[]{:S(2)}, u32[]{:S(2)}) %collective-permute-start.9) | collective-permute-done | bytes 245792 | tf_op jit(solution)/shard_map/ppermute | solution.py:241
  34.8 4.6 %collective-permute-done.11.refs_10_ = bf16[192,640]{1,0:T(8,128)(2,1)S(1)} collective-permute-done((bf16[192,640]{1,0:T(8,128)(2,1)S(1)}, bf16[192,640]{1,0:T(8,128)(2,1)S(1)}, u32[]{:S(2)}, u32[]{:S(2)}) %collective-permute-start.11) | collective-permute-done | bytes 245792 | tf_op jit(solution)/shard_map/ppermute | solution.py:241
  39.4 1.7 %collective-permute-start.17 = (bf16[192,640]{1,0:T(8,128)(2,1)S(1)}, bf16[192,640]{1,0:T(8,128)(2,1)S(1)}, u32[]{:S(2)}, u32[]{:S(2)}) collective-permute-start(bf16[192,640]{1,0:T(8,128)(2,1)S(1)} %collective-permute-done.12.refs_12_), channel_id=1, source_target_pairs={{0,2},{1,3},{2,0},{3,1},{4,6},{5,7},{6,4},{7,5},{8,10},{9,11},{10,... | collective-permute-start | bytes 737288 | tf_op jit(solution)/shard_map/ppermute | solution.py:241
  41.1 6.2 %shard_map.106 = (f32[128,1024]{1,0:T(8,128)}, f32[128,2048]{1,0:T(8,128)}) custom-call(s32[1]{0:T(128)} %bitcast.refs_0_.own_ref, bf16[128,8192]{1,0:T(8,128)(2,1)S(1)} %copy-done.1, f32[64,128]{1,0:T(8,128)S(1)} %bitcast.5, bf16[768,128]{1,0:T(8,128)(2,1)S(1)} %pad_maximum_fusion.2.keys_ref.refs_3_, ...), custom_call_target="tpu_custom_call" | custom-call | flops 8589934592 | bytes 4194304 | tf_op jit(solution)/shard_map/pallas_call | solution.py:338
  47.3 0.5 collective-permute-start.13
  47.9 0.4 collective-permute-start.18
  48.4 0.8 %collective-permute-done.13.refs_7_ = bf16[192,640]{1,0:T(8,128)(2,1)S(1)} collective-permute-done((bf16[192,640]{1,0:T(8,128)(2,1)S(1)}, bf16[192,640]{1,0:T(8,128)(2,1)S(1)}, u32[]{:S(2)}, u32[]{:S(2)}) %collective-permute-start.13) | collective-permute-done | bytes 245792 | tf_op jit(solution)/shard_map/ppermute | solution.py:241
  49.2 0.4 collective-permute-done.15.refs_11_
  49.6 0.3 collective-permute-done.18.refs_15_
  49.9 24.9 %shard_map.107 = bf16[128,32768]{1,0:T(8,128)(2,1)} custom-call(s32[1]{0:T(128)} %bitcast.refs_0_.own_ref, s32[2,12]{1,0:T(2,128)S(1)} %copy-done.3, bf16[128,36864]{1,0:T(8,128)(2,1)} %q_ref.1, bf16[192,640]{1,0:T(8,128)(2,1)S(1)} %pad.4.refs_0_, bf16[192,640]{1,0:T(8,128)(2,1)S(1)} %collective-permute-done.3.refs_1_, ...), custom_call_target="tpu_custom_call" | custom-call | flops 14495514624 | bytes 16777216 | tf_op jit(solution)/shard_map/pallas_call | solution.py:364
  (26 shorter events, 0.2 us)
Async XLA Ops:
  1.4 6.6 %collective-permute-start = (bf16[192,128]{1,0:T(8,128)(2,1)S(1)}, bf16[192,128]{1,0:T(8,128)(2,1)S(1)}, u32[]{:S(2)}, u32[]{:S(2)}) collective-permute-start(bf16[192,128]{1,0:T(8,128)(2,1)S(1)} %pad_maximum_fusion.4), channel_id=1, source_target_pairs={{0,8},{1,9},{2,10},{3,11},{4,12},{5,13},{6,14},{7,15},{8,0},{9,1},... | collective-permute-start | bytes 147464 | tf_op jit(solution)/shard_map/ppermute | solution.py:241
  8.0 5.6 %collective-permute-start.1 = (bf16[384,128]{1,0:T(8,128)(2,1)S(1)}, bf16[384,128]{1,0:T(8,128)(2,1)S(1)}, u32[]{:S(2)}, u32[]{:S(2)}) collective-permute-start(bf16[384,128]{1,0:T(8,128)(2,1)S(1)} %pad_maximum_fusion.3), channel_id=1, source_target_pairs={{0,4},{1,5},{2,6},{3,7},{4,0},{5,1},{6,2},{7,3},{8,12},{9,13},{10,... | collective-permute-start | bytes 294920 | tf_op jit(solution)/shard_map/ppermute | solution.py:241
  9.5 15.6 %collective-permute-start.7 = (bf16[192,640]{1,0:T(8,128)(2,1)S(1)}, bf16[192,640]{1,0:T(8,128)(2,1)S(1)}, u32[]{:S(2)}, u32[]{:S(2)}) collective-permute-start(bf16[192,640]{1,0:T(8,128)(2,1)S(1)} %pad.4.refs_0_), channel_id=1, source_target_pairs={{0,8},{1,9},{2,10},{3,11},{4,12},{5,13},{6,14},{7,15},{8,0},{9,1},... | collective-permute-start | bytes 737288 | tf_op jit(solution)/shard_map/ppermute | solution.py:241
  13.6 8.9 %collective-permute-start.6 = (bf16[768,128]{1,0:T(8,128)(2,1)S(1)}, bf16[768,128]{1,0:T(8,128)(2,1)S(1)}, u32[]{:S(2)}, u32[]{:S(2)}) collective-permute-start(bf16[768,128]{1,0:T(8,128)(2,1)S(1)} %pad_maximum_fusion.2.keys_ref.refs_3_), channel_id=1, source_target_pairs={{0,2},{1,3},{2,0},{3,1},{4,6},{5,7},{6,4},{7,5},{8,10},{9,11},{10,... | collective-permute-start | bytes 589832 | tf_op jit(solution)/shard_map/ppermute | solution.py:241
  15.4 10.6 %collective-permute-start.5 = (bf16[192,640]{1,0:T(8,128)(2,1)S(1)}, bf16[192,640]{1,0:T(8,128)(2,1)S(1)}, u32[]{:S(2)}, u32[]{:S(2)}) collective-permute-start(bf16[192,640]{1,0:T(8,128)(2,1)S(1)} %pad.4.refs_0_), channel_id=1, source_target_pairs={{0,4},{1,5},{2,6},{3,7},{4,0},{5,1},{6,2},{7,3},{8,12},{9,13},{10,... | collective-permute-start | bytes 737288 | tf_op jit(solution)/shard_map/ppermute | solution.py:241
  16.4 11.3 %collective-permute-start.2 = (bf16[192,640]{1,0:T(8,128)(2,1)S(1)}, bf16[192,640]{1,0:T(8,128)(2,1)S(1)}, u32[]{:S(2)}, u32[]{:S(2)}) collective-permute-start(bf16[192,640]{1,0:T(8,128)(2,1)S(1)} %pad.4.refs_0_), channel_id=1, source_target_pairs={{0,2},{1,3},{2,0},{3,1},{4,6},{5,7},{6,4},{7,5},{8,10},{9,11},{10,... | collective-permute-start | bytes 737288 | tf_op jit(solution)/shard_map/ppermute | solution.py:241
  16.9 1.6 %copy-start = (bf16[128,8192]{1,0:T(8,128)(2,1)S(1)}, bf16[128,8192]{1,0:T(8,128)(2,1)}, u32[]{:S(2)}) copy-start(bf16[128,8192]{1,0:T(8,128)(2,1)} %refs_1_.1) | copy-start | bytes 6291460
  18.5 0.8 %copy-start.2 = (f32[128,64]{0,1:T(8,128)S(1)}, f32[128,64]{0,1:T(8,128)}, u32[]{:S(2)}) copy-start(f32[128,64]{0,1:T(8,128)} %param.12) | copy-start | bytes 98308
  22.5 5.7 %collective-permute-start.10 = (bf16[1536,128]{1,0:T(8,128)(2,1)S(1)}, bf16[1536,128]{1,0:T(8,128)(2,1)S(1)}, u32[]{:S(2)}, u32[]{:S(2)}) collective-permute-start(bf16[1536,128]{1,0:T(8,128)(2,1)S(1)} %pad_maximum_fusion), channel_id=1, source_target_pairs={{0,1},{1,0},{2,3},{3,2},{4,5},{5,4},{6,7},{7,6},{8,9},{9,8},{10,11... | collective-permute-start | bytes 1179656 | tf_op jit(solution)/shard_map/ppermute | solution.py:241
  25.1 16.0 %copy-start.1 = (bf16[128,8192]{1,0:T(8,128)(2,1)S(1)}, bf16[128,8192]{1,0:T(8,128)(2,1)}, u32[]{:S(2)}) copy-start(bf16[128,8192]{1,0:T(8,128)(2,1)} %refs_1_.1) | copy-start | bytes 6291460
  25.1 8.4 %collective-permute-start.12 = (bf16[192,640]{1,0:T(8,128)(2,1)S(1)}, bf16[192,640]{1,0:T(8,128)(2,1)S(1)}, u32[]{:S(2)}, u32[]{:S(2)}) collective-permute-start(bf16[192,640]{1,0:T(8,128)(2,1)S(1)} %collective-permute-done.7.refs_8_), channel_id=1, source_target_pairs={{0,4},{1,5},{2,6},{3,7},{4,0},{5,1},{6,2},{7,3},{8,12},{9,13},{10,... | collective-permute-start | bytes 737288 | tf_op jit(solution)/shard_map/ppermute | solution.py:241
  26.0 8.8 %collective-permute-start.9 = (bf16[192,640]{1,0:T(8,128)(2,1)S(1)}, bf16[192,640]{1,0:T(8,128)(2,1)S(1)}, u32[]{:S(2)}, u32[]{:S(2)}) collective-permute-start(bf16[192,640]{1,0:T(8,128)(2,1)S(1)} %collective-permute-done.5.refs_4_), channel_id=1, source_target_pairs={{0,2},{1,3},{2,0},{3,1},{4,6},{5,7},{6,4},{7,5},{8,10},{9,11},{10,... | collective-permute-start | bytes 737288 | tf_op jit(solution)/shard_map/ppermute | solution.py:241
  27.7 19.6 %collective-permute-start.8 = (bf16[192,640]{1,0:T(8,128)(2,1)S(1)}, bf16[192,640]{1,0:T(8,128)(2,1)S(1)}, u32[]{:S(2)}, u32[]{:S(2)}) collective-permute-start(bf16[192,640]{1,0:T(8,128)(2,1)S(1)} %collective-permute-done.5.refs_4_), channel_id=1, source_target_pairs={{0,1},{1,0},{2,3},{3,2},{4,5},{5,4},{6,7},{7,6},{8,9},{9,8},{10,11... | collective-permute-start | bytes 737288 | tf_op jit(solution)/shard_map/ppermute | solution.py:241
  27.7 20.1 %collective-permute-start.14 = (bf16[192,640]{1,0:T(8,128)(2,1)S(1)}, bf16[192,640]{1,0:T(8,128)(2,1)S(1)}, u32[]{:S(2)}, u32[]{:S(2)}) collective-permute-start(bf16[192,640]{1,0:T(8,128)(2,1)S(1)} %collective-permute-done.7.refs_8_), channel_id=1, source_target_pairs={{0,1},{1,0},{2,3},{3,2},{4,5},{5,4},{6,7},{7,6},{8,9},{9,8},{10,11... | collective-permute-start | bytes 737288 | tf_op jit(solution)/shard_map/ppermute | solution.py:241
  28.2 11.1 %collective-permute-start.11 = (bf16[192,640]{1,0:T(8,128)(2,1)S(1)}, bf16[192,640]{1,0:T(8,128)(2,1)S(1)}, u32[]{:S(2)}, u32[]{:S(2)}) collective-permute-start(bf16[192,640]{1,0:T(8,128)(2,1)S(1)} %collective-permute-done.7.refs_8_), channel_id=1, source_target_pairs={{0,2},{1,3},{2,0},{3,1},{4,6},{5,7},{6,4},{7,5},{8,10},{9,11},{10,... | collective-permute-start | bytes 737288 | tf_op jit(solution)/shard_map/ppermute | solution.py:241
  33.6 14.3 %collective-permute-start.3 = (bf16[192,640]{1,0:T(8,128)(2,1)S(1)}, bf16[192,640]{1,0:T(8,128)(2,1)S(1)}, u32[]{:S(2)}, u32[]{:S(2)}) collective-permute-start(bf16[192,640]{1,0:T(8,128)(2,1)S(1)} %pad.4.refs_0_), channel_id=1, source_target_pairs={{0,1},{1,0},{2,3},{3,2},{4,5},{5,4},{6,7},{7,6},{8,9},{9,8},{10,11... | collective-permute-start | bytes 737288 | tf_op jit(solution)/shard_map/ppermute | solution.py:241
  34.8 13.6 %collective-permute-start.4 = (bf16[192,640]{1,0:T(8,128)(2,1)S(1)}, bf16[192,640]{1,0:T(8,128)(2,1)S(1)}, u32[]{:S(2)}, u32[]{:S(2)}) collective-permute-start(bf16[192,640]{1,0:T(8,128)(2,1)S(1)} %collective-permute-done.2.refs_2_), channel_id=1, source_target_pairs={{0,1},{1,0},{2,3},{3,2},{4,5},{5,4},{6,7},{7,6},{8,9},{9,8},{10,11... | collective-permute-start | bytes 737288 | tf_op jit(solution)/shard_map/ppermute | solution.py:241
  39.4 8.0 %collective-permute-start.17 = (bf16[192,640]{1,0:T(8,128)(2,1)S(1)}, bf16[192,640]{1,0:T(8,128)(2,1)S(1)}, u32[]{:S(2)}, u32[]{:S(2)}) collective-permute-start(bf16[192,640]{1,0:T(8,128)(2,1)S(1)} %collective-permute-done.12.refs_12_), channel_id=1, source_target_pairs={{0,2},{1,3},{2,0},{3,1},{4,6},{5,7},{6,4},{7,5},{8,10},{9,11},{10,... | collective-permute-start | bytes 737288 | tf_op jit(solution)/shard_map/ppermute | solution.py:241
  41.1 8.8 %copy-start.3 = (s32[2,12]{1,0:T(2,128)S(1)}, s32[2,12]{1,0:T(2,128)}, u32[]{:S(2)}) copy-start(s32[2,12]{1,0:T(2,128)} %pick_ref.1) | copy-start | bytes 292
  47.3 2.2 %collective-permute-start.16 = (bf16[192,640]{1,0:T(8,128)(2,1)S(1)}, bf16[192,640]{1,0:T(8,128)(2,1)S(1)}, u32[]{:S(2)}, u32[]{:S(2)}) collective-permute-start(bf16[192,640]{1,0:T(8,128)(2,1)S(1)} %collective-permute-done.12.refs_12_), channel_id=1, source_target_pairs={{0,1},{1,0},{2,3},{3,2},{4,5},{5,4},{6,7},{7,6},{8,9},{9,8},{10,11... | collective-permute-start | bytes 737288 | tf_op jit(solution)/shard_map/ppermute | solution.py:241
  47.3 1.9 %collective-permute-start.13 = (bf16[192,640]{1,0:T(8,128)(2,1)S(1)}, bf16[192,640]{1,0:T(8,128)(2,1)S(1)}, u32[]{:S(2)}, u32[]{:S(2)}) collective-permute-start(bf16[192,640]{1,0:T(8,128)(2,1)S(1)} %collective-permute-done.9.refs_6_), channel_id=1, source_target_pairs={{0,1},{1,0},{2,3},{3,2},{4,5},{5,4},{6,7},{7,6},{8,9},{9,8},{10,11... | collective-permute-start | bytes 737288 | tf_op jit(solution)/shard_map/ppermute | solution.py:241
  47.9 1.7 %collective-permute-start.15 = (bf16[192,640]{1,0:T(8,128)(2,1)S(1)}, bf16[192,640]{1,0:T(8,128)(2,1)S(1)}, u32[]{:S(2)}, u32[]{:S(2)}) collective-permute-start(bf16[192,640]{1,0:T(8,128)(2,1)S(1)} %collective-permute-done.11.refs_10_), channel_id=1, source_target_pairs={{0,1},{1,0},{2,3},{3,2},{4,5},{5,4},{6,7},{7,6},{8,9},{9,8},{10,11... | collective-permute-start | bytes 737288 | tf_op jit(solution)/shard_map/ppermute | solution.py:241
  47.9 2.0 %collective-permute-start.18 = (bf16[192,640]{1,0:T(8,128)(2,1)S(1)}, bf16[192,640]{1,0:T(8,128)(2,1)S(1)}, u32[]{:S(2)}, u32[]{:S(2)}) collective-permute-start(bf16[192,640]{1,0:T(8,128)(2,1)S(1)} %collective-permute-done.17.refs_14_), channel_id=1, source_target_pairs={{0,1},{1,0},{2,3},{3,2},{4,5},{5,4},{6,7},{7,6},{8,9},{9,8},{10,11... | collective-permute-start | bytes 737288 | tf_op jit(solution)/shard_map/ppermute | solution.py:241

commit v5 on v4

--- a/solution.py
+++ b/solution.py
@@ -24,6 +24,7 @@
 LOW = -1.0e30
 EXP2_SCALE = 192.0**-0.5 * 1.4426950408889634
 VMEM = 48 * 2**20
+INDEX_VMEM = 60 * 2**20
 
 
 def index_tile(iq_ref, weights, keys, pieces=None):
@@ -64,9 +65,8 @@
     )
 
 
-def index_line_kernel(shards, iq_hbm, w_hbm, keys_ref, out_ref, iq_ref, w_ref, sem):
+def index_tiles(iq_hbm, w_hbm, iq_ref, w_ref, sem, steps, load, store, aside=None):
     tok = iq_ref.shape[0]
-    each = TILE // tok
     w_copy = pltpu.make_async_copy(w_hbm, w_ref, sem.at[tok // TOK_TILE])
     w_copy.start()
     pieces = []
@@ -74,60 +74,83 @@
         part = pl.ds(n * TOK_TILE, TOK_TILE)
         pieces.append(pltpu.make_async_copy(iq_hbm.at[part], iq_ref.at[part], sem.at[n]))
         pieces[-1].start()
+    if aside is not None:
+        aside()
     w_copy.wait()
     weights = w_ref[...].T * IDX**-0.5
-    value = index_tile(iq_ref, weights, window_keys(keys_ref, tok, each, 0), pieces)
-    for n in range(each):
-        out_ref[n] = value[:, n * tok : (n + 1) * tok]
-
-    if shards > each:
-
-        @pl.loop(1, shards // each)
+    store(0, index_tile(iq_ref, weights, load(0), pieces))
+    if steps > 1:
+
+        @pl.loop(1, steps)
         def _(step):
-            value = index_tile(iq_ref, weights, window_keys(keys_ref, tok, each, step))
-            for n in range(each):
-                out_ref[step * each + n] = value[:, n * tok : (n + 1) * tok]
-
-
-def index_window_kernel(shards, iq_ref, w_ref, keys_ref, out_ref):
+            store(step, index_tile(iq_ref, weights, load(step)))
+
+
+def index_window_kernel(shards, iq_hbm, w_hbm, keys_ref, out_ref, iq_ref, w_ref, sem):
     tok = iq_ref.shape[0]
     each = TILE // tok
-    weights = w_ref[...].T * IDX**-0.5
-
-    @pl.loop(0, shards // each)
-    def _(step):
-        value = index_tile(iq_ref, weights, window_keys(keys_ref, tok, each, step))
+
+    def store(step, value):
         for n in range(each):
             out_ref[step * each + n] = value[:, n * tok : (n + 1) * tok]
 
-
-def index_prefix_kernel(places, *refs):
-    count = len(places)
-    own_ref, iq_ref, w_ref = refs[:3]
-    key_refs, done_refs = refs[3 : 3 + count], refs[3 + count : 3 + 2 * count]
-    prefix_ref, window_ref, keys_ref = refs[3 + 2 * count :]
-    own = own_ref[0]
-    tok = iq_ref.shape[0]
-    span = BLK + tok
-    weights = w_ref[...].T * IDX**-0.5
+    def load(step):
+        return window_keys(keys_ref, tok, each, step)
+
+    index_tiles(iq_hbm, w_hbm, iq_ref, w_ref, sem, shards // each, load, store)
+
+
+def order_prefix(places, own, tok, key_refs, keys_ref):
     for ref, rels in zip(key_refs, places):
         for n, rel in enumerate(rels):
             at = pl.multiple_of((own ^ rel) * BLK, BLK)
+            span = BLK + tok
             keys_ref[pl.ds(at, BLK), :] = ref[n * span : n * span + BLK, :]
-    row = lax.broadcasted_iota(jnp.int32, (tok, LANES), 0)
-    lane = lax.broadcasted_iota(jnp.int32, (tok, LANES), 1)
-    for ref, rels in zip(done_refs, places):
-        for n, rel in enumerate(rels):
-            other = own ^ rel
-            seen = other * tok + lane <= own * tok + row
-            window_ref[:, pl.ds(pl.multiple_of(other * tok, LANES), LANES)] = jnp.where(
-                seen, ref[n], 0.0
-            )
-
-    @pl.loop(0, keys_ref.shape[0] // TILE)
-    def _(step):
-        at = pl.multiple_of(step * TILE, TILE)
-        prefix_ref[:, pl.ds(at, TILE)] = index_tile(iq_ref, weights, keys_ref[pl.ds(at, TILE), :])
+
+
+def index_prefix_kernel(places, first, steps, own_ref, iq_hbm, w_hbm, *refs):
+    count = len(places)
+    out_ref, iq_ref, w_ref, sem, keys_ref = refs[count:]
+
+    def aside():
+        order_prefix(places, own_ref[0], iq_ref.shape[0], refs[:count], keys_ref)
+
+    def load(step):
+        return keys_ref[pl.ds(pl.multiple_of((first + step) * TILE, TILE), TILE), :]
+
+    def store(step, value):
+        out_ref[:, pl.ds(pl.multiple_of(step * TILE, TILE), TILE)] = value
+
+    index_tiles(iq_hbm, w_hbm, iq_ref, w_ref, sem, steps, load, store, aside)
+
+
+def index_last_kernel(places, first, steps, own_ref, iq_hbm, w_hbm, *refs):
+    count = len(places)
+    key_refs, done_refs = refs[:count], refs[count : 2 * count]
+    begun_ref, prefix_ref, window_ref, iq_ref, w_ref, sem, keys_ref = refs[2 * count :]
+
+    def aside():
+        own = own_ref[0]
+        tok = iq_ref.shape[0]
+        order_prefix(places, own, tok, key_refs, keys_ref)
+        prefix_ref[:, : first * TILE] = begun_ref[...]
+        row = lax.broadcasted_iota(jnp.int32, (tok, LANES), 0)
+        lane = lax.broadcasted_iota(jnp.int32, (tok, LANES), 1)
+        for ref, rels in zip(done_refs, places):
+            for n, rel in enumerate(rels):
+                other = own ^ rel
+                seen = other * tok + lane <= own * tok + row
+                window_ref[:, pl.ds(pl.multiple_of(other * tok, LANES), LANES)] = jnp.where(
+                    seen, ref[n], 0.0
+                )
+
+    def load(step):
+        return keys_ref[pl.ds(pl.multiple_of((first + step) * TILE, TILE), TILE), :]
+
+    def store(step, value):
+        prefix_ref[:, pl.ds(pl.multiple_of((first + step) * TILE, TILE), TILE)] = value
+
+    index_tiles(iq_hbm, w_hbm, iq_ref, w_ref, sem, steps, load, store, aside)
 
 
 def attention_kernel(devices, own_ref, pick_ref, q_ref, *refs):
@@ -252,30 +275,23 @@
 
     weights = index_weights.T
 
-    def index_line(shard_keys):
-        count = shard_keys.shape[0] // span
-        return pl.pallas_call(
-            functools.partial(index_line_kernel, count),
-            out_shape=jax.ShapeDtypeStruct((count, tok, LANES), jnp.float32),
-            in_specs=[hbm, hbm, vmem],
-            out_specs=vmem,
-            scratch_shapes=[
-                pltpu.VMEM((tok, IH * IDX), jnp.bfloat16),
-                pltpu.VMEM((IH, tok), jnp.float32),
-                pltpu.SemaphoreType.DMA((tok // TOK_TILE + 1,)),
-            ],
-            compiler_params=params,
-            cost_estimate=index_cost(count * tok),
-        )(index_queries, weights, shard_keys)
+    index_scratch = [
+        pltpu.VMEM((tok, IH * IDX), jnp.bfloat16),
+        pltpu.VMEM((IH, tok), jnp.float32),
+        pltpu.SemaphoreType.DMA((tok // TOK_TILE + 1,)),
+    ]
+    order_scratch = [pltpu.VMEM((devices * BLK, IDX), jnp.bfloat16)]
+    index_params = pltpu.CompilerParams(vmem_limit_bytes=INDEX_VMEM)
 
     def index_window(shard_keys):
         count = shard_keys.shape[0] // span
         return pl.pallas_call(
             functools.partial(index_window_kernel, count),
             out_shape=jax.ShapeDtypeStruct((count, tok, LANES), jnp.float32),
-            in_specs=[vmem, vmem, vmem],
+            in_specs=[hbm, hbm, vmem],
             out_specs=vmem,
-            compiler_params=params,
+            scratch_shapes=index_scratch,
+            compiler_params=index_params,
             cost_estimate=index_cost(count * tok),
         )(index_queries, weights, shard_keys)
 
@@ -315,9 +331,15 @@
         for rel, bit in moves:
             shards[rel ^ bit] = swap(held[rel], bit)
 
-    line_done = index_line(key_line)
-    send(line_done, (0, 1), (2, 1))
+    line_done = index_window(key_line)
+    send(line_done, (0, 1))
+    def settle(array, done, rels):
+        got = lax.optimization_barrier((array, done, *[shards[rel] for rel in rels]))
+        shards.update(zip(rels, got[2:]))
+        return got[0]
+
     side_done = index_window(key_side)
+    side_done = settle(side_done, weights, [1, 2])
     send(side_done, (low, 2), (low, 1), *[(bit, 2) for bit in high], *[(bit, 1) for bit in high])
     rest = []
     for n, bit in enumerate(high):
@@ -327,28 +349,35 @@
                 shards[rel ^ other] = swap(held, other)
                 rest.append(rel ^ other)
     far_done = index_window(key_far)
-    send(
-        far_done,
-        (low | 2, 1),
-        *[(bit | 2, 1) for bit in high],
-        *[(rel, 2) for rel in rest],
-        *[(rel, 1) for rel in rest],
-    )
-
+    send(far_done, *[(rel, 2) for rel in rest], *[(rel, 1) for rel in rest], (2, 1))
+    held = settle(index_queries, far_done, [rel ^ 1 for rel in bits] + rest)
+    places = [line, side, far]
+    tiles = devices * BLK // TILE
+    begun = pl.pallas_call(
+        functools.partial(index_prefix_kernel, places, 0, tiles // 2),
+        out_shape=jax.ShapeDtypeStruct((tok, tiles // 2 * TILE), jnp.float32),
+        in_specs=[smem, hbm, hbm, vmem, vmem, vmem],
+        out_specs=vmem,
+        scratch_shapes=index_scratch + order_scratch,
+        compiler_params=index_params,
+        cost_estimate=index_cost(tiles // 2 * TILE),
+    )(own, held, weights, key_line, key_side, key_far)
+    send(begun, (low | 2, 1), *[(bit | 2, 1) for bit in high])
+    held = settle(index_queries, begun, [rel ^ 1 for rel in rest] + [3] + [rel | 2 for rel in bits])
     prefix_index, window_index = pl.pallas_call(
-        functools.partial(index_prefix_kernel, [line, side, far]),
+        functools.partial(index_last_kernel, places, tiles // 2, tiles - tiles // 2),
         out_shape=(
             jax.ShapeDtypeStruct((tok, devices * BLK), jnp.float32),
             jax.ShapeDtypeStruct((tok, devices * tok), jnp.float32),
         ),
-        in_specs=[smem] + [vmem] * 8,
+        in_specs=[smem, hbm, hbm] + [vmem] * 7,
         out_specs=(vmem, vmem),
-        scratch_shapes=[pltpu.VMEM((devices * BLK, IDX), jnp.bfloat16)],
-        compiler_params=params,
-        cost_estimate=index_cost(devices * BLK),
+        scratch_shapes=index_scratch + order_scratch,
+        compiler_params=index_params,
+        cost_estimate=index_cost(tiles // 2 * TILE),
     )(
         own,
-        index_queries,
+        held,
         weights,
         key_line,
         key_side,
@@ -356,6 +385,7 @@
         line_done,
         side_done,
         far_done,
+        begun,
     )
     send(prefix_index, *[(rel | 2, 1) for rel in rest])
     shards = [shards[rel] for rel in range(devices)]

time: 75.3 us -> 82.6 us (1.097)
  Pallas kernels: 41.9 us -> 56.5 us
  waiting for transfers between devices: 9.33 us -> 3.54 us
  local copies, waits for them, and re-layouts: 2.68 us -> 0.42 us
    pallas_call x2 -> x3, Pallas kernels: 7.5 us -> 19.5 us  [index_window(): pl.pallas_call(functools.partial(index_window_kernel, count), out_shape=j...]
    ppermute x19, waiting for transfers between devices: 9.33 us -> 3.54 us  [swap(): return lax.ppermute(array, 'ctx', [(i, i ^ rel) for i in range(devices)])]
    pallas_call x2, Pallas kernels: 9.45 us -> 12.3 us  [the longest x1 6.37 us: body(): pl.pallas_call(functools.partial(index_last_kernel, places, tiles // 2, t...]
    unnamed x8, local copies, waits for them, and re-layouts: 2.36 us -> 0.09 us
  transfers between devices with their start and end apart: 19 -> 19, of which waited for: 7 -> 3; matrix products, arithmetic and copies ran while one was open for 2% -> 2% of each run, Pallas kernels for 23% -> 39%
where the time goes in v5:
time: 82.6 us; the launch traced here: 82.1 us
  Pallas kernels  56.5 us (68%)
  starting transfers between devices  18.5 us (22%)
  waiting for transfers between devices  3.54 us (4%)
  other arithmetic  2.1 us (3%)
  between operations  0.99 us (1%)
    pallas_call x1, Pallas kernels, body(): pl.pallas_call(functools.partial(attention_kernel, devices), grid_spec=pl...  24.7 us
    pallas_call x3, Pallas kernels, index_window(): pl.pallas_call(functools.partial(index_window_kernel, count), out_shape=j...  19.5 us
    ppermute x19, starting transfers between devices, swap(): return lax.ppermute(array, 'ctx', [(i, i ^ rel) for i in range(devices)])  18.5 us
    pallas_call x1, Pallas kernels, body(): pl.pallas_call(functools.partial(index_last_kernel, places, tiles // 2, t...  6.37 us
    pallas_call x1, Pallas kernels, body(): pl.pallas_call(functools.partial(index_prefix_kernel, places, 0, tiles //...  5.95 us
    ppermute x19, waiting for transfers between devices, swap(): return lax.ppermute(array, 'ctx', [(i, i ^ rel) for i in range(devices)])  3.54 us
  transfers between devices with their start and end apart: 19, of which 3 were waited for; matrix products, arithmetic and copies ran while one was open for 2% of the time, Pallas kernels for 39%

profile of v5, /device:TPU:0, one launch (start us, length us, event | category | flops | bytes accessed | tf_op | source)
XLA Modules:
  0.0 82.1 jit_solution(6366810346938670194)
XLA Ops:
  0.6 0.8 pad_maximum_fusion.4
  1.4 4.0 %collective-permute-start = (bf16[192,128]{1,0:T(8,128)(2,1)S(1)}, bf16[192,128]{1,0:T(8,128)(2,1)S(1)}, u32[]{:S(2)}, u32[]{:S(2)}) collective-permute-start(bf16[192,128]{1,0:T(8,128)(2,1)S(1)} %pad_maximum_fusion.4), channel_id=1, source_target_pairs={{0,8},{1,9},{2,10},{3,11},{4,12},{5,13},{6,14},{7,15},{8,0},{9,1},... | collective-permute-start | bytes 147464 | tf_op jit(solution)/shard_map/ppermute | solution.py:264
  5.4 1.3 %pad_maximum_fusion.1 = bf16[3,36864]{1,0:T(4,128)(2,1)S(1)} fusion(bf16[2,36864]{1,0:T(2,128)(2,1)} %param.10, bf16[1,36864]{1,0:T(2,128)(2,1)} %param.9), kind=kLoop, calls=%fused_computation.1 | loop fusion | flops 442368 | bytes 442368 | tf_op jit(solution)/shard_map/concatenate | solution.py:308
  6.7 0.3 reshape.13
  7.1 1.0 %collective-permute-done = bf16[192,128]{1,0:T(8,128)(2,1)S(1)} collective-permute-done((bf16[192,128]{1,0:T(8,128)(2,1)S(1)}, bf16[192,128]{1,0:T(8,128)(2,1)S(1)}, u32[]{:S(2)}, u32[]{:S(2)}) %collective-permute-start) | collective-permute-done | bytes 49184 | tf_op jit(solution)/shard_map/ppermute | solution.py:264
  8.0 1.4 %collective-permute-start.1 = (bf16[384,128]{1,0:T(8,128)(2,1)S(1)}, bf16[384,128]{1,0:T(8,128)(2,1)S(1)}, u32[]{:S(2)}, u32[]{:S(2)}) collective-permute-start(bf16[384,128]{1,0:T(8,128)(2,1)S(1)} %pad_maximum_fusion.3), channel_id=1, source_target_pairs={{0,4},{1,5},{2,6},{3,7},{4,0},{5,1},{6,2},{7,3},{8,12},{9,13},{10,... | collective-permute-start | bytes 294920 | tf_op jit(solution)/shard_map/ppermute | solution.py:264
  9.5 3.0 %collective-permute-start.7 = (bf16[192,640]{1,0:T(8,128)(2,1)S(1)}, bf16[192,640]{1,0:T(8,128)(2,1)S(1)}, u32[]{:S(2)}, u32[]{:S(2)}) collective-permute-start(bf16[192,640]{1,0:T(8,128)(2,1)S(1)} %pad.4.refs_0_), channel_id=1, source_target_pairs={{0,8},{1,9},{2,10},{3,11},{4,12},{5,13},{6,14},{7,15},{8,0},{9,1},... | collective-permute-start | bytes 737288 | tf_op jit(solution)/shard_map/ppermute | solution.py:264
  12.5 1.1 %collective-permute-done.1 = bf16[384,128]{1,0:T(8,128)(2,1)S(1)} collective-permute-done((bf16[384,128]{1,0:T(8,128)(2,1)S(1)}, bf16[384,128]{1,0:T(8,128)(2,1)S(1)}, u32[]{:S(2)}, u32[]{:S(2)}) %collective-permute-start.1) | collective-permute-done | bytes 98336 | tf_op jit(solution)/shard_map/ppermute | solution.py:264
  13.6 1.8 %collective-permute-start.2 = (bf16[768,128]{1,0:T(8,128)(2,1)S(1)}, bf16[768,128]{1,0:T(8,128)(2,1)S(1)}, u32[]{:S(2)}, u32[]{:S(2)}) collective-permute-start(bf16[768,128]{1,0:T(8,128)(2,1)S(1)} %pad_maximum_fusion.2.keys_ref.refs_0_), channel_id=1, source_target_pairs={{0,2},{1,3},{2,0},{3,1},{4,6},{5,7},{6,4},{7,5},{8,10},{9,11},{10,... | collective-permute-start | bytes 589832 | tf_op jit(solution)/shard_map/ppermute | solution.py:264
  15.4 1.0 %collective-permute-start.6 = (bf16[192,640]{1,0:T(8,128)(2,1)S(1)}, bf16[192,640]{1,0:T(8,128)(2,1)S(1)}, u32[]{:S(2)}, u32[]{:S(2)}) collective-permute-start(bf16[192,640]{1,0:T(8,128)(2,1)S(1)} %pad.4.refs_0_), channel_id=1, source_target_pairs={{0,4},{1,5},{2,6},{3,7},{4,0},{5,1},{6,2},{7,3},{8,12},{9,13},{10,... | collective-permute-start | bytes 737288 | tf_op jit(solution)/shard_map/ppermute | solution.py:264
  16.4 0.5 collective-permute-start.4
  16.9 5.7 %shard_map.104.refs_3_ = f32[4,128,128]{2,1,0:T(8,128)} custom-call(bf16[128,8192]{1,0:T(8,128)(2,1)} %iq_hbm.7, f32[64,128]{1,0:T(8,128)} %bitcast.2, bf16[768,128]{1,0:T(8,128)(2,1)} %copy-done.1), custom_call_target="tpu_custom_call" | custom-call | flops 4294967296 | bytes 4194304 | tf_op jit(solution)/shard_map/pallas_call | solution.py:288
  22.6 0.1 collective-permute-start.3
  22.7 0.5 collective-permute-start.5
  23.3 0.1 copy-done.2
  23.3 5.7 %shard_map.103.refs_4_ = f32[4,128,128]{2,1,0:T(8,128)} custom-call(bf16[128,8192]{1,0:T(8,128)(2,1)} %iq_hbm.7, f32[64,128]{1,0:T(8,128)} %bitcast.3, bf16[768,128]{1,0:T(8,128)(2,1)} %copy-done.2), custom_call_target="tpu_custom_call" | custom-call | flops 4294967296 | bytes 4194304 | tf_op jit(solution)/shard_map/pallas_call | solution.py:288
  29.1 1.5 %collective-permute-start.13 = (bf16[192,640]{1,0:T(8,128)(2,1)S(1)}, bf16[192,640]{1,0:T(8,128)(2,1)S(1)}, u32[]{:S(2)}, u32[]{:S(2)}) collective-permute-start(bf16[192,640]{1,0:T(8,128)(2,1)S(1)} %collective-permute-done.7.refs_8_), channel_id=1, source_target_pairs={{0,2},{1,3},{2,0},{3,1},{4,6},{5,7},{6,4},{7,5},{8,10},{9,11},{10,... | collective-permute-start | bytes 737288 | tf_op jit(solution)/shard_map/ppermute | solution.py:264
  30.6 0.2 collective-permute-start.8
  30.8 0.5 collective-permute-start.14
  31.3 0.0 collective-permute-start.9
  31.4 0.9 %collective-permute-start.10 = (bf16[192,640]{1,0:T(8,128)(2,1)S(1)}, bf16[192,640]{1,0:T(8,128)(2,1)S(1)}, u32[]{:S(2)}, u32[]{:S(2)}) collective-permute-start(bf16[192,640]{1,0:T(8,128)(2,1)S(1)} %collective-permute-done.7.refs_8_), channel_id=1, source_target_pairs={{0,4},{1,5},{2,6},{3,7},{4,0},{5,1},{6,2},{7,3},{8,12},{9,13},{10,... | collective-permute-start | bytes 737288 | tf_op jit(solution)/shard_map/ppermute | solution.py:264
  32.2 8.2 %shard_map.105.refs_5_ = f32[8,128,128]{2,1,0:T(8,128)} custom-call(bf16[128,8192]{1,0:T(8,128)(2,1)} %iq_hbm.7, f32[64,128]{1,0:T(8,128)} %bitcast.4, bf16[1536,128]{1,0:T(8,128)(2,1)} %copy-done.3), custom_call_target="tpu_custom_call" | custom-call | flops 8589934592 | bytes 4194304 | tf_op jit(solution)/shard_map/pallas_call | solution.py:288
  40.4 1.7 %collective-permute-start.17 = (bf16[192,640]{1,0:T(8,128)(2,1)S(1)}, bf16[192,640]{1,0:T(8,128)(2,1)S(1)}, u32[]{:S(2)}, u32[]{:S(2)}) collective-permute-start(bf16[192,640]{1,0:T(8,128)(2,1)S(1)} %collective-permute-done.10.refs_12_), channel_id=1, source_target_pairs={{0,2},{1,3},{2,0},{3,1},{4,6},{5,7},{6,4},{7,5},{8,10},{9,11},{10,... | collective-permute-start | bytes 737288 | tf_op jit(solution)/shard_map/ppermute | solution.py:264
  42.2 0.5 collective-permute-start.12
  42.7 5.9 %shard_map.106.refs_6_ = f32[128,512]{1,0:T(8,128)} custom-call(s32[1]{0:T(128)} %bitcast.own_ref, bf16[128,8192]{1,0:T(8,128)(2,1)} %iq_hbm.7, f32[64,128]{1,0:T(8,128)} %bitcast.5, bf16[768,128]{1,0:T(8,128)(2,1)} %copy-done.1, bf16[768,128]{1,0:T(8,128)(2,1)} %copy-done.2, bf16[1536,128]{1,0:T(8,128)(2,1)} %copy-done.3), custom_call_target="tpu_custom_call" | custom-call | flops 4294967296 | bytes 4194304 | tf_op jit(solution)/shard_map/pallas_call | solution.py:356
  48.6 0.0 copy-start
  48.7 0.1 collective-permute-start.15
  48.8 0.5 collective-permute-start.16
  49.2 6.4 %shard_map.107 = (f32[128,1024]{1,0:T(8,128)}, f32[128,2048]{1,0:T(8,128)}) custom-call(s32[1]{0:T(128)} %bitcast.own_ref, bf16[128,8192]{1,0:T(8,128)(2,1)} %iq_hbm.7, f32[64,128]{1,0:T(8,128)} %bitcast.6, bf16[768,128]{1,0:T(8,128)(2,1)} %copy-done.1, bf16[768,128]{1,0:T(8,128)(2,1)} %copy-done.2, bf16[1536,128]{1,0:T(8,128)(2,1)} %copy-done.3, ...), custom_call_target="tpu_custom_call" | custom-call | flops 4294967296 | bytes 4194304 | tf_op jit(solution)/shard_map/pallas_call | solution.py:367
  55.6 0.1 collective-permute-start.18
  55.8 1.4 %collective-permute-done.18.refs_15_ = bf16[192,640]{1,0:T(8,128)(2,1)S(1)} collective-permute-done((bf16[192,640]{1,0:T(8,128)(2,1)S(1)}, bf16[192,640]{1,0:T(8,128)(2,1)S(1)}, u32[]{:S(2)}, u32[]{:S(2)}) %collective-permute-start.18) | collective-permute-done | bytes 245792 | tf_op jit(solution)/shard_map/ppermute | solution.py:264
  57.2 24.7 %shard_map.108 = bf16[128,32768]{1,0:T(8,128)(2,1)} custom-call(s32[1]{0:T(128)} %bitcast.own_ref, s32[2,12]{1,0:T(2,128)S(1)} %copy-done, bf16[128,36864]{1,0:T(8,128)(2,1)} %q_ref.1, bf16[192,640]{1,0:T(8,128)(2,1)S(1)} %pad.4.refs_0_, bf16[192,640]{1,0:T(8,128)(2,1)S(1)} %collective-permute-done.3.refs_1_, ...), custom_call_target="tpu_custom_call" | custom-call | flops 14495514624 | bytes 16777216 | tf_op jit(solution)/shard_map/pallas_call | solution.py:394
  (27 shorter events, 0.1 us)
Async XLA Ops:
  1.4 6.6 %collective-permute-start = (bf16[192,128]{1,0:T(8,128)(2,1)S(1)}, bf16[192,128]{1,0:T(8,128)(2,1)S(1)}, u32[]{:S(2)}, u32[]{:S(2)}) collective-permute-start(bf16[192,128]{1,0:T(8,128)(2,1)S(1)} %pad_maximum_fusion.4), channel_id=1, source_target_pairs={{0,8},{1,9},{2,10},{3,11},{4,12},{5,13},{6,14},{7,15},{8,0},{9,1},... | collective-permute-start | bytes 147464 | tf_op jit(solution)/shard_map/ppermute | solution.py:264
  8.0 5.6 %collective-permute-start.1 = (bf16[384,128]{1,0:T(8,128)(2,1)S(1)}, bf16[384,128]{1,0:T(8,128)(2,1)S(1)}, u32[]{:S(2)}, u32[]{:S(2)}) collective-permute-start(bf16[384,128]{1,0:T(8,128)(2,1)S(1)} %pad_maximum_fusion.3), channel_id=1, source_target_pairs={{0,4},{1,5},{2,6},{3,7},{4,0},{5,1},{6,2},{7,3},{8,12},{9,13},{10,... | collective-permute-start | bytes 294920 | tf_op jit(solution)/shard_map/ppermute | solution.py:264
  9.5 19.5 %collective-permute-start.7 = (bf16[192,640]{1,0:T(8,128)(2,1)S(1)}, bf16[192,640]{1,0:T(8,128)(2,1)S(1)}, u32[]{:S(2)}, u32[]{:S(2)}) collective-permute-start(bf16[192,640]{1,0:T(8,128)(2,1)S(1)} %pad.4.refs_0_), channel_id=1, source_target_pairs={{0,8},{1,9},{2,10},{3,11},{4,12},{5,13},{6,14},{7,15},{8,0},{9,1},... | collective-permute-start | bytes 737288 | tf_op jit(solution)/shard_map/ppermute | solution.py:264
  13.6 3.3 %copy-start.1 = (bf16[768,128]{1,0:T(8,128)(2,1)}, bf16[768,128]{1,0:T(8,128)(2,1)S(1)}, u32[]{:S(2)}) copy-start(bf16[768,128]{1,0:T(8,128)(2,1)S(1)} %pad_maximum_fusion.2.keys_ref.refs_0_) | copy-start | bytes 589828
  13.6 9.0 %collective-permute-start.2 = (bf16[768,128]{1,0:T(8,128)(2,1)S(1)}, bf16[768,128]{1,0:T(8,128)(2,1)S(1)}, u32[]{:S(2)}, u32[]{:S(2)}) collective-permute-start(bf16[768,128]{1,0:T(8,128)(2,1)S(1)} %pad_maximum_fusion.2.keys_ref.refs_0_), channel_id=1, source_target_pairs={{0,2},{1,3},{2,0},{3,1},{4,6},{5,7},{6,4},{7,5},{8,10},{9,11},{10,... | collective-permute-start | bytes 589832 | tf_op jit(solution)/shard_map/ppermute | solution.py:264
  15.4 13.7 %collective-permute-start.6 = (bf16[192,640]{1,0:T(8,128)(2,1)S(1)}, bf16[192,640]{1,0:T(8,128)(2,1)S(1)}, u32[]{:S(2)}, u32[]{:S(2)}) collective-permute-start(bf16[192,640]{1,0:T(8,128)(2,1)S(1)} %pad.4.refs_0_), channel_id=1, source_target_pairs={{0,4},{1,5},{2,6},{3,7},{4,0},{5,1},{6,2},{7,3},{8,12},{9,13},{10,... | collective-permute-start | bytes 737288 | tf_op jit(solution)/shard_map/ppermute | solution.py:264
  16.4 12.6 %collective-permute-start.4 = (bf16[192,640]{1,0:T(8,128)(2,1)S(1)}, bf16[192,640]{1,0:T(8,128)(2,1)S(1)}, u32[]{:S(2)}, u32[]{:S(2)}) collective-permute-start(bf16[192,640]{1,0:T(8,128)(2,1)S(1)} %pad.4.refs_0_), channel_id=1, source_target_pairs={{0,2},{1,3},{2,0},{3,1},{4,6},{5,7},{6,4},{7,5},{8,10},{9,11},{10,... | collective-permute-start | bytes 737288 | tf_op jit(solution)/shard_map/ppermute | solution.py:264
  22.6 6.4 %collective-permute-start.3 = (bf16[192,640]{1,0:T(8,128)(2,1)S(1)}, bf16[192,640]{1,0:T(8,128)(2,1)S(1)}, u32[]{:S(2)}, u32[]{:S(2)}) collective-permute-start(bf16[192,640]{1,0:T(8,128)(2,1)S(1)} %pad.4.refs_0_), channel_id=1, source_target_pairs={{0,1},{1,0},{2,3},{3,2},{4,5},{5,4},{6,7},{7,6},{8,9},{9,8},{10,11... | collective-permute-start | bytes 737288 | tf_op jit(solution)/shard_map/ppermute | solution.py:264
  22.7 0.7 copy-start.2
  22.7 8.7 %collective-permute-start.5 = (bf16[1536,128]{1,0:T(8,128)(2,1)S(1)}, bf16[1536,128]{1,0:T(8,128)(2,1)S(1)}, u32[]{:S(2)}, u32[]{:S(2)}) collective-permute-start(bf16[1536,128]{1,0:T(8,128)(2,1)S(1)} %pad_maximum_fusion), channel_id=1, source_target_pairs={{0,1},{1,0},{2,3},{3,2},{4,5},{5,4},{6,7},{7,6},{8,9},{9,8},{10,11... | collective-permute-start | bytes 1179656 | tf_op jit(solution)/shard_map/ppermute | solution.py:264
  29.1 19.6 %collective-permute-start.13 = (bf16[192,640]{1,0:T(8,128)(2,1)S(1)}, bf16[192,640]{1,0:T(8,128)(2,1)S(1)}, u32[]{:S(2)}, u32[]{:S(2)}) collective-permute-start(bf16[192,640]{1,0:T(8,128)(2,1)S(1)} %collective-permute-done.7.refs_8_), channel_id=1, source_target_pairs={{0,2},{1,3},{2,0},{3,1},{4,6},{5,7},{6,4},{7,5},{8,10},{9,11},{10,... | collective-permute-start | bytes 737288 | tf_op jit(solution)/shard_map/ppermute | solution.py:264
  30.6 11.6 %collective-permute-start.8 = (bf16[192,640]{1,0:T(8,128)(2,1)S(1)}, bf16[192,640]{1,0:T(8,128)(2,1)S(1)}, u32[]{:S(2)}, u32[]{:S(2)}) collective-permute-start(bf16[192,640]{1,0:T(8,128)(2,1)S(1)} %collective-permute-done.7.refs_8_), channel_id=1, source_target_pairs={{0,1},{1,0},{2,3},{3,2},{4,5},{5,4},{6,7},{7,6},{8,9},{9,8},{10,11... | collective-permute-start | bytes 737288 | tf_op jit(solution)/shard_map/ppermute | solution.py:264
  30.8 17.9 %collective-permute-start.14 = (bf16[192,640]{1,0:T(8,128)(2,1)S(1)}, bf16[192,640]{1,0:T(8,128)(2,1)S(1)}, u32[]{:S(2)}, u32[]{:S(2)}) collective-permute-start(bf16[192,640]{1,0:T(8,128)(2,1)S(1)} %collective-permute-done.6.refs_4_), channel_id=1, source_target_pairs={{0,2},{1,3},{2,0},{3,1},{4,6},{5,7},{6,4},{7,5},{8,10},{9,11},{10,... | collective-permute-start | bytes 737288 | tf_op jit(solution)/shard_map/ppermute | solution.py:264
  31.3 10.8 %collective-permute-start.9 = (bf16[192,640]{1,0:T(8,128)(2,1)S(1)}, bf16[192,640]{1,0:T(8,128)(2,1)S(1)}, u32[]{:S(2)}, u32[]{:S(2)}) collective-permute-start(bf16[192,640]{1,0:T(8,128)(2,1)S(1)} %collective-permute-done.6.refs_4_), channel_id=1, source_target_pairs={{0,1},{1,0},{2,3},{3,2},{4,5},{5,4},{6,7},{7,6},{8,9},{9,8},{10,11... | collective-permute-start | bytes 737288 | tf_op jit(solution)/shard_map/ppermute | solution.py:264
  31.4 0.9 %copy-start.3 = (bf16[1536,128]{1,0:T(8,128)(2,1)}, bf16[1536,128]{1,0:T(8,128)(2,1)S(1)}, u32[]{:S(2)}) copy-start(bf16[1536,128]{1,0:T(8,128)(2,1)S(1)} %collective-permute-done.5.keys_ref.refs_2_) | copy-start | bytes 1179652
  31.4 9.0 %collective-permute-start.10 = (bf16[192,640]{1,0:T(8,128)(2,1)S(1)}, bf16[192,640]{1,0:T(8,128)(2,1)S(1)}, u32[]{:S(2)}, u32[]{:S(2)}) collective-permute-start(bf16[192,640]{1,0:T(8,128)(2,1)S(1)} %collective-permute-done.7.refs_8_), channel_id=1, source_target_pairs={{0,4},{1,5},{2,6},{3,7},{4,0},{5,1},{6,2},{7,3},{8,12},{9,13},{10,... | collective-permute-start | bytes 737288 | tf_op jit(solution)/shard_map/ppermute | solution.py:264
  40.4 15.2 %collective-permute-start.17 = (bf16[192,640]{1,0:T(8,128)(2,1)S(1)}, bf16[192,640]{1,0:T(8,128)(2,1)S(1)}, u32[]{:S(2)}, u32[]{:S(2)}) collective-permute-start(bf16[192,640]{1,0:T(8,128)(2,1)S(1)} %collective-permute-done.10.refs_12_), channel_id=1, source_target_pairs={{0,2},{1,3},{2,0},{3,1},{4,6},{5,7},{6,4},{7,5},{8,10},{9,11},{10,... | collective-permute-start | bytes 737288 | tf_op jit(solution)/shard_map/ppermute | solution.py:264
  42.2 7.1 %collective-permute-start.11 = (bf16[192,640]{1,0:T(8,128)(2,1)S(1)}, bf16[192,640]{1,0:T(8,128)(2,1)S(1)}, u32[]{:S(2)}, u32[]{:S(2)}) collective-permute-start(bf16[192,640]{1,0:T(8,128)(2,1)S(1)} %collective-permute-done.10.refs_12_), channel_id=1, source_target_pairs={{0,1},{1,0},{2,3},{3,2},{4,5},{5,4},{6,7},{7,6},{8,9},{9,8},{10,11... | collective-permute-start | bytes 737288 | tf_op jit(solution)/shard_map/ppermute | solution.py:264
  42.2 7.1 %collective-permute-start.12 = (bf16[192,640]{1,0:T(8,128)(2,1)S(1)}, bf16[192,640]{1,0:T(8,128)(2,1)S(1)}, u32[]{:S(2)}, u32[]{:S(2)}) collective-permute-start(bf16[192,640]{1,0:T(8,128)(2,1)S(1)} %collective-permute-done.4.refs_2_), channel_id=1, source_target_pairs={{0,1},{1,0},{2,3},{3,2},{4,5},{5,4},{6,7},{7,6},{8,9},{9,8},{10,11... | collective-permute-start | bytes 737288 | tf_op jit(solution)/shard_map/ppermute | solution.py:264
  48.6 8.6 %copy-start = (s32[2,12]{1,0:T(2,128)S(1)}, s32[2,12]{1,0:T(2,128)}, u32[]{:S(2)}) copy-start(s32[2,12]{1,0:T(2,128)} %pick_ref.1) | copy-start | bytes 292
  48.7 7.1 %collective-permute-start.15 = (bf16[192,640]{1,0:T(8,128)(2,1)S(1)}, bf16[192,640]{1,0:T(8,128)(2,1)S(1)}, u32[]{:S(2)}, u32[]{:S(2)}) collective-permute-start(bf16[192,640]{1,0:T(8,128)(2,1)S(1)} %collective-permute-done.14.refs_6_), channel_id=1, source_target_pairs={{0,1},{1,0},{2,3},{3,2},{4,5},{5,4},{6,7},{7,6},{8,9},{9,8},{10,11... | collective-permute-start | bytes 737288 | tf_op jit(solution)/shard_map/ppermute | solution.py:264
  48.8 7.0 %collective-permute-start.16 = (bf16[192,640]{1,0:T(8,128)(2,1)S(1)}, bf16[192,640]{1,0:T(8,128)(2,1)S(1)}, u32[]{:S(2)}, u32[]{:S(2)}) collective-permute-start(bf16[192,640]{1,0:T(8,128)(2,1)S(1)} %collective-permute-done.13.refs_10_), channel_id=1, source_target_pairs={{0,1},{1,0},{2,3},{3,2},{4,5},{5,4},{6,7},{7,6},{8,9},{9,8},{10,11... | collective-permute-start | bytes 737288 | tf_op jit(solution)/shard_map/ppermute | solution.py:264
  55.6 1.6 %collective-permute-start.18 = (bf16[192,640]{1,0:T(8,128)(2,1)S(1)}, bf16[192,640]{1,0:T(8,128)(2,1)S(1)}, u32[]{:S(2)}, u32[]{:S(2)}) collective-permute-start(bf16[192,640]{1,0:T(8,128)(2,1)S(1)} %collective-permute-done.17.refs_14_), channel_id=1, source_target_pairs={{0,1},{1,0},{2,3},{3,2},{4,5},{5,4},{6,7},{7,6},{8,9},{9,8},{10,11... | collective-permute-start | bytes 737288 | tf_op jit(solution)/shard_map/ppermute | solution.py:264

commit v6 on v5

--- a/solution.py
+++ b/solution.py
@@ -24,16 +24,13 @@
 LOW = -1.0e30
 EXP2_SCALE = 192.0**-0.5 * 1.4426950408889634
 VMEM = 48 * 2**20
-INDEX_VMEM = 60 * 2**20
-
-
-def index_tile(iq_ref, weights, keys, pieces=None):
+
+
+def index_tile(iq_ref, weights, keys):
     keys_t = keys.T
     rows, width = iq_ref.shape[0], keys.shape[0]
     parts = []
     for t0 in range(0, rows, TOK_TILE):
-        if pieces is not None:
-            pieces[t0 // TOK_TILE].wait()
         acc = jnp.zeros((TOK_TILE, width), jnp.float32)
         for j0 in range(0, IH, HEAD_STEP):
             lhs = jnp.concatenate(
@@ -65,28 +62,19 @@
     )
 
 
-def index_tiles(iq_hbm, w_hbm, iq_ref, w_ref, sem, steps, load, store, aside=None):
-    tok = iq_ref.shape[0]
-    w_copy = pltpu.make_async_copy(w_hbm, w_ref, sem.at[tok // TOK_TILE])
-    w_copy.start()
-    pieces = []
-    for n in range(tok // TOK_TILE):
-        part = pl.ds(n * TOK_TILE, TOK_TILE)
-        pieces.append(pltpu.make_async_copy(iq_hbm.at[part], iq_ref.at[part], sem.at[n]))
-        pieces[-1].start()
-    if aside is not None:
-        aside()
-    w_copy.wait()
-    weights = w_ref[...].T * IDX**-0.5
-    store(0, index_tile(iq_ref, weights, load(0), pieces))
-    if steps > 1:
-
-        @pl.loop(1, steps)
-        def _(step):
-            store(step, index_tile(iq_ref, weights, load(step)))
-
-
-def index_window_kernel(shards, iq_hbm, w_hbm, keys_ref, out_ref, iq_ref, w_ref, sem):
+def weights_kernel(iq_ref, w_ref, out_ref):
+    out_ref[...] = w_ref[...].T * IDX**-0.5
+
+
+def index_tiles(iq_ref, w_ref, steps, load, store):
+    weights = w_ref[...]
+
+    @pl.loop(0, steps)
+    def _(step):
+        store(step, index_tile(iq_ref, weights, load(step)))
+
+
+def index_window_kernel(shards, iq_ref, w_ref, keys_ref, out_ref):
     tok = iq_ref.shape[0]
     each = TILE // tok
 
@@ -97,7 +85,7 @@
     def load(step):
         return window_keys(keys_ref, tok, each, step)
 
-    index_tiles(iq_hbm, w_hbm, iq_ref, w_ref, sem, shards // each, load, store)
+    index_tiles(iq_ref, w_ref, shards // each, load, store)
 
 
 def order_prefix(places, own, tok, key_refs, keys_ref):
@@ -108,12 +96,10 @@
             keys_ref[pl.ds(at, BLK), :] = ref[n * span : n * span + BLK, :]
 
 
-def index_prefix_kernel(places, first, steps, own_ref, iq_hbm, w_hbm, *refs):
+def index_prefix_kernel(places, first, steps, own_ref, iq_ref, w_ref, *refs):
     count = len(places)
-    out_ref, iq_ref, w_ref, sem, keys_ref = refs[count:]
-
-    def aside():
-        order_prefix(places, own_ref[0], iq_ref.shape[0], refs[:count], keys_ref)
+    out_ref, keys_ref = refs[count:]
+    order_prefix(places, own_ref[0], iq_ref.shape[0], refs[:count], keys_ref)
 
     def load(step):
         return keys_ref[pl.ds(pl.multiple_of((first + step) * TILE, TILE), TILE), :]
@@ -121,28 +107,26 @@
     def store(step, value):
         out_ref[:, pl.ds(pl.multiple_of(step * TILE, TILE), TILE)] = value
 
-    index_tiles(iq_hbm, w_hbm, iq_ref, w_ref, sem, steps, load, store, aside)
-
-
-def index_last_kernel(places, first, steps, own_ref, iq_hbm, w_hbm, *refs):
+    index_tiles(iq_ref, w_ref, steps, load, store)
+
+
+def index_last_kernel(places, first, steps, own_ref, iq_ref, w_ref, *refs):
     count = len(places)
     key_refs, done_refs = refs[:count], refs[count : 2 * count]
-    begun_ref, prefix_ref, window_ref, iq_ref, w_ref, sem, keys_ref = refs[2 * count :]
-
-    def aside():
-        own = own_ref[0]
-        tok = iq_ref.shape[0]
-        order_prefix(places, own, tok, key_refs, keys_ref)
-        prefix_ref[:, : first * TILE] = begun_ref[...]
-        row = lax.broadcasted_iota(jnp.int32, (tok, LANES), 0)
-        lane = lax.broadcasted_iota(jnp.int32, (tok, LANES), 1)
-        for ref, rels in zip(done_refs, places):
-            for n, rel in enumerate(rels):
-                other = own ^ rel
-                seen = other * tok + lane <= own * tok + row
-                window_ref[:, pl.ds(pl.multiple_of(other * tok, LANES), LANES)] = jnp.where(
-                    seen, ref[n], 0.0
-                )
+    begun_ref, prefix_ref, window_ref, keys_ref = refs[2 * count :]
+    own = own_ref[0]
+    tok = iq_ref.shape[0]
+    order_prefix(places, own, tok, key_refs, keys_ref)
+    prefix_ref[:, : first * TILE] = begun_ref[...]
+    row = lax.broadcasted_iota(jnp.int32, (tok, LANES), 0)
+    lane = lax.broadcasted_iota(jnp.int32, (tok, LANES), 1)
+    for ref, rels in zip(done_refs, places):
+        for n, rel in enumerate(rels):
+            other = own ^ rel
+            seen = other * tok + lane <= own * tok + row
+            window_ref[:, pl.ds(pl.multiple_of(other * tok, LANES), LANES)] = jnp.where(
+                seen, ref[n], 0.0
+            )
 
     def load(step):
         return keys_ref[pl.ds(pl.multiple_of((first + step) * TILE, TILE), TILE), :]
@@ -150,7 +134,7 @@
     def store(step, value):
         prefix_ref[:, pl.ds(pl.multiple_of((first + step) * TILE, TILE), TILE)] = value
 
-    index_tiles(iq_hbm, w_hbm, iq_ref, w_ref, sem, steps, load, store, aside)
+    index_tiles(iq_ref, w_ref, steps, load, store)
 
 
 def attention_kernel(devices, own_ref, pick_ref, q_ref, *refs):
@@ -273,25 +257,16 @@
             flops=2 * tok * IH * IDX * keys * 4, bytes_accessed=2**22, transcendentals=0
         )
 
-    weights = index_weights.T
-
-    index_scratch = [
-        pltpu.VMEM((tok, IH * IDX), jnp.bfloat16),
-        pltpu.VMEM((IH, tok), jnp.float32),
-        pltpu.SemaphoreType.DMA((tok // TOK_TILE + 1,)),
-    ]
     order_scratch = [pltpu.VMEM((devices * BLK, IDX), jnp.bfloat16)]
-    index_params = pltpu.CompilerParams(vmem_limit_bytes=INDEX_VMEM)
 
     def index_window(shard_keys):
         count = shard_keys.shape[0] // span
         return pl.pallas_call(
             functools.partial(index_window_kernel, count),
             out_shape=jax.ShapeDtypeStruct((count, tok, LANES), jnp.float32),
-            in_specs=[hbm, hbm, vmem],
+            in_specs=[vmem, vmem, vmem],
             out_specs=vmem,
-            scratch_shapes=index_scratch,
-            compiler_params=index_params,
+            compiler_params=params,
             cost_estimate=index_cost(count * tok),
         )(index_queries, weights, shard_keys)
 
@@ -317,6 +292,16 @@
             shards[bit] = swap(held, bit)
         key_line = jnp.concatenate([key_line, other], 0)
         line = line + [rel ^ bit for rel in line]
+        if bit != low:
+            touch_on = key_line
+    (early_queries, early_weights) = after(touch_on, index_queries, index_weights.T)
+    weights = pl.pallas_call(
+        weights_kernel,
+        out_shape=jax.ShapeDtypeStruct((tok, IH), jnp.float32),
+        in_specs=[vmem, vmem],
+        out_specs=vmem,
+        compiler_params=params,
+    )(early_queries, early_weights)
     (held,) = after(key_line, rows)
     for bit in (low, 2):
         shards[bit] = swap(held, bit)
@@ -356,10 +341,10 @@
     begun = pl.pallas_call(
         functools.partial(index_prefix_kernel, places, 0, tiles // 2),
         out_shape=jax.ShapeDtypeStruct((tok, tiles // 2 * TILE), jnp.float32),
-        in_specs=[smem, hbm, hbm, vmem, vmem, vmem],
+        in_specs=[smem] + [vmem] * 5,
         out_specs=vmem,
-        scratch_shapes=index_scratch + order_scratch,
-        compiler_params=index_params,
+        scratch_shapes=order_scratch,
+        compiler_params=params,
         cost_estimate=index_cost(tiles // 2 * TILE),
     )(own, held, weights, key_line, key_side, key_far)
     send(begun, (low | 2, 1), *[(bit | 2, 1) for bit in high])
@@ -370,10 +355,10 @@
             jax.ShapeDtypeStruct((tok, devices * BLK), jnp.float32),
             jax.ShapeDtypeStruct((tok, devices * tok), jnp.float32),
         ),
-        in_specs=[smem, hbm, hbm] + [vmem] * 7,
+        in_specs=[smem] + [vmem] * 9,
         out_specs=(vmem, vmem),
-        scratch_shapes=index_scratch + order_scratch,
-        compiler_params=index_params,
+        scratch_shapes=order_scratch,
+        compiler_params=params,
         cost_estimate=index_cost(tiles // 2 * TILE),
     )(
         own,

time: 82.6 us -> 71.1 us (0.86)
  Pallas kernels: 56.5 us -> 40.3 us
  waiting for transfers between devices: 3.54 us -> 8.52 us
  starting transfers between devices: 18.5 us -> 16.2 us
  local copies, waits for them, and re-layouts: 0.42 us -> 2.68 us
    pallas_call x3, Pallas kernels: 19.5 us -> 9.63 us  [index_window(): pl.pallas_call(functools.partial(index_window_kernel, count), out_shape=j...]
    ppermute x19, waiting for transfers between devices: 3.54 us -> 8.52 us  [swap(): return lax.ppermute(array, 'ctx', [(i, i ^ rel) for i in range(devices)])]
    pallas_call x1, Pallas kernels: 5.95 us -> 2.43 us  [body(): pl.pallas_call(functools.partial(index_prefix_kernel, places, 0, tiles //...]
    pallas_call x1, Pallas kernels: 6.37 us -> 3.38 us  [body(): pl.pallas_call(functools.partial(index_last_kernel, places, tiles // 2, t...]
    ppermute x19, starting transfers between devices: 18.5 us -> 16.2 us  [swap(): return lax.ppermute(array, 'ctx', [(i, i ^ rel) for i in range(devices)])]
    unnamed x8, local copies, waits for them, and re-layouts: 0.09 us -> 2.36 us
  transfers between devices with their start and end apart: 19 -> 19, of which waited for: 3 -> 6; matrix products, arithmetic and copies ran while one was open for 2% -> 2% of each run, Pallas kernels for 39% -> 22%
where the time goes in v6:
time: 71.1 us; the launch traced here: 70.8 us
  Pallas kernels  40.3 us (57%)
  starting transfers between devices  16.2 us (23%)
  waiting for transfers between devices  8.52 us (12%)
  local copies, waits for them, and re-layouts  2.68 us (4%)
  other arithmetic  2.1 us (3%)
  between operations  0.94 us (1%)
    pallas_call x1, Pallas kernels, body(): pl.pallas_call(functools.partial(attention_kernel, devices), grid_spec=pl...  24.7 us
    ppermute x19, starting transfers between devices, swap(): return lax.ppermute(array, 'ctx', [(i, i ^ rel) for i in range(devices)])  16.2 us
    pallas_call x3, Pallas kernels, index_window(): pl.pallas_call(functools.partial(index_window_kernel, count), out_shape=j...  9.63 us
    ppermute x19, waiting for transfers between devices, swap(): return lax.ppermute(array, 'ctx', [(i, i ^ rel) for i in range(devices)])  8.52 us
    pallas_call x1, Pallas kernels, body(): pl.pallas_call(functools.partial(index_last_kernel, places, tiles // 2, t...  3.38 us
    pallas_call x1, Pallas kernels, body(): pl.pallas_call(functools.partial(index_prefix_kernel, places, 0, tiles //...  2.43 us
    unnamed x8, local copies, waits for them, and re-layouts  2.36 us
  transfers between devices with their start and end apart: 19, of which 6 were waited for; matrix products, arithmetic and copies ran while one was open for 2% of the time, Pallas kernels for 22%

profile of v6, /device:TPU:0, one launch (start us, length us, event | category | flops | bytes accessed | tf_op | source)
XLA Modules:
  0.0 70.8 jit_solution(9593190229930993087)
XLA Ops:
  0.6 0.8 %pad_maximum_fusion.4 = bf16[192,128]{1,0:T(8,128)(2,1)S(1)} fusion(bf16[128,128]{1,0:T(8,128)(2,1)} %param.14, bf16[64,128]{1,0:T(8,128)(2,1)} %param.13), kind=kLoop, calls=%fused_computation.4 | loop fusion | flops 98304 | bytes 98304 | tf_op jit(solution)/shard_map/concatenate | solution.py:286
  1.4 4.0 %collective-permute-start = (bf16[192,128]{1,0:T(8,128)(2,1)S(1)}, bf16[192,128]{1,0:T(8,128)(2,1)S(1)}, u32[]{:S(2)}, u32[]{:S(2)}) collective-permute-start(bf16[192,128]{1,0:T(8,128)(2,1)S(1)} %pad_maximum_fusion.4), channel_id=1, source_target_pairs={{0,8},{1,9},{2,10},{3,11},{4,12},{5,13},{6,14},{7,15},{8,0},{9,1},... | collective-permute-start | bytes 147464 | tf_op jit(solution)/shard_map/ppermute | solution.py:248
  5.4 1.3 %pad_maximum_fusion.1 = bf16[3,36864]{1,0:T(4,128)(2,1)S(1)} fusion(bf16[2,36864]{1,0:T(2,128)(2,1)} %param.10, bf16[1,36864]{1,0:T(2,128)(2,1)} %param.9), kind=kLoop, calls=%fused_computation.1 | loop fusion | flops 442368 | bytes 442368 | tf_op jit(solution)/shard_map/concatenate | solution.py:283
  6.7 0.3 reshape.13
  7.1 1.0 %collective-permute-done = bf16[192,128]{1,0:T(8,128)(2,1)S(1)} collective-permute-done((bf16[192,128]{1,0:T(8,128)(2,1)S(1)}, bf16[192,128]{1,0:T(8,128)(2,1)S(1)}, u32[]{:S(2)}, u32[]{:S(2)}) %collective-permute-start) | collective-permute-done | bytes 49184 | tf_op jit(solution)/shard_map/ppermute | solution.py:248
  8.0 1.4 %collective-permute-start.1 = (bf16[384,128]{1,0:T(8,128)(2,1)S(1)}, bf16[384,128]{1,0:T(8,128)(2,1)S(1)}, u32[]{:S(2)}, u32[]{:S(2)}) collective-permute-start(bf16[384,128]{1,0:T(8,128)(2,1)S(1)} %pad_maximum_fusion.3), channel_id=1, source_target_pairs={{0,4},{1,5},{2,6},{3,7},{4,0},{5,1},{6,2},{7,3},{8,12},{9,13},{10,... | collective-permute-start | bytes 294920 | tf_op jit(solution)/shard_map/ppermute | solution.py:248
  9.5 3.0 %collective-permute-start.7 = (bf16[192,640]{1,0:T(8,128)(2,1)S(1)}, bf16[192,640]{1,0:T(8,128)(2,1)S(1)}, u32[]{:S(2)}, u32[]{:S(2)}) collective-permute-start(bf16[192,640]{1,0:T(8,128)(2,1)S(1)} %pad.4.refs_0_), channel_id=1, source_target_pairs={{0,8},{1,9},{2,10},{3,11},{4,12},{5,13},{6,14},{7,15},{8,0},{9,1},... | collective-permute-start | bytes 737288 | tf_op jit(solution)/shard_map/ppermute | solution.py:248
  12.5 1.6 %copy-done = bf16[128,8192]{1,0:T(8,128)(2,1)S(1)} copy-done((bf16[128,8192]{1,0:T(8,128)(2,1)S(1)}, bf16[128,8192]{1,0:T(8,128)(2,1)}, u32[]{:S(2)}) %copy-start) | copy-done | bytes 2097176
  14.1 0.8 %copy-done.2 = f32[128,64]{0,1:T(8,128)S(1)} copy-done((f32[128,64]{0,1:T(8,128)S(1)}, f32[128,64]{0,1:T(8,128)}, u32[]{:S(2)}) %copy-start.2) | copy-done | bytes 32792
  14.8 0.1 shard_map.103.w_ref
  15.0 1.6 %collective-permute-start.2 = (bf16[768,128]{1,0:T(8,128)(2,1)S(1)}, bf16[768,128]{1,0:T(8,128)(2,1)S(1)}, u32[]{:S(2)}, u32[]{:S(2)}) collective-permute-start(bf16[768,128]{1,0:T(8,128)(2,1)S(1)} %pad_maximum_fusion.2.keys_ref.refs_0_), channel_id=1, source_target_pairs={{0,2},{1,3},{2,0},{3,1},{4,6},{5,7},{6,4},{7,5},{8,10},{9,11},{10,... | collective-permute-start | bytes 589832 | tf_op jit(solution)/shard_map/ppermute | solution.py:248
  16.6 0.5 collective-permute-start.4
  17.1 2.4 %shard_map.105.refs_3_ = f32[4,128,128]{2,1,0:T(8,128)S(1)} custom-call(bf16[128,8192]{1,0:T(8,128)(2,1)S(1)} %copy-done, f32[128,64]{1,0:T(8,128)S(1)} %shard_map.103.w_ref, bf16[768,128]{1,0:T(8,128)(2,1)S(1)} %pad_maximum_fusion.2.keys_ref.refs_0_), custom_call_target="tpu_custom_call" | custom-call | flops 4294967296 | bytes 4194304 | tf_op jit(solution)/shard_map/pallas_call | solution.py:264
  19.6 3.0 %collective-permute-done.2.keys_ref.refs_1_ = bf16[768,128]{1,0:T(8,128)(2,1)S(1)} collective-permute-done((bf16[768,128]{1,0:T(8,128)(2,1)S(1)}, bf16[768,128]{1,0:T(8,128)(2,1)S(1)}, u32[]{:S(2)}, u32[]{:S(2)}) %collective-permute-start.2) | collective-permute-done | bytes 196640 | tf_op jit(solution)/shard_map/ppermute | solution.py:248
  22.7 2.4 %shard_map.104.refs_4_ = f32[4,128,128]{2,1,0:T(8,128)S(1)} custom-call(bf16[128,8192]{1,0:T(8,128)(2,1)S(1)} %copy-done, f32[128,64]{1,0:T(8,128)S(1)} %shard_map.103.w_ref, bf16[768,128]{1,0:T(8,128)(2,1)S(1)} %collective-permute-done.2.keys_ref.refs_1_), custom_call_target="tpu_custom_call" | custom-call | flops 4294967296 | bytes 4194304 | tf_op jit(solution)/shard_map/pallas_call | solution.py:264
  25.1 0.1 collective-permute-done.4.refs_2_
  25.2 0.3 collective-permute-done.6.refs_4_
  25.6 1.3 %collective-permute-start.13 = (bf16[192,640]{1,0:T(8,128)(2,1)S(1)}, bf16[192,640]{1,0:T(8,128)(2,1)S(1)}, u32[]{:S(2)}, u32[]{:S(2)}) collective-permute-start(bf16[192,640]{1,0:T(8,128)(2,1)S(1)} %collective-permute-done.7.refs_8_), channel_id=1, source_target_pairs={{0,2},{1,3},{2,0},{3,1},{4,6},{5,7},{6,4},{7,5},{8,10},{9,11},{10,... | collective-permute-start | bytes 737288 | tf_op jit(solution)/shard_map/ppermute | solution.py:248
  26.8 0.2 collective-permute-start.8
  27.0 0.6 collective-permute-start.14
  27.6 0.2 collective-permute-start.9
  27.8 0.6 collective-permute-start.10
  28.4 4.8 %shard_map.106.refs_5_ = f32[8,128,128]{2,1,0:T(8,128)S(1)} custom-call(bf16[128,8192]{1,0:T(8,128)(2,1)S(1)} %copy-done, f32[128,64]{1,0:T(8,128)S(1)} %shard_map.103.w_ref, bf16[1536,128]{1,0:T(8,128)(2,1)S(1)} %collective-permute-done.5.keys_ref.refs_2_), custom_call_target="tpu_custom_call" | custom-call | flops 8589934592 | bytes 4194304 | tf_op jit(solution)/shard_map/pallas_call | solution.py:264
  33.2 2.7 %collective-permute-done.10.refs_12_ = bf16[192,640]{1,0:T(8,128)(2,1)S(1)} collective-permute-done((bf16[192,640]{1,0:T(8,128)(2,1)S(1)}, bf16[192,640]{1,0:T(8,128)(2,1)S(1)}, u32[]{:S(2)}, u32[]{:S(2)}) %collective-permute-start.10) | collective-permute-done | bytes 245792 | tf_op jit(solution)/shard_map/ppermute | solution.py:248
  36.0 1.4 %collective-permute-start.17 = (bf16[192,640]{1,0:T(8,128)(2,1)S(1)}, bf16[192,640]{1,0:T(8,128)(2,1)S(1)}, u32[]{:S(2)}, u32[]{:S(2)}) collective-permute-start(bf16[192,640]{1,0:T(8,128)(2,1)S(1)} %collective-permute-done.10.refs_12_), channel_id=1, source_target_pairs={{0,2},{1,3},{2,0},{3,1},{4,6},{5,7},{6,4},{7,5},{8,10},{9,11},{10,... | collective-permute-start | bytes 737288 | tf_op jit(solution)/shard_map/ppermute | solution.py:248
  37.4 0.5 collective-permute-start.12
  37.9 2.4 %shard_map.107.refs_6_ = f32[128,512]{1,0:T(8,128)S(1)} custom-call(s32[1]{0:T(128)} %bitcast.own_ref, bf16[128,8192]{1,0:T(8,128)(2,1)S(1)} %copy-done.1, f32[128,64]{1,0:T(8,128)S(1)} %shard_map.103.w_ref, bf16[768,128]{1,0:T(8,128)(2,1)S(1)} %pad_maximum_fusion.2.keys_ref.refs_0_, bf16[768,128]{1,0:T(8,128)(2,1)S(1)} %collective-permute-done.2.keys_ref.refs_1_, ...), custom_call_target="tpu_custom_call" | custom-call | flops 4294967296 | bytes 4194304 | tf_op jit(solution)/shard_map/pallas_call | solution.py:341
  40.4 0.1 collective-permute-start.15
  40.5 0.4 collective-permute-start.16
  41.0 3.4 %shard_map.108 = (f32[128,1024]{1,0:T(8,128)}, f32[128,2048]{1,0:T(8,128)}) custom-call(s32[1]{0:T(128)} %bitcast.own_ref, bf16[128,8192]{1,0:T(8,128)(2,1)S(1)} %copy-done.1, f32[128,64]{1,0:T(8,128)S(1)} %shard_map.103.w_ref, bf16[768,128]{1,0:T(8,128)(2,1)S(1)} %pad_maximum_fusion.2.keys_ref.refs_0_, ...), custom_call_target="tpu_custom_call" | custom-call | flops 4294967296 | bytes 4194304 | tf_op jit(solution)/shard_map/pallas_call | solution.py:352
  44.4 1.4 %collective-permute-done.18.refs_15_ = bf16[192,640]{1,0:T(8,128)(2,1)S(1)} collective-permute-done((bf16[192,640]{1,0:T(8,128)(2,1)S(1)}, bf16[192,640]{1,0:T(8,128)(2,1)S(1)}, u32[]{:S(2)}, u32[]{:S(2)}) %collective-permute-start.18) | collective-permute-done | bytes 245792 | tf_op jit(solution)/shard_map/ppermute | solution.py:248
  45.9 24.7 %shard_map.109 = bf16[128,32768]{1,0:T(8,128)(2,1)} custom-call(s32[1]{0:T(128)} %bitcast.own_ref, s32[2,12]{1,0:T(2,128)S(1)} %copy-done.3, bf16[128,36864]{1,0:T(8,128)(2,1)} %q_ref.1, bf16[192,640]{1,0:T(8,128)(2,1)S(1)} %pad.4.refs_0_, bf16[192,640]{1,0:T(8,128)(2,1)S(1)} %collective-permute-done.3.refs_1_, ...), custom_call_target="tpu_custom_call" | custom-call | flops 14495514624 | bytes 16777216 | tf_op jit(solution)/shard_map/pallas_call | solution.py:379
  (28 shorter events, 0.4 us)
Async XLA Ops:
  1.4 6.6 %collective-permute-start = (bf16[192,128]{1,0:T(8,128)(2,1)S(1)}, bf16[192,128]{1,0:T(8,128)(2,1)S(1)}, u32[]{:S(2)}, u32[]{:S(2)}) collective-permute-start(bf16[192,128]{1,0:T(8,128)(2,1)S(1)} %pad_maximum_fusion.4), channel_id=1, source_target_pairs={{0,8},{1,9},{2,10},{3,11},{4,12},{5,13},{6,14},{7,15},{8,0},{9,1},... | collective-permute-start | bytes 147464 | tf_op jit(solution)/shard_map/ppermute | solution.py:248
  8.0 6.9 %collective-permute-start.1 = (bf16[384,128]{1,0:T(8,128)(2,1)S(1)}, bf16[384,128]{1,0:T(8,128)(2,1)S(1)}, u32[]{:S(2)}, u32[]{:S(2)}) collective-permute-start(bf16[384,128]{1,0:T(8,128)(2,1)S(1)} %pad_maximum_fusion.3), channel_id=1, source_target_pairs={{0,4},{1,5},{2,6},{3,7},{4,0},{5,1},{6,2},{7,3},{8,12},{9,13},{10,... | collective-permute-start | bytes 294920 | tf_op jit(solution)/shard_map/ppermute | solution.py:248
  9.5 15.8 %collective-permute-start.7 = (bf16[192,640]{1,0:T(8,128)(2,1)S(1)}, bf16[192,640]{1,0:T(8,128)(2,1)S(1)}, u32[]{:S(2)}, u32[]{:S(2)}) collective-permute-start(bf16[192,640]{1,0:T(8,128)(2,1)S(1)} %pad.4.refs_0_), channel_id=1, source_target_pairs={{0,8},{1,9},{2,10},{3,11},{4,12},{5,13},{6,14},{7,15},{8,0},{9,1},... | collective-permute-start | bytes 737288 | tf_op jit(solution)/shard_map/ppermute | solution.py:248
  12.5 1.6 %copy-start = (bf16[128,8192]{1,0:T(8,128)(2,1)S(1)}, bf16[128,8192]{1,0:T(8,128)(2,1)}, u32[]{:S(2)}) copy-start(bf16[128,8192]{1,0:T(8,128)(2,1)} %iq_ref.8) | copy-start | bytes 6291460
  14.1 0.8 %copy-start.2 = (f32[128,64]{0,1:T(8,128)S(1)}, f32[128,64]{0,1:T(8,128)}, u32[]{:S(2)}) copy-start(f32[128,64]{0,1:T(8,128)} %param.12) | copy-start | bytes 98308
  15.0 7.6 %collective-permute-start.2 = (bf16[768,128]{1,0:T(8,128)(2,1)S(1)}, bf16[768,128]{1,0:T(8,128)(2,1)S(1)}, u32[]{:S(2)}, u32[]{:S(2)}) collective-permute-start(bf16[768,128]{1,0:T(8,128)(2,1)S(1)} %pad_maximum_fusion.2.keys_ref.refs_0_), channel_id=1, source_target_pairs={{0,2},{1,3},{2,0},{3,1},{4,6},{5,7},{6,4},{7,5},{8,10},{9,11},{10,... | collective-permute-start | bytes 589832 | tf_op jit(solution)/shard_map/ppermute | solution.py:248
  16.6 9.0 %collective-permute-start.6 = (bf16[192,640]{1,0:T(8,128)(2,1)S(1)}, bf16[192,640]{1,0:T(8,128)(2,1)S(1)}, u32[]{:S(2)}, u32[]{:S(2)}) collective-permute-start(bf16[192,640]{1,0:T(8,128)(2,1)S(1)} %pad.4.refs_0_), channel_id=1, source_target_pairs={{0,4},{1,5},{2,6},{3,7},{4,0},{5,1},{6,2},{7,3},{8,12},{9,13},{10,... | collective-permute-start | bytes 737288 | tf_op jit(solution)/shard_map/ppermute | solution.py:248
  16.6 8.6 %collective-permute-start.4 = (bf16[192,640]{1,0:T(8,128)(2,1)S(1)}, bf16[192,640]{1,0:T(8,128)(2,1)S(1)}, u32[]{:S(2)}, u32[]{:S(2)}) collective-permute-start(bf16[192,640]{1,0:T(8,128)(2,1)S(1)} %pad.4.refs_0_), channel_id=1, source_target_pairs={{0,2},{1,3},{2,0},{3,1},{4,6},{5,7},{6,4},{7,5},{8,10},{9,11},{10,... | collective-permute-start | bytes 737288 | tf_op jit(solution)/shard_map/ppermute | solution.py:248
  19.6 5.7 %collective-permute-start.3 = (bf16[192,640]{1,0:T(8,128)(2,1)S(1)}, bf16[192,640]{1,0:T(8,128)(2,1)S(1)}, u32[]{:S(2)}, u32[]{:S(2)}) collective-permute-start(bf16[192,640]{1,0:T(8,128)(2,1)S(1)} %pad.4.refs_0_), channel_id=1, source_target_pairs={{0,1},{1,0},{2,3},{3,2},{4,5},{5,4},{6,7},{7,6},{8,9},{9,8},{10,11... | collective-permute-start | bytes 737288 | tf_op jit(solution)/shard_map/ppermute | solution.py:248
  22.6 5.2 %collective-permute-start.5 = (bf16[1536,128]{1,0:T(8,128)(2,1)S(1)}, bf16[1536,128]{1,0:T(8,128)(2,1)S(1)}, u32[]{:S(2)}, u32[]{:S(2)}) collective-permute-start(bf16[1536,128]{1,0:T(8,128)(2,1)S(1)} %pad_maximum_fusion), channel_id=1, source_target_pairs={{0,1},{1,0},{2,3},{3,2},{4,5},{5,4},{6,7},{7,6},{8,9},{9,8},{10,11... | collective-permute-start | bytes 1179656 | tf_op jit(solution)/shard_map/ppermute | solution.py:248
  25.1 12.8 %copy-start.1 = (bf16[128,8192]{1,0:T(8,128)(2,1)S(1)}, bf16[128,8192]{1,0:T(8,128)(2,1)}, u32[]{:S(2)}) copy-start(bf16[128,8192]{1,0:T(8,128)(2,1)} %iq_ref.8) | copy-start | bytes 6291460
  25.6 14.8 %collective-permute-start.13 = (bf16[192,640]{1,0:T(8,128)(2,1)S(1)}, bf16[192,640]{1,0:T(8,128)(2,1)S(1)}, u32[]{:S(2)}, u32[]{:S(2)}) collective-permute-start(bf16[192,640]{1,0:T(8,128)(2,1)S(1)} %collective-permute-done.7.refs_8_), channel_id=1, source_target_pairs={{0,2},{1,3},{2,0},{3,1},{4,6},{5,7},{6,4},{7,5},{8,10},{9,11},{10,... | collective-permute-start | bytes 737288 | tf_op jit(solution)/shard_map/ppermute | solution.py:248
  26.8 10.6 %collective-permute-start.8 = (bf16[192,640]{1,0:T(8,128)(2,1)S(1)}, bf16[192,640]{1,0:T(8,128)(2,1)S(1)}, u32[]{:S(2)}, u32[]{:S(2)}) collective-permute-start(bf16[192,640]{1,0:T(8,128)(2,1)S(1)} %collective-permute-done.7.refs_8_), channel_id=1, source_target_pairs={{0,1},{1,0},{2,3},{3,2},{4,5},{5,4},{6,7},{7,6},{8,9},{9,8},{10,11... | collective-permute-start | bytes 737288 | tf_op jit(solution)/shard_map/ppermute | solution.py:248
  27.0 13.4 %collective-permute-start.14 = (bf16[192,640]{1,0:T(8,128)(2,1)S(1)}, bf16[192,640]{1,0:T(8,128)(2,1)S(1)}, u32[]{:S(2)}, u32[]{:S(2)}) collective-permute-start(bf16[192,640]{1,0:T(8,128)(2,1)S(1)} %collective-permute-done.6.refs_4_), channel_id=1, source_target_pairs={{0,2},{1,3},{2,0},{3,1},{4,6},{5,7},{6,4},{7,5},{8,10},{9,11},{10,... | collective-permute-start | bytes 737288 | tf_op jit(solution)/shard_map/ppermute | solution.py:248
  27.6 9.8 %collective-permute-start.9 = (bf16[192,640]{1,0:T(8,128)(2,1)S(1)}, bf16[192,640]{1,0:T(8,128)(2,1)S(1)}, u32[]{:S(2)}, u32[]{:S(2)}) collective-permute-start(bf16[192,640]{1,0:T(8,128)(2,1)S(1)} %collective-permute-done.6.refs_4_), channel_id=1, source_target_pairs={{0,1},{1,0},{2,3},{3,2},{4,5},{5,4},{6,7},{7,6},{8,9},{9,8},{10,11... | collective-permute-start | bytes 737288 | tf_op jit(solution)/shard_map/ppermute | solution.py:248
  27.8 8.1 %collective-permute-start.10 = (bf16[192,640]{1,0:T(8,128)(2,1)S(1)}, bf16[192,640]{1,0:T(8,128)(2,1)S(1)}, u32[]{:S(2)}, u32[]{:S(2)}) collective-permute-start(bf16[192,640]{1,0:T(8,128)(2,1)S(1)} %collective-permute-done.7.refs_8_), channel_id=1, source_target_pairs={{0,4},{1,5},{2,6},{3,7},{4,0},{5,1},{6,2},{7,3},{8,12},{9,13},{10,... | collective-permute-start | bytes 737288 | tf_op jit(solution)/shard_map/ppermute | solution.py:248
  36.0 8.4 %collective-permute-start.17 = (bf16[192,640]{1,0:T(8,128)(2,1)S(1)}, bf16[192,640]{1,0:T(8,128)(2,1)S(1)}, u32[]{:S(2)}, u32[]{:S(2)}) collective-permute-start(bf16[192,640]{1,0:T(8,128)(2,1)S(1)} %collective-permute-done.10.refs_12_), channel_id=1, source_target_pairs={{0,2},{1,3},{2,0},{3,1},{4,6},{5,7},{6,4},{7,5},{8,10},{9,11},{10,... | collective-permute-start | bytes 737288 | tf_op jit(solution)/shard_map/ppermute | solution.py:248
  37.4 3.6 %collective-permute-start.11 = (bf16[192,640]{1,0:T(8,128)(2,1)S(1)}, bf16[192,640]{1,0:T(8,128)(2,1)S(1)}, u32[]{:S(2)}, u32[]{:S(2)}) collective-permute-start(bf16[192,640]{1,0:T(8,128)(2,1)S(1)} %collective-permute-done.10.refs_12_), channel_id=1, source_target_pairs={{0,1},{1,0},{2,3},{3,2},{4,5},{5,4},{6,7},{7,6},{8,9},{9,8},{10,11... | collective-permute-start | bytes 737288 | tf_op jit(solution)/shard_map/ppermute | solution.py:248
  37.4 3.6 %collective-permute-start.12 = (bf16[192,640]{1,0:T(8,128)(2,1)S(1)}, bf16[192,640]{1,0:T(8,128)(2,1)S(1)}, u32[]{:S(2)}, u32[]{:S(2)}) collective-permute-start(bf16[192,640]{1,0:T(8,128)(2,1)S(1)} %collective-permute-done.4.refs_2_), channel_id=1, source_target_pairs={{0,1},{1,0},{2,3},{3,2},{4,5},{5,4},{6,7},{7,6},{8,9},{9,8},{10,11... | collective-permute-start | bytes 737288 | tf_op jit(solution)/shard_map/ppermute | solution.py:248
  40.4 5.5 %copy-start.3 = (s32[2,12]{1,0:T(2,128)S(1)}, s32[2,12]{1,0:T(2,128)}, u32[]{:S(2)}) copy-start(s32[2,12]{1,0:T(2,128)} %pick_ref.1) | copy-start | bytes 292
  40.4 4.0 %collective-permute-start.15 = (bf16[192,640]{1,0:T(8,128)(2,1)S(1)}, bf16[192,640]{1,0:T(8,128)(2,1)S(1)}, u32[]{:S(2)}, u32[]{:S(2)}) collective-permute-start(bf16[192,640]{1,0:T(8,128)(2,1)S(1)} %collective-permute-done.14.refs_6_), channel_id=1, source_target_pairs={{0,1},{1,0},{2,3},{3,2},{4,5},{5,4},{6,7},{7,6},{8,9},{9,8},{10,11... | collective-permute-start | bytes 737288 | tf_op jit(solution)/shard_map/ppermute | solution.py:248
  40.5 3.9 %collective-permute-start.16 = (bf16[192,640]{1,0:T(8,128)(2,1)S(1)}, bf16[192,640]{1,0:T(8,128)(2,1)S(1)}, u32[]{:S(2)}, u32[]{:S(2)}) collective-permute-start(bf16[192,640]{1,0:T(8,128)(2,1)S(1)} %collective-permute-done.13.refs_10_), channel_id=1, source_target_pairs={{0,1},{1,0},{2,3},{3,2},{4,5},{5,4},{6,7},{7,6},{8,9},{9,8},{10,11... | collective-permute-start | bytes 737288 | tf_op jit(solution)/shard_map/ppermute | solution.py:248
  44.4 1.5 %collective-permute-start.18 = (bf16[192,640]{1,0:T(8,128)(2,1)S(1)}, bf16[192,640]{1,0:T(8,128)(2,1)S(1)}, u32[]{:S(2)}, u32[]{:S(2)}) collective-permute-start(bf16[192,640]{1,0:T(8,128)(2,1)S(1)} %collective-permute-done.17.refs_14_), channel_id=1, source_target_pairs={{0,1},{1,0},{2,3},{3,2},{4,5},{5,4},{6,7},{7,6},{8,9},{9,8},{10,11... | collective-permute-start | bytes 737288 | tf_op jit(solution)/shard_map/ppermute | solution.py:248

commit v7 on v6

--- a/solution.py
+++ b/solution.py
@@ -110,14 +110,50 @@
     index_tiles(iq_ref, w_ref, steps, load, store)
 
 
-def index_last_kernel(places, first, steps, own_ref, iq_ref, w_ref, *refs):
+def split_pick(pick, devices, own):
+    window = pick - devices
+    holder = jnp.where(window < 0, pick, window // 2)
+    return holder ^ own, jnp.where(window < 0, 0, 1 + window % 2)
+
+
+def find_blocks(need, pick_ref, devices, own):
+    for rel in range(devices):
+        need[rel] = 0
+    for b in range(pick_ref.shape[0]):
+        for s in range(pick_ref.shape[1]):
+            rel, inner = split_pick(pick_ref[b, s], devices, own)
+            need[rel] = inner
+
+
+def block_copy(shard, inner, target, sem):
+    return pltpu.make_async_copy(
+        shard.at[pl.ds(pl.multiple_of(inner * BLK, BLK), BLK)], target, sem
+    )
+
+
+def index_last_kernel(places, early, first, steps, own_ref, pick_ref, iq_ref, w_ref, *refs):
     count = len(places)
     key_refs, done_refs = refs[:count], refs[count : 2 * count]
-    begun_ref, prefix_ref, window_ref, keys_ref = refs[2 * count :]
+    begun_ref, shards = refs[2 * count], refs[2 * count + 1 : 2 * count + 1 + len(early)]
+    rest = refs[2 * count + 1 + len(early) :]
+    prefix_hbm, window_hbm, cache, keys_ref, prefix_ref, window_ref, need, sem = rest
     own = own_ref[0]
     tok = iq_ref.shape[0]
+    devices = prefix_ref.shape[1] // BLK
+    find_blocks(need, pick_ref, devices, own)
+    copies = []
+    for n, rel in enumerate(early):
+        if rel:
+            copies.append(block_copy(shards[n], need[rel], cache.at[n], sem.at[n]))
+        else:
+            slots = [n, len(early), len(early) + 1]
+            copies += [
+                block_copy(shards[n], inner, cache.at[slot], sem.at[slot])
+                for inner, slot in enumerate(slots)
+            ]
+    for copy in copies:
+        copy.start()
     order_prefix(places, own, tok, key_refs, keys_ref)
-    prefix_ref[:, : first * TILE] = begun_ref[...]
     row = lax.broadcasted_iota(jnp.int32, (tok, LANES), 0)
     lane = lax.broadcasted_iota(jnp.int32, (tok, LANES), 1)
     for ref, rels in zip(done_refs, places):
@@ -127,6 +163,9 @@
             window_ref[:, pl.ds(pl.multiple_of(other * tok, LANES), LANES)] = jnp.where(
                 seen, ref[n], 0.0
             )
+    prefix_ref[:, : first * TILE] = begun_ref[...]
+    window_out = pltpu.make_async_copy(window_ref, window_hbm, sem.at[len(early) + 2])
+    window_out.start()
 
     def load(step):
         return keys_ref[pl.ds(pl.multiple_of((first + step) * TILE, TILE), TILE), :]
@@ -135,43 +174,37 @@
         prefix_ref[:, pl.ds(pl.multiple_of((first + step) * TILE, TILE), TILE)] = value
 
     index_tiles(iq_ref, w_ref, steps, load, store)
-
-
-def attention_kernel(devices, own_ref, pick_ref, q_ref, *refs):
-    shards = refs[:devices]
-    out_ref, cache, raw, even_t, odd_t, need, sem = refs[devices:]
+    prefix_out = pltpu.make_async_copy(prefix_ref, prefix_hbm, sem.at[len(early) + 3])
+    prefix_out.start()
+    for copy in copies:
+        copy.wait()
+    window_out.wait()
+    prefix_out.wait()
+
+
+def attention_kernel(early, late, own_ref, pick_ref, q_ref, cache, *refs):
+    shards = refs[: len(late)]
+    out_ref, fetched, raw, even_t, odd_t, need, slot_of, sem = refs[len(late) :]
     block = pl.program_id(0)
     own = own_ref[0]
     picks = pick_ref.shape[1]
-
-    def split(pick):
-        window = pick - devices
-        holder = jnp.where(window < 0, pick, window // 2)
-        return holder ^ own, jnp.where(window < 0, 0, 1 + window % 2)
-
-    def fetch(rel, inner, slot):
-        return pltpu.make_async_copy(
-            shards[rel].at[pl.ds(pl.multiple_of(inner * BLK, BLK), BLK)],
-            cache.at[slot],
-            sem.at[slot],
-        )
+    devices = len(early) + len(late)
 
     @pl.when((block == 0) & (pl.program_id(1) == 0))
     def _():
-        for rel in range(devices):
-            need[rel] = 0
-        for b in range(pick_ref.shape[0]):
-            for s in range(picks):
-                rel, inner = split(pick_ref[b, s])
-                need[rel] = inner
-        for n in range(3):
-            fetch(0, n, 0 if n == 0 else devices - 1 + n).start()
-        for rel in range(1, devices):
-            fetch(rel, need[rel], rel).start()
-        for n in range(3):
-            fetch(0, n, 0 if n == 0 else devices - 1 + n).wait()
-        for rel in range(1, devices):
-            fetch(rel, need[rel], rel).wait()
+        find_blocks(need, pick_ref, devices, own)
+        copies = [
+            block_copy(shards[n], need[rel], fetched.at[n], sem.at[n])
+            for n, rel in enumerate(late)
+        ]
+        for copy in copies:
+            copy.start()
+        for n, rel in enumerate(early):
+            slot_of[rel] = n
+        for n, rel in enumerate(late):
+            slot_of[rel] = len(early) + 2 + n
+        for copy in copies:
+            copy.wait()
 
     @pl.when(pl.program_id(1) == 0)
     def _():
@@ -181,9 +214,18 @@
             own_slot = jnp.where(pick_ref[block, s] == own_pick, s, own_slot)
         for s in range(picks):
             place = jnp.where(own_slot == s, picks - 1, own_slot if s == picks - 1 else s)
-            rel, inner = split(pick_ref[block, s])
-            slot = jnp.where((rel == 0) & (inner > 0), devices - 1 + inner, rel)
-            raw[pl.ds(pl.multiple_of(place * BLK, BLK), BLK), :] = cache[slot]
+            rel, inner = split_pick(pick_ref[block, s], devices, own)
+            slot = jnp.where((rel == 0) & (inner > 0), len(early) - 1 + inner, slot_of[rel])
+            rows = pl.ds(pl.multiple_of(place * BLK, BLK), BLK)
+
+            @pl.when(slot < len(early) + 2)
+            def _():
+                raw[rows, :] = cache[slot]
+
+            @pl.when(slot >= len(early) + 2)
+            def _():
+                raw[rows, :] = fetched[slot - (len(early) + 2)]
+
         turned = raw[...].T
         even_t[...] = turned
         odd_t[0:ROPE] = turned[ROW:WIDE]
@@ -325,7 +367,7 @@
 
     side_done = index_window(key_side)
     side_done = settle(side_done, weights, [1, 2])
-    send(side_done, (low, 2), (low, 1), *[(bit, 2) for bit in high], *[(bit, 1) for bit in high])
+    send(side_done, *[(bit, 2) for bit in high], (low, 2), (2, 1))
     rest = []
     for n, bit in enumerate(high):
         for other in bits[n + 1 :]:
@@ -334,8 +376,15 @@
                 shards[rel ^ other] = swap(held, other)
                 rest.append(rel ^ other)
     far_done = index_window(key_far)
-    send(far_done, *[(rel, 2) for rel in rest], *[(rel, 1) for rel in rest], (2, 1))
-    held = settle(index_queries, far_done, [rel ^ 1 for rel in bits] + rest)
+    far_done = settle(far_done, weights, [bit | 2 for bit in high])
+    send(
+        far_done,
+        *[(rel, 2) for rel in rest],
+        *[(bit | 2, 1) for bit in high],
+        *[(rel, 1) for rel in rest],
+        *[(bit, 1) for bit in high],
+    )
+    held = settle(index_queries, far_done, rest + [3])
     places = [line, side, far]
     tiles = devices * BLK // TILE
     begun = pl.pallas_call(
@@ -347,22 +396,33 @@
         compiler_params=params,
         cost_estimate=index_cost(tiles // 2 * TILE),
     )(own, held, weights, key_line, key_side, key_far)
-    send(begun, (low | 2, 1), *[(bit | 2, 1) for bit in high])
-    held = settle(index_queries, begun, [rel ^ 1 for rel in rest] + [3] + [rel | 2 for rel in bits])
-    prefix_index, window_index = pl.pallas_call(
-        functools.partial(index_last_kernel, places, tiles // 2, tiles - tiles // 2),
+    early = [0, 1, 2, 3, low, low | 2] + [rel for bit in high for rel in (bit, bit | 1, bit | 2, bit | 3)]
+    early += [rel | n for rel in rest for n in (0, 1)]
+    begun = settle(begun, weights, [rel for rel in early if rel])
+    send(begun, (low, 1), (low | 2, 1))
+    late = [rel for rel in range(devices) if rel not in early]
+    prefix_index, window_index, cache = pl.pallas_call(
+        functools.partial(index_last_kernel, places, early, tiles // 2, tiles - tiles // 2),
         out_shape=(
             jax.ShapeDtypeStruct((tok, devices * BLK), jnp.float32),
             jax.ShapeDtypeStruct((tok, devices * tok), jnp.float32),
+            jax.ShapeDtypeStruct((len(early) + 2, BLK, WIDE), jnp.bfloat16),
         ),
-        in_specs=[smem] + [vmem] * 9,
-        out_specs=(vmem, vmem),
-        scratch_shapes=order_scratch,
+        in_specs=[smem, smem] + [vmem] * 9 + [hbm] * len(early),
+        out_specs=(hbm, hbm, vmem),
+        scratch_shapes=order_scratch
+        + [
+            pltpu.VMEM((tok, devices * BLK), jnp.float32),
+            pltpu.VMEM((tok, devices * tok), jnp.float32),
+            pltpu.SMEM((devices,), jnp.int32),
+            pltpu.SemaphoreType.DMA((len(early) + 4,)),
+        ],
         compiler_params=params,
         cost_estimate=index_cost(tiles // 2 * TILE),
     )(
         own,
-        held,
+        picks,
+        index_queries,
         weights,
         key_line,
         key_side,
@@ -371,26 +431,28 @@
         side_done,
         far_done,
         begun,
+        *[shards[rel] for rel in early],
     )
     send(prefix_index, *[(rel | 2, 1) for rel in rest])
-    shards = [shards[rel] for rel in range(devices)]
 
     count = picks.shape[1] * BLK
     attention = pl.pallas_call(
-        functools.partial(attention_kernel, devices),
+        functools.partial(attention_kernel, early, late),
         grid_spec=pltpu.PrefetchScalarGridSpec(
             num_scalar_prefetch=2,
             grid=(per_device, H // 2 // PAIRS),
             in_specs=[pl.BlockSpec((BLK, PAIRS * 2 * ROW), lambda b, h, *_: (b, h))]
-            + [hbm] * devices,
+            + [vmem]
+            + [hbm] * len(late),
             out_specs=pl.BlockSpec((BLK, PAIRS * 2 * LAT), lambda b, h, *_: (b, h)),
             scratch_shapes=[
-                pltpu.VMEM((devices + 2, BLK, WIDE), jnp.bfloat16),
+                pltpu.VMEM((len(late), BLK, WIDE), jnp.bfloat16),
                 pltpu.VMEM((count, WIDE), jnp.bfloat16),
                 pltpu.VMEM((WIDE, count), jnp.bfloat16),
                 pltpu.VMEM((WIDE, count), jnp.bfloat16),
                 pltpu.SMEM((devices,), jnp.int32),
-                pltpu.SemaphoreType.DMA((devices + 2,)),
+                pltpu.SMEM((devices,), jnp.int32),
+                pltpu.SemaphoreType.DMA((len(late),)),
             ],
         ),
         out_shape=jax.ShapeDtypeStruct((tok, H * LAT), jnp.bfloat16),
@@ -398,7 +460,7 @@
         cost_estimate=pl.CostEstimate(
             flops=2 * tok * H * count * (WIDE + LAT), bytes_accessed=2**24, transcendentals=0
         ),
-    )(own, picks, queries, *shards)
+    )(own, picks, queries, cache, *[shards[rel] for rel in late])
     return (attention, prefix_index, window_index)
 
 

time: 71.1 us -> 75.6 us (1.063)
  Pallas kernels: 40.3 us -> 43.5 us
  local copies, waits for them, and re-layouts: 2.68 us -> 3.94 us
    pallas_call x2, Pallas kernels: 28.1 us -> 31.2 us  [the longest x1 23.4 us: body(): pl.pallas_call(functools.partial(attention_kernel, early, late), grid_spe...]
    unnamed x8, local copies, waits for them, and re-layouts: 2.36 us -> 3.61 us
  transfers between devices with their start and end apart: 19 -> 19, of which waited for: 6 -> 9; matrix products, arithmetic and copies ran while one was open for 2% -> 2% of each run, Pallas kernels for 22% -> 27%
where the time goes in v7:
time: 75.6 us; the launch traced here: 75.2 us
  Pallas kernels  43.5 us (58%)
  starting transfers between devices  15.6 us (21%)
  waiting for transfers between devices  9.14 us (12%)
  local copies, waits for them, and re-layouts  3.94 us (5%)
  other arithmetic  2.1 us (3%)
  between operations  0.95 us (1%)
    pallas_call x1, Pallas kernels, body(): pl.pallas_call(functools.partial(attention_kernel, early, late), grid_spe...  23.4 us
    ppermute x19, starting transfers between devices, swap(): return lax.ppermute(array, 'ctx', [(i, i ^ rel) for i in range(devices)])  15.6 us
    pallas_call x3, Pallas kernels, index_window(): pl.pallas_call(functools.partial(index_window_kernel, count), out_shape=j...  9.82 us
    ppermute x19, waiting for transfers between devices, swap(): return lax.ppermute(array, 'ctx', [(i, i ^ rel) for i in range(devices)])  9.14 us
    pallas_call x1, Pallas kernels, body(): pl.pallas_call(functools.partial(index_last_kernel, places, early, tiles...  7.8 us
    unnamed x8, local copies, waits for them, and re-layouts  3.61 us
    pallas_call x1, Pallas kernels, body(): pl.pallas_call(functools.partial(index_prefix_kernel, places, 0, tiles //...  2.4 us
  transfers between devices with their start and end apart: 19, of which 9 were waited for; matrix products, arithmetic and copies ran while one was open for 2% of the time, Pallas kernels for 27%

profile of v7, /device:TPU:0, one launch (start us, length us, event | category | flops | bytes accessed | tf_op | source)
XLA Modules:
  0.0 75.2 jit_solution(7517559500496671842)
XLA Ops:
  0.6 0.8 %pad_maximum_fusion.4 = bf16[192,128]{1,0:T(8,128)(2,1)S(1)} fusion(bf16[128,128]{1,0:T(8,128)(2,1)} %param.14, bf16[64,128]{1,0:T(8,128)(2,1)} %param.13), kind=kLoop, calls=%fused_computation.4 | loop fusion | flops 98304 | bytes 98304 | tf_op jit(solution)/shard_map/concatenate | solution.py:328
  1.4 4.0 %collective-permute-start = (bf16[192,128]{1,0:T(8,128)(2,1)S(1)}, bf16[192,128]{1,0:T(8,128)(2,1)S(1)}, u32[]{:S(2)}, u32[]{:S(2)}) collective-permute-start(bf16[192,128]{1,0:T(8,128)(2,1)S(1)} %pad_maximum_fusion.4), channel_id=1, source_target_pairs={{0,8},{1,9},{2,10},{3,11},{4,12},{5,13},{6,14},{7,15},{8,0},{9,1},... | collective-permute-start | bytes 147464 | tf_op jit(solution)/shard_map/ppermute | solution.py:290
  5.4 1.3 %pad_maximum_fusion.1 = bf16[3,36864]{1,0:T(4,128)(2,1)S(1)} fusion(bf16[2,36864]{1,0:T(2,128)(2,1)} %param.10, bf16[1,36864]{1,0:T(2,128)(2,1)} %param.9), kind=kLoop, calls=%fused_computation.1 | loop fusion | flops 442368 | bytes 442368 | tf_op jit(solution)/shard_map/concatenate | solution.py:325
  6.7 0.3 reshape.13
  7.1 1.0 %collective-permute-done = bf16[192,128]{1,0:T(8,128)(2,1)S(1)} collective-permute-done((bf16[192,128]{1,0:T(8,128)(2,1)S(1)}, bf16[192,128]{1,0:T(8,128)(2,1)S(1)}, u32[]{:S(2)}, u32[]{:S(2)}) %collective-permute-start) | collective-permute-done | bytes 49184 | tf_op jit(solution)/shard_map/ppermute | solution.py:290
  8.0 1.4 %collective-permute-start.1 = (bf16[384,128]{1,0:T(8,128)(2,1)S(1)}, bf16[384,128]{1,0:T(8,128)(2,1)S(1)}, u32[]{:S(2)}, u32[]{:S(2)}) collective-permute-start(bf16[384,128]{1,0:T(8,128)(2,1)S(1)} %pad_maximum_fusion.3), channel_id=1, source_target_pairs={{0,4},{1,5},{2,6},{3,7},{4,0},{5,1},{6,2},{7,3},{8,12},{9,13},{10,... | collective-permute-start | bytes 294920 | tf_op jit(solution)/shard_map/ppermute | solution.py:290
  9.5 3.0 %collective-permute-start.7 = (bf16[192,640]{1,0:T(8,128)(2,1)S(1)}, bf16[192,640]{1,0:T(8,128)(2,1)S(1)}, u32[]{:S(2)}, u32[]{:S(2)}) collective-permute-start(bf16[192,640]{1,0:T(8,128)(2,1)S(1)} %pad.4.refs_7_), channel_id=1, source_target_pairs={{0,8},{1,9},{2,10},{3,11},{4,12},{5,13},{6,14},{7,15},{8,0},{9,1},... | collective-permute-start | bytes 737288 | tf_op jit(solution)/shard_map/ppermute | solution.py:290
  12.5 1.6 %copy-done = bf16[128,8192]{1,0:T(8,128)(2,1)S(1)} copy-done((bf16[128,8192]{1,0:T(8,128)(2,1)S(1)}, bf16[128,8192]{1,0:T(8,128)(2,1)}, u32[]{:S(2)}) %copy-start) | copy-done | bytes 2097176
  14.1 0.8 %copy-done.1 = f32[128,64]{0,1:T(8,128)S(1)} copy-done((f32[128,64]{0,1:T(8,128)S(1)}, f32[128,64]{0,1:T(8,128)}, u32[]{:S(2)}) %copy-start.1) | copy-done | bytes 32792
  15.0 1.6 %collective-permute-start.2 = (bf16[768,128]{1,0:T(8,128)(2,1)S(1)}, bf16[768,128]{1,0:T(8,128)(2,1)S(1)}, u32[]{:S(2)}, u32[]{:S(2)}) collective-permute-start(bf16[768,128]{1,0:T(8,128)(2,1)S(1)} %pad_maximum_fusion.2.keys_ref.refs_0_), channel_id=1, source_target_pairs={{0,2},{1,3},{2,0},{3,1},{4,6},{5,7},{6,4},{7,5},{8,10},{9,11},{10,... | collective-permute-start | bytes 589832 | tf_op jit(solution)/shard_map/ppermute | solution.py:290
  16.6 0.5 collective-permute-start.5
  17.1 2.4 %shard_map.104.refs_3_ = f32[4,128,128]{2,1,0:T(8,128)S(1)} custom-call(bf16[128,8192]{1,0:T(8,128)(2,1)S(1)} %copy-done, f32[128,64]{1,0:T(8,128)S(1)} %shard_map.103.w_ref, bf16[768,128]{1,0:T(8,128)(2,1)S(1)} %pad_maximum_fusion.2.keys_ref.refs_0_), custom_call_target="tpu_custom_call" | custom-call | flops 4294967296 | bytes 4194304 | tf_op jit(solution)/shard_map/pallas_call | solution.py:306
  19.6 3.0 %collective-permute-done.2.keys_ref.refs_1_ = bf16[768,128]{1,0:T(8,128)(2,1)S(1)} collective-permute-done((bf16[768,128]{1,0:T(8,128)(2,1)S(1)}, bf16[768,128]{1,0:T(8,128)(2,1)S(1)}, u32[]{:S(2)}, u32[]{:S(2)}) %collective-permute-start.2) | collective-permute-done | bytes 196640 | tf_op jit(solution)/shard_map/ppermute | solution.py:290
  22.7 2.4 %shard_map.105.refs_4_ = f32[4,128,128]{2,1,0:T(8,128)S(1)} custom-call(bf16[128,8192]{1,0:T(8,128)(2,1)S(1)} %copy-done, f32[128,64]{1,0:T(8,128)S(1)} %shard_map.103.w_ref, bf16[768,128]{1,0:T(8,128)(2,1)S(1)} %collective-permute-done.2.keys_ref.refs_1_), custom_call_target="tpu_custom_call" | custom-call | flops 4294967296 | bytes 4194304 | tf_op jit(solution)/shard_map/pallas_call | solution.py:306
  25.1 0.1 collective-permute-done.5.refs_9_
  25.2 0.3 collective-permute-done.6.refs_11_
  25.6 0.6 collective-permute-start.9
  26.1 1.1 %collective-permute-start.8 = (bf16[192,640]{1,0:T(8,128)(2,1)S(1)}, bf16[192,640]{1,0:T(8,128)(2,1)S(1)}, u32[]{:S(2)}, u32[]{:S(2)}) collective-permute-start(bf16[192,640]{1,0:T(8,128)(2,1)S(1)} %collective-permute-done.7.refs_13_), channel_id=1, source_target_pairs={{0,2},{1,3},{2,0},{3,1},{4,6},{5,7},{6,4},{7,5},{8,10},{9,11},{10,... | collective-permute-start | bytes 737288 | tf_op jit(solution)/shard_map/ppermute | solution.py:290
  27.2 1.0 %collective-permute-start.11 = (bf16[192,640]{1,0:T(8,128)(2,1)S(1)}, bf16[192,640]{1,0:T(8,128)(2,1)S(1)}, u32[]{:S(2)}, u32[]{:S(2)}) collective-permute-start(bf16[192,640]{1,0:T(8,128)(2,1)S(1)} %collective-permute-done.6.refs_11_), channel_id=1, source_target_pairs={{0,2},{1,3},{2,0},{3,1},{4,6},{5,7},{6,4},{7,5},{8,10},{9,11},{10,... | collective-permute-start | bytes 737288 | tf_op jit(solution)/shard_map/ppermute | solution.py:290
  28.2 5.0 %shard_map.106.refs_5_ = f32[8,128,128]{2,1,0:T(8,128)S(1)} custom-call(bf16[128,8192]{1,0:T(8,128)(2,1)S(1)} %copy-done, f32[128,64]{1,0:T(8,128)S(1)} %shard_map.103.w_ref, bf16[1536,128]{1,0:T(8,128)(2,1)S(1)} %collective-permute-done.3.keys_ref.refs_2_), custom_call_target="tpu_custom_call" | custom-call | flops 8589934592 | bytes 4194304 | tf_op jit(solution)/shard_map/pallas_call | solution.py:306
  33.2 1.8 %collective-permute-done.8.refs_15_ = bf16[192,640]{1,0:T(8,128)(2,1)S(1)} collective-permute-done((bf16[192,640]{1,0:T(8,128)(2,1)S(1)}, bf16[192,640]{1,0:T(8,128)(2,1)S(1)}, u32[]{:S(2)}, u32[]{:S(2)}) %collective-permute-start.8) | collective-permute-done | bytes 245792 | tf_op jit(solution)/shard_map/ppermute | solution.py:290
  35.0 1.0 %collective-permute-start.17 = (bf16[192,640]{1,0:T(8,128)(2,1)S(1)}, bf16[192,640]{1,0:T(8,128)(2,1)S(1)}, u32[]{:S(2)}, u32[]{:S(2)}) collective-permute-start(bf16[192,640]{1,0:T(8,128)(2,1)S(1)} %collective-permute-done.9.refs_17_), channel_id=1, source_target_pairs={{0,2},{1,3},{2,0},{3,1},{4,6},{5,7},{6,4},{7,5},{8,10},{9,11},{10,... | collective-permute-start | bytes 737288 | tf_op jit(solution)/shard_map/ppermute | solution.py:290
  36.0 0.5 collective-permute-start.12
  36.5 2.4 %shard_map.107.refs_6_ = f32[128,512]{1,0:T(8,128)S(1)} custom-call(s32[1]{0:T(128)} %bitcast.own_ref, bf16[128,8192]{1,0:T(8,128)(2,1)S(1)} %copy-done, f32[128,64]{1,0:T(8,128)S(1)} %shard_map.103.w_ref, bf16[768,128]{1,0:T(8,128)(2,1)S(1)} %pad_maximum_fusion.2.keys_ref.refs_0_, bf16[768,128]{1,0:T(8,128)(2,1)S(1)} %collective-permute-done.2.keys_ref.refs_1_, ...), custom_call_target="tpu_custom_call" | custom-call | flops 4294967296 | bytes 4194304 | tf_op jit(solution)/shard_map/pallas_call | solution.py:390
  38.9 1.3 %collective-permute-done.11.refs_12_ = bf16[192,640]{1,0:T(8,128)(2,1)S(1)} collective-permute-done((bf16[192,640]{1,0:T(8,128)(2,1)S(1)}, bf16[192,640]{1,0:T(8,128)(2,1)S(1)}, u32[]{:S(2)}, u32[]{:S(2)}) %collective-permute-start.11) | collective-permute-done | bytes 245792 | tf_op jit(solution)/shard_map/ppermute | solution.py:290
  40.3 7.8 %shard_map.108 = (f32[128,1024]{1,0:T(8,128)}, f32[128,2048]{1,0:T(8,128)}, bf16[14,64,640]{2,1,0:T(8,128)(2,1)}) custom-call(s32[1]{0:T(128)} %bitcast.own_ref, s32[2,12]{1,0:T(2,128)S(1)} %copy-done.2, bf16[128,8192]{1,0:T(8,128)(2,1)} %iq_ref.9, f32[128,64]{1,0:T(8,128)S(1)} %shard_map.103.w_ref, bf16[768,128]{1,0:T(8,128)(2,1)S(1)} %pad_maximum_fusion.2.keys_ref.refs_0_, ...), custom_call_target="tpu_custom_call" | custom-call | flops 4294967296 | bytes 4194304 | tf_op jit(solution)/shard_map/pallas_call | solution.py:404
  48.2 0.5 collective-permute-start.16
  48.8 0.9 %collective-permute-done.15.refs_0_ = bf16[192,640]{1,0:T(8,128)(2,1)S(1)} collective-permute-done((bf16[192,640]{1,0:T(8,128)(2,1)S(1)}, bf16[192,640]{1,0:T(8,128)(2,1)S(1)}, u32[]{:S(2)}, u32[]{:S(2)}) %collective-permute-start.15) | collective-permute-done | bytes 245792 | tf_op jit(solution)/shard_map/ppermute | solution.py:290
  49.7 0.4 collective-permute-done.16.refs_1_
  50.0 0.4 collective-permute-done.18.refs_3_
  50.4 1.3 %copy-done.3 = bf16[14,64,640]{2,1,0:T(8,128)(2,1)S(1)} copy-done((bf16[14,64,640]{2,1,0:T(8,128)(2,1)S(1)}, bf16[14,64,640]{2,1,0:T(8,128)(2,1)}, u32[]{:S(2)}) %copy-start.3) | copy-done | bytes 1146904
  51.7 23.4 %shard_map.109 = bf16[128,32768]{1,0:T(8,128)(2,1)} custom-call(s32[1]{0:T(128)} %bitcast.own_ref, s32[2,12]{1,0:T(2,128)S(1)} %copy-done.2, bf16[128,36864]{1,0:T(8,128)(2,1)} %q_ref.1, bf16[14,64,640]{2,1,0:T(8,128)(2,1)S(1)} %copy-done.3, bf16[192,640]{1,0:T(8,128)(2,1)S(1)} %collective-permute-done.15.refs_0_, ...), custom_call_target="tpu_custom_call" | custom-call | flops 14495514624 | bytes 16777216 | tf_op jit(solution)/shard_map/pallas_call | solution.py:439
  (28 shorter events, 0.6 us)
Async XLA Ops:
  1.4 6.6 %collective-permute-start = (bf16[192,128]{1,0:T(8,128)(2,1)S(1)}, bf16[192,128]{1,0:T(8,128)(2,1)S(1)}, u32[]{:S(2)}, u32[]{:S(2)}) collective-permute-start(bf16[192,128]{1,0:T(8,128)(2,1)S(1)} %pad_maximum_fusion.4), channel_id=1, source_target_pairs={{0,8},{1,9},{2,10},{3,11},{4,12},{5,13},{6,14},{7,15},{8,0},{9,1},... | collective-permute-start | bytes 147464 | tf_op jit(solution)/shard_map/ppermute | solution.py:290
  8.0 6.9 %collective-permute-start.1 = (bf16[384,128]{1,0:T(8,128)(2,1)S(1)}, bf16[384,128]{1,0:T(8,128)(2,1)S(1)}, u32[]{:S(2)}, u32[]{:S(2)}) collective-permute-start(bf16[384,128]{1,0:T(8,128)(2,1)S(1)} %pad_maximum_fusion.3), channel_id=1, source_target_pairs={{0,4},{1,5},{2,6},{3,7},{4,0},{5,1},{6,2},{7,3},{8,12},{9,13},{10,... | collective-permute-start | bytes 294920 | tf_op jit(solution)/shard_map/ppermute | solution.py:290
  9.5 15.8 %collective-permute-start.7 = (bf16[192,640]{1,0:T(8,128)(2,1)S(1)}, bf16[192,640]{1,0:T(8,128)(2,1)S(1)}, u32[]{:S(2)}, u32[]{:S(2)}) collective-permute-start(bf16[192,640]{1,0:T(8,128)(2,1)S(1)} %pad.4.refs_7_), channel_id=1, source_target_pairs={{0,8},{1,9},{2,10},{3,11},{4,12},{5,13},{6,14},{7,15},{8,0},{9,1},... | collective-permute-start | bytes 737288 | tf_op jit(solution)/shard_map/ppermute | solution.py:290
  12.5 1.6 %copy-start = (bf16[128,8192]{1,0:T(8,128)(2,1)S(1)}, bf16[128,8192]{1,0:T(8,128)(2,1)}, u32[]{:S(2)}) copy-start(bf16[128,8192]{1,0:T(8,128)(2,1)} %iq_ref.9) | copy-start | bytes 6291460
  14.1 0.8 %copy-start.1 = (f32[128,64]{0,1:T(8,128)S(1)}, f32[128,64]{0,1:T(8,128)}, u32[]{:S(2)}) copy-start(f32[128,64]{0,1:T(8,128)} %param.12) | copy-start | bytes 98308
  15.0 7.6 %collective-permute-start.2 = (bf16[768,128]{1,0:T(8,128)(2,1)S(1)}, bf16[768,128]{1,0:T(8,128)(2,1)S(1)}, u32[]{:S(2)}, u32[]{:S(2)}) collective-permute-start(bf16[768,128]{1,0:T(8,128)(2,1)S(1)} %pad_maximum_fusion.2.keys_ref.refs_0_), channel_id=1, source_target_pairs={{0,2},{1,3},{2,0},{3,1},{4,6},{5,7},{6,4},{7,5},{8,10},{9,11},{10,... | collective-permute-start | bytes 589832 | tf_op jit(solution)/shard_map/ppermute | solution.py:290
  16.6 9.0 %collective-permute-start.6 = (bf16[192,640]{1,0:T(8,128)(2,1)S(1)}, bf16[192,640]{1,0:T(8,128)(2,1)S(1)}, u32[]{:S(2)}, u32[]{:S(2)}) collective-permute-start(bf16[192,640]{1,0:T(8,128)(2,1)S(1)} %pad.4.refs_7_), channel_id=1, source_target_pairs={{0,4},{1,5},{2,6},{3,7},{4,0},{5,1},{6,2},{7,3},{8,12},{9,13},{10,... | collective-permute-start | bytes 737288 | tf_op jit(solution)/shard_map/ppermute | solution.py:290
  16.6 8.6 %collective-permute-start.5 = (bf16[192,640]{1,0:T(8,128)(2,1)S(1)}, bf16[192,640]{1,0:T(8,128)(2,1)S(1)}, u32[]{:S(2)}, u32[]{:S(2)}) collective-permute-start(bf16[192,640]{1,0:T(8,128)(2,1)S(1)} %pad.4.refs_7_), channel_id=1, source_target_pairs={{0,2},{1,3},{2,0},{3,1},{4,6},{5,7},{6,4},{7,5},{8,10},{9,11},{10,... | collective-permute-start | bytes 737288 | tf_op jit(solution)/shard_map/ppermute | solution.py:290
  19.6 5.7 %collective-permute-start.4 = (bf16[192,640]{1,0:T(8,128)(2,1)S(1)}, bf16[192,640]{1,0:T(8,128)(2,1)S(1)}, u32[]{:S(2)}, u32[]{:S(2)}) collective-permute-start(bf16[192,640]{1,0:T(8,128)(2,1)S(1)} %pad.4.refs_7_), channel_id=1, source_target_pairs={{0,1},{1,0},{2,3},{3,2},{4,5},{5,4},{6,7},{7,6},{8,9},{9,8},{10,11... | collective-permute-start | bytes 737288 | tf_op jit(solution)/shard_map/ppermute | solution.py:290
  22.6 5.5 %collective-permute-start.3 = (bf16[1536,128]{1,0:T(8,128)(2,1)S(1)}, bf16[1536,128]{1,0:T(8,128)(2,1)S(1)}, u32[]{:S(2)}, u32[]{:S(2)}) collective-permute-start(bf16[1536,128]{1,0:T(8,128)(2,1)S(1)} %pad_maximum_fusion), channel_id=1, source_target_pairs={{0,1},{1,0},{2,3},{3,2},{4,5},{5,4},{6,7},{7,6},{8,9},{9,8},{10,11... | collective-permute-start | bytes 1179656 | tf_op jit(solution)/shard_map/ppermute | solution.py:290
  25.6 9.5 %collective-permute-start.9 = (bf16[192,640]{1,0:T(8,128)(2,1)S(1)}, bf16[192,640]{1,0:T(8,128)(2,1)S(1)}, u32[]{:S(2)}, u32[]{:S(2)}) collective-permute-start(bf16[192,640]{1,0:T(8,128)(2,1)S(1)} %collective-permute-done.7.refs_13_), channel_id=1, source_target_pairs={{0,4},{1,5},{2,6},{3,7},{4,0},{5,1},{6,2},{7,3},{8,12},{9,13},{10,... | collective-permute-start | bytes 737288 | tf_op jit(solution)/shard_map/ppermute | solution.py:290
  26.1 8.9 %collective-permute-start.8 = (bf16[192,640]{1,0:T(8,128)(2,1)S(1)}, bf16[192,640]{1,0:T(8,128)(2,1)S(1)}, u32[]{:S(2)}, u32[]{:S(2)}) collective-permute-start(bf16[192,640]{1,0:T(8,128)(2,1)S(1)} %collective-permute-done.7.refs_13_), channel_id=1, source_target_pairs={{0,2},{1,3},{2,0},{3,1},{4,6},{5,7},{6,4},{7,5},{8,10},{9,11},{10,... | collective-permute-start | bytes 737288 | tf_op jit(solution)/shard_map/ppermute | solution.py:290
  27.2 8.8 %collective-permute-start.10 = (bf16[192,640]{1,0:T(8,128)(2,1)S(1)}, bf16[192,640]{1,0:T(8,128)(2,1)S(1)}, u32[]{:S(2)}, u32[]{:S(2)}) collective-permute-start(bf16[192,640]{1,0:T(8,128)(2,1)S(1)} %collective-permute-done.5.refs_9_), channel_id=1, source_target_pairs={{0,1},{1,0},{2,3},{3,2},{4,5},{5,4},{6,7},{7,6},{8,9},{9,8},{10,11... | collective-permute-start | bytes 737288 | tf_op jit(solution)/shard_map/ppermute | solution.py:290
  27.2 13.1 %collective-permute-start.11 = (bf16[192,640]{1,0:T(8,128)(2,1)S(1)}, bf16[192,640]{1,0:T(8,128)(2,1)S(1)}, u32[]{:S(2)}, u32[]{:S(2)}) collective-permute-start(bf16[192,640]{1,0:T(8,128)(2,1)S(1)} %collective-permute-done.6.refs_11_), channel_id=1, source_target_pairs={{0,2},{1,3},{2,0},{3,1},{4,6},{5,7},{6,4},{7,5},{8,10},{9,11},{10,... | collective-permute-start | bytes 737288 | tf_op jit(solution)/shard_map/ppermute | solution.py:290
  33.2 7.1 %copy-start.2 = (s32[2,12]{1,0:T(2,128)S(1)}, s32[2,12]{1,0:T(2,128)}, u32[]{:S(2)}) copy-start(s32[2,12]{1,0:T(2,128)} %pick_ref.3) | copy-start | bytes 292
  35.0 13.1 %collective-permute-start.17 = (bf16[192,640]{1,0:T(8,128)(2,1)S(1)}, bf16[192,640]{1,0:T(8,128)(2,1)S(1)}, u32[]{:S(2)}, u32[]{:S(2)}) collective-permute-start(bf16[192,640]{1,0:T(8,128)(2,1)S(1)} %collective-permute-done.9.refs_17_), channel_id=1, source_target_pairs={{0,2},{1,3},{2,0},{3,1},{4,6},{5,7},{6,4},{7,5},{8,10},{9,11},{10,... | collective-permute-start | bytes 737288 | tf_op jit(solution)/shard_map/ppermute | solution.py:290
  36.0 4.3 %collective-permute-start.14 = (bf16[192,640]{1,0:T(8,128)(2,1)S(1)}, bf16[192,640]{1,0:T(8,128)(2,1)S(1)}, u32[]{:S(2)}, u32[]{:S(2)}) collective-permute-start(bf16[192,640]{1,0:T(8,128)(2,1)S(1)} %collective-permute-done.9.refs_17_), channel_id=1, source_target_pairs={{0,1},{1,0},{2,3},{3,2},{4,5},{5,4},{6,7},{7,6},{8,9},{9,8},{10,11... | collective-permute-start | bytes 737288 | tf_op jit(solution)/shard_map/ppermute | solution.py:290
  36.0 4.3 %collective-permute-start.12 = (bf16[192,640]{1,0:T(8,128)(2,1)S(1)}, bf16[192,640]{1,0:T(8,128)(2,1)S(1)}, u32[]{:S(2)}, u32[]{:S(2)}) collective-permute-start(bf16[192,640]{1,0:T(8,128)(2,1)S(1)} %collective-permute-done.7.refs_13_), channel_id=1, source_target_pairs={{0,1},{1,0},{2,3},{3,2},{4,5},{5,4},{6,7},{7,6},{8,9},{9,8},{10,11... | collective-permute-start | bytes 737288 | tf_op jit(solution)/shard_map/ppermute | solution.py:290
  36.5 3.8 %collective-permute-start.13 = (bf16[192,640]{1,0:T(8,128)(2,1)S(1)}, bf16[192,640]{1,0:T(8,128)(2,1)S(1)}, u32[]{:S(2)}, u32[]{:S(2)}) collective-permute-start(bf16[192,640]{1,0:T(8,128)(2,1)S(1)} %collective-permute-done.8.refs_15_), channel_id=1, source_target_pairs={{0,1},{1,0},{2,3},{3,2},{4,5},{5,4},{6,7},{7,6},{8,9},{9,8},{10,11... | collective-permute-start | bytes 737288 | tf_op jit(solution)/shard_map/ppermute | solution.py:290
  48.1 1.6 %collective-permute-start.15 = (bf16[192,640]{1,0:T(8,128)(2,1)S(1)}, bf16[192,640]{1,0:T(8,128)(2,1)S(1)}, u32[]{:S(2)}, u32[]{:S(2)}) collective-permute-start(bf16[192,640]{1,0:T(8,128)(2,1)S(1)} %collective-permute-done.6.refs_11_), channel_id=1, source_target_pairs={{0,1},{1,0},{2,3},{3,2},{4,5},{5,4},{6,7},{7,6},{8,9},{9,8},{10,11... | collective-permute-start | bytes 737288 | tf_op jit(solution)/shard_map/ppermute | solution.py:290
  48.2 1.9 %collective-permute-start.16 = (bf16[192,640]{1,0:T(8,128)(2,1)S(1)}, bf16[192,640]{1,0:T(8,128)(2,1)S(1)}, u32[]{:S(2)}, u32[]{:S(2)}) collective-permute-start(bf16[192,640]{1,0:T(8,128)(2,1)S(1)} %collective-permute-done.11.refs_12_), channel_id=1, source_target_pairs={{0,1},{1,0},{2,3},{3,2},{4,5},{5,4},{6,7},{7,6},{8,9},{9,8},{10,11... | collective-permute-start | bytes 737288 | tf_op jit(solution)/shard_map/ppermute | solution.py:290
  48.7 1.7 %collective-permute-start.18 = (bf16[192,640]{1,0:T(8,128)(2,1)S(1)}, bf16[192,640]{1,0:T(8,128)(2,1)S(1)}, u32[]{:S(2)}, u32[]{:S(2)}) collective-permute-start(bf16[192,640]{1,0:T(8,128)(2,1)S(1)} %collective-permute-done.17.refs_2_), channel_id=1, source_target_pairs={{0,1},{1,0},{2,3},{3,2},{4,5},{5,4},{6,7},{7,6},{8,9},{9,8},{10,11... | collective-permute-start | bytes 737288 | tf_op jit(solution)/shard_map/ppermute | solution.py:290
  50.4 1.3 %copy-start.3 = (bf16[14,64,640]{2,1,0:T(8,128)(2,1)S(1)}, bf16[14,64,640]{2,1,0:T(8,128)(2,1)}, u32[]{:S(2)}) copy-start(bf16[14,64,640]{2,1,0:T(8,128)(2,1)} %get-tuple-element.75.cache) | copy-start | bytes 3440644

commit v8 on v6

--- a/solution.py
+++ b/solution.py
@@ -139,7 +139,7 @@
 
 def attention_kernel(devices, own_ref, pick_ref, q_ref, *refs):
     shards = refs[:devices]
-    out_ref, cache, raw, even_t, odd_t, need, sem = refs[devices:]
+    out_ref, cache, raw, even_t, odd_t, need = refs[devices:]
     block = pl.program_id(0)
     own = own_ref[0]
     picks = pick_ref.shape[1]
@@ -148,13 +148,6 @@
         window = pick - devices
         holder = jnp.where(window < 0, pick, window // 2)
         return holder ^ own, jnp.where(window < 0, 0, 1 + window % 2)
-
-    def fetch(rel, inner, slot):
-        return pltpu.make_async_copy(
-            shards[rel].at[pl.ds(pl.multiple_of(inner * BLK, BLK), BLK)],
-            cache.at[slot],
-            sem.at[slot],
-        )
 
     @pl.when((block == 0) & (pl.program_id(1) == 0))
     def _():
@@ -164,14 +157,11 @@
             for s in range(picks):
                 rel, inner = split(pick_ref[b, s])
                 need[rel] = inner
+        for rel in range(1, devices):
+            at = pl.multiple_of(need[rel] * BLK, BLK)
+            cache[rel] = shards[rel][pl.ds(at, BLK), :]
         for n in range(3):
-            fetch(0, n, 0 if n == 0 else devices - 1 + n).start()
-        for rel in range(1, devices):
-            fetch(rel, need[rel], rel).start()
-        for n in range(3):
-            fetch(0, n, 0 if n == 0 else devices - 1 + n).wait()
-        for rel in range(1, devices):
-            fetch(rel, need[rel], rel).wait()
+            cache[0 if n == 0 else devices - 1 + n] = shards[0][n * BLK : (n + 1) * BLK, :]
 
     @pl.when(pl.program_id(1) == 0)
     def _():
@@ -249,7 +239,6 @@
 
     smem = pl.BlockSpec(memory_space=pltpu.SMEM)
     vmem = pl.BlockSpec(memory_space=pltpu.VMEM)
-    hbm = pl.BlockSpec(memory_space=pltpu.HBM)
     params = pltpu.CompilerParams(vmem_limit_bytes=VMEM)
 
     def index_cost(keys):
@@ -285,16 +274,7 @@
     shards = {0: rows}
     line, key_line = [0], jnp.concatenate([prefix_index_keys, window_index_keys], 0)
     (key_line,) = lax.optimization_barrier((key_line,))
-    for bit in bits:
-        other = swap(key_line, bit)
-        if bit != low:
-            (other, held) = lax.optimization_barrier((other, rows))
-            shards[bit] = swap(held, bit)
-        key_line = jnp.concatenate([key_line, other], 0)
-        line = line + [rel ^ bit for rel in line]
-        if bit != low:
-            touch_on = key_line
-    (early_queries, early_weights) = after(touch_on, index_queries, index_weights.T)
+    (early_queries, early_weights) = after(rows, index_queries, index_weights.T)
     weights = pl.pallas_call(
         weights_kernel,
         out_shape=jax.ShapeDtypeStruct((tok, IH), jnp.float32),
@@ -302,6 +282,13 @@
         out_specs=vmem,
         compiler_params=params,
     )(early_queries, early_weights)
+    for bit in bits:
+        other = swap(key_line, bit)
+        if bit != low:
+            (other, held, weights) = lax.optimization_barrier((other, rows, weights))
+            shards[bit] = swap(held, bit)
+        key_line = jnp.concatenate([key_line, other], 0)
+        line = line + [rel ^ bit for rel in line]
     (held,) = after(key_line, rows)
     for bit in (low, 2):
         shards[bit] = swap(held, bit)
@@ -325,7 +312,7 @@
 
     side_done = index_window(key_side)
     side_done = settle(side_done, weights, [1, 2])
-    send(side_done, (low, 2), (low, 1), *[(bit, 2) for bit in high], *[(bit, 1) for bit in high])
+    send(side_done, *[(bit, 2) for bit in high], (low, 2), (2, 1))
     rest = []
     for n, bit in enumerate(high):
         for other in bits[n + 1 :]:
@@ -334,8 +321,8 @@
                 shards[rel ^ other] = swap(held, other)
                 rest.append(rel ^ other)
     far_done = index_window(key_far)
-    send(far_done, *[(rel, 2) for rel in rest], *[(rel, 1) for rel in rest], (2, 1))
-    held = settle(index_queries, far_done, [rel ^ 1 for rel in bits] + rest)
+    send(far_done, *[(rel, 2) for rel in rest], *[(rel, 1) for rel in bits])
+    held = settle(index_queries, far_done, rest + [3])
     places = [line, side, far]
     tiles = devices * BLK // TILE
     begun = pl.pallas_call(
@@ -347,8 +334,8 @@
         compiler_params=params,
         cost_estimate=index_cost(tiles // 2 * TILE),
     )(own, held, weights, key_line, key_side, key_far)
-    send(begun, (low | 2, 1), *[(bit | 2, 1) for bit in high])
-    held = settle(index_queries, begun, [rel ^ 1 for rel in rest] + [3] + [rel | 2 for rel in bits])
+    send(begun, *[(bit | 2, 1) for bit in bits], *[(rel, 1) for rel in rest])
+    held = settle(index_queries, begun, [rel ^ 1 for rel in bits] + [rel | 2 for rel in bits])
     prefix_index, window_index = pl.pallas_call(
         functools.partial(index_last_kernel, places, tiles // 2, tiles - tiles // 2),
         out_shape=(
@@ -382,7 +369,7 @@
             num_scalar_prefetch=2,
             grid=(per_device, H // 2 // PAIRS),
             in_specs=[pl.BlockSpec((BLK, PAIRS * 2 * ROW), lambda b, h, *_: (b, h))]
-            + [hbm] * devices,
+            + [vmem] * devices,
             out_specs=pl.BlockSpec((BLK, PAIRS * 2 * LAT), lambda b, h, *_: (b, h)),
             scratch_shapes=[
                 pltpu.VMEM((devices + 2, BLK, WIDE), jnp.bfloat16),
@@ -390,7 +377,6 @@
                 pltpu.VMEM((WIDE, count), jnp.bfloat16),
                 pltpu.VMEM((WIDE, count), jnp.bfloat16),
                 pltpu.SMEM((devices,), jnp.int32),
-                pltpu.SemaphoreType.DMA((devices + 2,)),
             ],
         ),
         out_shape=jax.ShapeDtypeStruct((tok, H * LAT), jnp.bfloat16),

time: 71.1 us -> 70.1 us (0.986)
  Pallas kernels: 40.3 us -> 38.4 us
  local copies, waits for them, and re-layouts: 2.68 us -> 4.27 us
  waiting for transfers between devices: 8.52 us -> 7.51 us
    pallas_call x1, Pallas kernels: 24.7 us -> 22.7 us  [body(): pl.pallas_call(functools.partial(attention_kernel, devices), grid_spec=pl...]
    unnamed x8 -> x10, local copies, waits for them, and re-layouts: 2.36 us -> 3.95 us
    ppermute x19, waiting for transfers between devices: 8.52 us -> 7.51 us  [swap(): return lax.ppermute(array, 'ctx', [(i, i ^ rel) for i in range(devices)])]
where the time goes in v8:
time: 70.1 us; the launch traced here: 69.8 us
  Pallas kernels  38.4 us (55%)
  starting transfers between devices  16.7 us (24%)
  waiting for transfers between devices  7.51 us (11%)
  local copies, waits for them, and re-layouts  4.27 us (6%)
  other arithmetic  2.11 us (3%)
  between operations  0.82 us (1%)
    pallas_call x1, Pallas kernels, body(): pl.pallas_call(functools.partial(attention_kernel, devices), grid_spec=pl...  22.7 us
    ppermute x19, starting transfers between devices, swap(): return lax.ppermute(array, 'ctx', [(i, i ^ rel) for i in range(devices)])  16.7 us
    pallas_call x3, Pallas kernels, index_window(): pl.pallas_call(functools.partial(index_window_kernel, count), out_shape=j...  9.8 us
    ppermute x19, waiting for transfers between devices, swap(): return lax.ppermute(array, 'ctx', [(i, i ^ rel) for i in range(devices)])  7.51 us
    unnamed x10, local copies, waits for them, and re-layouts  3.95 us
    pallas_call x1, Pallas kernels, body(): pl.pallas_call(functools.partial(index_last_kernel, places, tiles // 2, t...  3.37 us
    pallas_call x1, Pallas kernels, body(): pl.pallas_call(functools.partial(index_prefix_kernel, places, 0, tiles //...  2.43 us
  transfers between devices with their start and end apart: 19, of which 6 were waited for; matrix products, arithmetic and copies ran while one was open for 2% of the time, Pallas kernels for 22%

profile of v8, /device:TPU:0, one launch (start us, length us, event | category | flops | bytes accessed | tf_op | source)
XLA Modules:
  0.0 69.8 jit_solution(15122833329717842594)
XLA Ops:
  0.6 0.8 %pad_maximum_fusion.4 = bf16[192,128]{1,0:T(8,128)(2,1)S(1)} fusion(bf16[128,128]{1,0:T(8,128)(2,1)} %param.14, bf16[64,128]{1,0:T(8,128)(2,1)} %param.13), kind=kLoop, calls=%fused_computation.4 | loop fusion | flops 98304 | bytes 98304 | tf_op jit(solution)/shard_map/concatenate | solution.py:275
  1.4 4.0 %collective-permute-start = (bf16[192,128]{1,0:T(8,128)(2,1)S(1)}, bf16[192,128]{1,0:T(8,128)(2,1)S(1)}, u32[]{:S(2)}, u32[]{:S(2)}) collective-permute-start(bf16[192,128]{1,0:T(8,128)(2,1)S(1)} %pad_maximum_fusion.4), channel_id=1, source_target_pairs={{0,8},{1,9},{2,10},{3,11},{4,12},{5,13},{6,14},{7,15},{8,0},{9,1},... | collective-permute-start | bytes 147464 | tf_op jit(solution)/shard_map/ppermute | solution.py:238
  5.4 1.3 %pad_maximum_fusion.1 = bf16[3,36864]{1,0:T(4,128)(2,1)S(1)} fusion(bf16[2,36864]{1,0:T(2,128)(2,1)} %param.10, bf16[1,36864]{1,0:T(2,128)(2,1)} %param.9), kind=kLoop, calls=%fused_computation.1 | loop fusion | flops 442368 | bytes 442368 | tf_op jit(solution)/shard_map/concatenate | solution.py:272
  6.7 0.3 reshape.13
  7.1 1.6 %copy-done = bf16[128,8192]{1,0:T(8,128)(2,1)S(1)} copy-done((bf16[128,8192]{1,0:T(8,128)(2,1)S(1)}, bf16[128,8192]{1,0:T(8,128)(2,1)}, u32[]{:S(2)}) %copy-start) | copy-done | bytes 2097176
  8.7 0.8 %copy-done.3 = f32[128,64]{0,1:T(8,128)S(1)} copy-done((f32[128,64]{0,1:T(8,128)S(1)}, f32[128,64]{0,1:T(8,128)}, u32[]{:S(2)}) %copy-start.3) | copy-done | bytes 32792
  9.4 0.1 shard_map.103.w_ref
  9.5 1.6 %collective-permute-start.1 = (bf16[384,128]{1,0:T(8,128)(2,1)S(1)}, bf16[384,128]{1,0:T(8,128)(2,1)S(1)}, u32[]{:S(2)}, u32[]{:S(2)}) collective-permute-start(bf16[384,128]{1,0:T(8,128)(2,1)S(1)} %pad_maximum_fusion.3), channel_id=1, source_target_pairs={{0,4},{1,5},{2,6},{3,7},{4,0},{5,1},{6,2},{7,3},{8,12},{9,13},{10,... | collective-permute-start | bytes 294920 | tf_op jit(solution)/shard_map/ppermute | solution.py:238
  11.2 1.3 %collective-permute-start.6 = (bf16[192,640]{1,0:T(8,128)(2,1)S(1)}, bf16[192,640]{1,0:T(8,128)(2,1)S(1)}, u32[]{:S(2)}, u32[]{:S(2)}) collective-permute-start(bf16[192,640]{1,0:T(8,128)(2,1)S(1)} %pad.4.refs_0_), channel_id=1, source_target_pairs={{0,8},{1,9},{2,10},{3,11},{4,12},{5,13},{6,14},{7,15},{8,0},{9,1},... | collective-permute-start | bytes 737288 | tf_op jit(solution)/shard_map/ppermute | solution.py:238
  12.5 2.0 %collective-permute-done.1 = bf16[384,128]{1,0:T(8,128)(2,1)S(1)} collective-permute-done((bf16[384,128]{1,0:T(8,128)(2,1)S(1)}, bf16[384,128]{1,0:T(8,128)(2,1)S(1)}, u32[]{:S(2)}, u32[]{:S(2)}) %collective-permute-start.1) | collective-permute-done | bytes 98336 | tf_op jit(solution)/shard_map/ppermute | solution.py:238
  14.5 1.6 %collective-permute-start.2 = (bf16[768,128]{1,0:T(8,128)(2,1)S(1)}, bf16[768,128]{1,0:T(8,128)(2,1)S(1)}, u32[]{:S(2)}, u32[]{:S(2)}) collective-permute-start(bf16[768,128]{1,0:T(8,128)(2,1)S(1)} %pad_maximum_fusion.2.keys_ref.refs_0_), channel_id=1, source_target_pairs={{0,2},{1,3},{2,0},{3,1},{4,6},{5,7},{6,4},{7,5},{8,10},{9,11},{10,... | collective-permute-start | bytes 589832 | tf_op jit(solution)/shard_map/ppermute | solution.py:238
  16.1 2.4 %collective-permute-start.8 = (bf16[192,640]{1,0:T(8,128)(2,1)S(1)}, bf16[192,640]{1,0:T(8,128)(2,1)S(1)}, u32[]{:S(2)}, u32[]{:S(2)}) collective-permute-start(bf16[192,640]{1,0:T(8,128)(2,1)S(1)} %pad.4.refs_0_), channel_id=1, source_target_pairs={{0,4},{1,5},{2,6},{3,7},{4,0},{5,1},{6,2},{7,3},{8,12},{9,13},{10,... | collective-permute-start | bytes 737288 | tf_op jit(solution)/shard_map/ppermute | solution.py:238
  18.5 0.5 collective-permute-start.4
  19.0 1.6 %copy-done.1 = bf16[128,8192]{1,0:T(8,128)(2,1)S(1)} copy-done((bf16[128,8192]{1,0:T(8,128)(2,1)S(1)}, bf16[128,8192]{1,0:T(8,128)(2,1)}, u32[]{:S(2)}) %copy-start.1) | copy-done | bytes 2097176
  20.6 2.4 %shard_map.105.refs_3_ = f32[4,128,128]{2,1,0:T(8,128)S(1)} custom-call(bf16[128,8192]{1,0:T(8,128)(2,1)S(1)} %copy-done.1, f32[128,64]{1,0:T(8,128)S(1)} %shard_map.103.w_ref, bf16[768,128]{1,0:T(8,128)(2,1)S(1)} %pad_maximum_fusion.2.keys_ref.refs_0_), custom_call_target="tpu_custom_call" | custom-call | flops 4294967296 | bytes 4194304 | tf_op jit(solution)/shard_map/pallas_call | solution.py:253
  23.0 0.1 collective-permute-start.3
  23.1 0.5 collective-permute-start.5
  23.7 2.4 %shard_map.104.refs_4_ = f32[4,128,128]{2,1,0:T(8,128)S(1)} custom-call(bf16[128,8192]{1,0:T(8,128)(2,1)S(1)} %copy-done.1, f32[128,64]{1,0:T(8,128)S(1)} %shard_map.103.w_ref, bf16[768,128]{1,0:T(8,128)(2,1)S(1)} %collective-permute-done.2.keys_ref.refs_1_), custom_call_target="tpu_custom_call" | custom-call | flops 4294967296 | bytes 4194304 | tf_op jit(solution)/shard_map/pallas_call | solution.py:253
  26.2 0.5 collective-permute-done.8.refs_4_
  26.6 1.5 %collective-permute-start.12 = (bf16[192,640]{1,0:T(8,128)(2,1)S(1)}, bf16[192,640]{1,0:T(8,128)(2,1)S(1)}, u32[]{:S(2)}, u32[]{:S(2)}) collective-permute-start(bf16[192,640]{1,0:T(8,128)(2,1)S(1)} %collective-permute-done.6.refs_8_), channel_id=1, source_target_pairs={{0,2},{1,3},{2,0},{3,1},{4,6},{5,7},{6,4},{7,5},{8,10},{9,11},{10,... | collective-permute-start | bytes 737288 | tf_op jit(solution)/shard_map/ppermute | solution.py:238
  28.1 0.5 collective-permute-start.13
  28.7 5.0 %shard_map.106.refs_5_ = f32[8,128,128]{2,1,0:T(8,128)S(1)} custom-call(bf16[128,8192]{1,0:T(8,128)(2,1)S(1)} %copy-done.1, f32[128,64]{1,0:T(8,128)S(1)} %shard_map.103.w_ref, bf16[1536,128]{1,0:T(8,128)(2,1)S(1)} %collective-permute-done.5.keys_ref.refs_2_), custom_call_target="tpu_custom_call" | custom-call | flops 8589934592 | bytes 4194304 | tf_op jit(solution)/shard_map/pallas_call | solution.py:253
  33.7 0.5 collective-permute-done.7.refs_12_
  34.1 0.5 collective-permute-start.11
  34.6 1.5 %collective-permute-start.17 = (bf16[192,640]{1,0:T(8,128)(2,1)S(1)}, bf16[192,640]{1,0:T(8,128)(2,1)S(1)}, u32[]{:S(2)}, u32[]{:S(2)}) collective-permute-start(bf16[192,640]{1,0:T(8,128)(2,1)S(1)} %collective-permute-done.7.refs_12_), channel_id=1, source_target_pairs={{0,2},{1,3},{2,0},{3,1},{4,6},{5,7},{6,4},{7,5},{8,10},{9,11},{10,... | collective-permute-start | bytes 737288 | tf_op jit(solution)/shard_map/ppermute | solution.py:238
  36.2 2.4 %shard_map.107.refs_6_ = f32[128,512]{1,0:T(8,128)S(1)} custom-call(s32[1]{0:T(128)} %bitcast.own_ref, bf16[128,8192]{1,0:T(8,128)(2,1)S(1)} %copy-done.2, f32[128,64]{1,0:T(8,128)S(1)} %shard_map.103.w_ref, bf16[768,128]{1,0:T(8,128)(2,1)S(1)} %pad_maximum_fusion.2.keys_ref.refs_0_, bf16[768,128]{1,0:T(8,128)(2,1)S(1)} %collective-permute-done.2.keys_ref.refs_1_, ...), custom_call_target="tpu_custom_call" | custom-call | flops 4294967296 | bytes 4194304 | tf_op jit(solution)/shard_map/pallas_call | solution.py:328
  38.6 2.0 %collective-permute-done.13.refs_6_ = bf16[192,640]{1,0:T(8,128)(2,1)S(1)} collective-permute-done((bf16[192,640]{1,0:T(8,128)(2,1)S(1)}, bf16[192,640]{1,0:T(8,128)(2,1)S(1)}, u32[]{:S(2)}, u32[]{:S(2)}) %collective-permute-start.13) | collective-permute-done | bytes 245792 | tf_op jit(solution)/shard_map/ppermute | solution.py:238
  40.7 0.5 collective-permute-start.15
  41.2 3.4 %shard_map.108 = (f32[128,1024]{1,0:T(8,128)}, f32[128,2048]{1,0:T(8,128)}) custom-call(s32[1]{0:T(128)} %bitcast.own_ref, bf16[128,8192]{1,0:T(8,128)(2,1)S(1)} %copy-done.2, f32[128,64]{1,0:T(8,128)S(1)} %shard_map.103.w_ref, bf16[768,128]{1,0:T(8,128)(2,1)S(1)} %pad_maximum_fusion.2.keys_ref.refs_0_, ...), custom_call_target="tpu_custom_call" | custom-call | flops 4294967296 | bytes 4194304 | tf_op jit(solution)/shard_map/pallas_call | solution.py:339
  44.6 1.0 %collective-permute-done.17.refs_14_ = bf16[192,640]{1,0:T(8,128)(2,1)S(1)} collective-permute-done((bf16[192,640]{1,0:T(8,128)(2,1)S(1)}, bf16[192,640]{1,0:T(8,128)(2,1)S(1)}, u32[]{:S(2)}, u32[]{:S(2)}) %collective-permute-start.17) | collective-permute-done | bytes 245792 | tf_op jit(solution)/shard_map/ppermute | solution.py:238
  45.6 1.5 %collective-permute-done.18.refs_15_ = bf16[192,640]{1,0:T(8,128)(2,1)S(1)} collective-permute-done((bf16[192,640]{1,0:T(8,128)(2,1)S(1)}, bf16[192,640]{1,0:T(8,128)(2,1)S(1)}, u32[]{:S(2)}, u32[]{:S(2)}) %collective-permute-start.18) | collective-permute-done | bytes 245792 | tf_op jit(solution)/shard_map/ppermute | solution.py:238
  47.1 22.7 %shard_map.109 = bf16[128,32768]{1,0:T(8,128)(2,1)} custom-call(s32[1]{0:T(128)} %bitcast.own_ref, s32[2,12]{1,0:T(2,128)S(1)} %copy-done.4, bf16[128,36864]{1,0:T(8,128)(2,1)} %q_ref.1, bf16[192,640]{1,0:T(8,128)(2,1)S(1)} %pad.4.refs_0_, bf16[192,640]{1,0:T(8,128)(2,1)S(1)} %collective-permute-done.3.refs_1_, ...), custom_call_target="tpu_custom_call" | custom-call | flops 14495514624 | bytes 16777216 | tf_op jit(solution)/shard_map/pallas_call | solution.py:366
  (30 shorter events, 0.1 us)
Async XLA Ops:
  1.4 8.1 %collective-permute-start = (bf16[192,128]{1,0:T(8,128)(2,1)S(1)}, bf16[192,128]{1,0:T(8,128)(2,1)S(1)}, u32[]{:S(2)}, u32[]{:S(2)}) collective-permute-start(bf16[192,128]{1,0:T(8,128)(2,1)S(1)} %pad_maximum_fusion.4), channel_id=1, source_target_pairs={{0,8},{1,9},{2,10},{3,11},{4,12},{5,13},{6,14},{7,15},{8,0},{9,1},... | collective-permute-start | bytes 147464 | tf_op jit(solution)/shard_map/ppermute | solution.py:238
  7.1 1.6 %copy-start = (bf16[128,8192]{1,0:T(8,128)(2,1)S(1)}, bf16[128,8192]{1,0:T(8,128)(2,1)}, u32[]{:S(2)}) copy-start(bf16[128,8192]{1,0:T(8,128)(2,1)} %iq_ref.8) | copy-start | bytes 6291460
  8.7 0.8 %copy-start.3 = (f32[128,64]{0,1:T(8,128)S(1)}, f32[128,64]{0,1:T(8,128)}, u32[]{:S(2)}) copy-start(f32[128,64]{0,1:T(8,128)} %param.12) | copy-start | bytes 98308
  9.5 5.0 %collective-permute-start.1 = (bf16[384,128]{1,0:T(8,128)(2,1)S(1)}, bf16[384,128]{1,0:T(8,128)(2,1)S(1)}, u32[]{:S(2)}, u32[]{:S(2)}) collective-permute-start(bf16[384,128]{1,0:T(8,128)(2,1)S(1)} %pad_maximum_fusion.3), channel_id=1, source_target_pairs={{0,4},{1,5},{2,6},{3,7},{4,0},{5,1},{6,2},{7,3},{8,12},{9,13},{10,... | collective-permute-start | bytes 294920 | tf_op jit(solution)/shard_map/ppermute | solution.py:238
  11.2 15.0 %collective-permute-start.6 = (bf16[192,640]{1,0:T(8,128)(2,1)S(1)}, bf16[192,640]{1,0:T(8,128)(2,1)S(1)}, u32[]{:S(2)}, u32[]{:S(2)}) collective-permute-start(bf16[192,640]{1,0:T(8,128)(2,1)S(1)} %pad.4.refs_0_), channel_id=1, source_target_pairs={{0,8},{1,9},{2,10},{3,11},{4,12},{5,13},{6,14},{7,15},{8,0},{9,1},... | collective-permute-start | bytes 737288 | tf_op jit(solution)/shard_map/ppermute | solution.py:238
  14.5 8.6 %collective-permute-start.2 = (bf16[768,128]{1,0:T(8,128)(2,1)S(1)}, bf16[768,128]{1,0:T(8,128)(2,1)S(1)}, u32[]{:S(2)}, u32[]{:S(2)}) collective-permute-start(bf16[768,128]{1,0:T(8,128)(2,1)S(1)} %pad_maximum_fusion.2.keys_ref.refs_0_), channel_id=1, source_target_pairs={{0,2},{1,3},{2,0},{3,1},{4,6},{5,7},{6,4},{7,5},{8,10},{9,11},{10,... | collective-permute-start | bytes 589832 | tf_op jit(solution)/shard_map/ppermute | solution.py:238
  16.1 10.5 %collective-permute-start.8 = (bf16[192,640]{1,0:T(8,128)(2,1)S(1)}, bf16[192,640]{1,0:T(8,128)(2,1)S(1)}, u32[]{:S(2)}, u32[]{:S(2)}) collective-permute-start(bf16[192,640]{1,0:T(8,128)(2,1)S(1)} %pad.4.refs_0_), channel_id=1, source_target_pairs={{0,4},{1,5},{2,6},{3,7},{4,0},{5,1},{6,2},{7,3},{8,12},{9,13},{10,... | collective-permute-start | bytes 737288 | tf_op jit(solution)/shard_map/ppermute | solution.py:238
  18.5 7.6 %collective-permute-start.4 = (bf16[192,640]{1,0:T(8,128)(2,1)S(1)}, bf16[192,640]{1,0:T(8,128)(2,1)S(1)}, u32[]{:S(2)}, u32[]{:S(2)}) collective-permute-start(bf16[192,640]{1,0:T(8,128)(2,1)S(1)} %pad.4.refs_0_), channel_id=1, source_target_pairs={{0,2},{1,3},{2,0},{3,1},{4,6},{5,7},{6,4},{7,5},{8,10},{9,11},{10,... | collective-permute-start | bytes 737288 | tf_op jit(solution)/shard_map/ppermute | solution.py:238
  19.0 1.6 %copy-start.1 = (bf16[128,8192]{1,0:T(8,128)(2,1)S(1)}, bf16[128,8192]{1,0:T(8,128)(2,1)}, u32[]{:S(2)}) copy-start(bf16[128,8192]{1,0:T(8,128)(2,1)} %iq_ref.8) | copy-start | bytes 6291460
  23.0 3.1 %collective-permute-start.3 = (bf16[192,640]{1,0:T(8,128)(2,1)S(1)}, bf16[192,640]{1,0:T(8,128)(2,1)S(1)}, u32[]{:S(2)}, u32[]{:S(2)}) collective-permute-start(bf16[192,640]{1,0:T(8,128)(2,1)S(1)} %pad.4.refs_0_), channel_id=1, source_target_pairs={{0,1},{1,0},{2,3},{3,2},{4,5},{5,4},{6,7},{7,6},{8,9},{9,8},{10,11... | collective-permute-start | bytes 737288 | tf_op jit(solution)/shard_map/ppermute | solution.py:238
  23.1 5.5 %collective-permute-start.5 = (bf16[1536,128]{1,0:T(8,128)(2,1)S(1)}, bf16[1536,128]{1,0:T(8,128)(2,1)S(1)}, u32[]{:S(2)}, u32[]{:S(2)}) collective-permute-start(bf16[1536,128]{1,0:T(8,128)(2,1)S(1)} %pad_maximum_fusion), channel_id=1, source_target_pairs={{0,1},{1,0},{2,3},{3,2},{4,5},{5,4},{6,7},{7,6},{8,9},{9,8},{10,11... | collective-permute-start | bytes 1179656 | tf_op jit(solution)/shard_map/ppermute | solution.py:238
  26.1 10.0 %copy-start.2 = (bf16[128,8192]{1,0:T(8,128)(2,1)S(1)}, bf16[128,8192]{1,0:T(8,128)(2,1)}, u32[]{:S(2)}) copy-start(bf16[128,8192]{1,0:T(8,128)(2,1)} %iq_ref.8) | copy-start | bytes 6291460
  26.6 7.5 %collective-permute-start.7 = (bf16[192,640]{1,0:T(8,128)(2,1)S(1)}, bf16[192,640]{1,0:T(8,128)(2,1)S(1)}, u32[]{:S(2)}, u32[]{:S(2)}) collective-permute-start(bf16[192,640]{1,0:T(8,128)(2,1)S(1)} %collective-permute-done.6.refs_8_), channel_id=1, source_target_pairs={{0,4},{1,5},{2,6},{3,7},{4,0},{5,1},{6,2},{7,3},{8,12},{9,13},{10,... | collective-permute-start | bytes 737288 | tf_op jit(solution)/shard_map/ppermute | solution.py:238
  26.6 7.5 %collective-permute-start.9 = (bf16[192,640]{1,0:T(8,128)(2,1)S(1)}, bf16[192,640]{1,0:T(8,128)(2,1)S(1)}, u32[]{:S(2)}, u32[]{:S(2)}) collective-permute-start(bf16[192,640]{1,0:T(8,128)(2,1)S(1)} %collective-permute-done.4.refs_2_), channel_id=1, source_target_pairs={{0,1},{1,0},{2,3},{3,2},{4,5},{5,4},{6,7},{7,6},{8,9},{9,8},{10,11... | collective-permute-start | bytes 737288 | tf_op jit(solution)/shard_map/ppermute | solution.py:238
  26.6 12.0 %collective-permute-start.12 = (bf16[192,640]{1,0:T(8,128)(2,1)S(1)}, bf16[192,640]{1,0:T(8,128)(2,1)S(1)}, u32[]{:S(2)}, u32[]{:S(2)}) collective-permute-start(bf16[192,640]{1,0:T(8,128)(2,1)S(1)} %collective-permute-done.6.refs_8_), channel_id=1, source_target_pairs={{0,2},{1,3},{2,0},{3,1},{4,6},{5,7},{6,4},{7,5},{8,10},{9,11},{10,... | collective-permute-start | bytes 737288 | tf_op jit(solution)/shard_map/ppermute | solution.py:238
  28.1 12.5 %collective-permute-start.13 = (bf16[192,640]{1,0:T(8,128)(2,1)S(1)}, bf16[192,640]{1,0:T(8,128)(2,1)S(1)}, u32[]{:S(2)}, u32[]{:S(2)}) collective-permute-start(bf16[192,640]{1,0:T(8,128)(2,1)S(1)} %collective-permute-done.8.refs_4_), channel_id=1, source_target_pairs={{0,2},{1,3},{2,0},{3,1},{4,6},{5,7},{6,4},{7,5},{8,10},{9,11},{10,... | collective-permute-start | bytes 737288 | tf_op jit(solution)/shard_map/ppermute | solution.py:238
  34.1 7.0 %collective-permute-start.10 = (bf16[192,640]{1,0:T(8,128)(2,1)S(1)}, bf16[192,640]{1,0:T(8,128)(2,1)S(1)}, u32[]{:S(2)}, u32[]{:S(2)}) collective-permute-start(bf16[192,640]{1,0:T(8,128)(2,1)S(1)} %collective-permute-done.6.refs_8_), channel_id=1, source_target_pairs={{0,1},{1,0},{2,3},{3,2},{4,5},{5,4},{6,7},{7,6},{8,9},{9,8},{10,11... | collective-permute-start | bytes 737288 | tf_op jit(solution)/shard_map/ppermute | solution.py:238
  34.1 7.0 %collective-permute-start.11 = (bf16[192,640]{1,0:T(8,128)(2,1)S(1)}, bf16[192,640]{1,0:T(8,128)(2,1)S(1)}, u32[]{:S(2)}, u32[]{:S(2)}) collective-permute-start(bf16[192,640]{1,0:T(8,128)(2,1)S(1)} %collective-permute-done.8.refs_4_), channel_id=1, source_target_pairs={{0,1},{1,0},{2,3},{3,2},{4,5},{5,4},{6,7},{7,6},{8,9},{9,8},{10,11... | collective-permute-start | bytes 737288 | tf_op jit(solution)/shard_map/ppermute | solution.py:238
  34.6 10.9 %collective-permute-start.17 = (bf16[192,640]{1,0:T(8,128)(2,1)S(1)}, bf16[192,640]{1,0:T(8,128)(2,1)S(1)}, u32[]{:S(2)}, u32[]{:S(2)}) collective-permute-start(bf16[192,640]{1,0:T(8,128)(2,1)S(1)} %collective-permute-done.7.refs_12_), channel_id=1, source_target_pairs={{0,2},{1,3},{2,0},{3,1},{4,6},{5,7},{6,4},{7,5},{8,10},{9,11},{10,... | collective-permute-start | bytes 737288 | tf_op jit(solution)/shard_map/ppermute | solution.py:238
  38.6 8.5 %copy-start.4 = (s32[2,12]{1,0:T(2,128)S(1)}, s32[2,12]{1,0:T(2,128)}, u32[]{:S(2)}) copy-start(s32[2,12]{1,0:T(2,128)} %pick_ref.1) | copy-start | bytes 292
  40.7 4.9 %collective-permute-start.14 = (bf16[192,640]{1,0:T(8,128)(2,1)S(1)}, bf16[192,640]{1,0:T(8,128)(2,1)S(1)}, u32[]{:S(2)}, u32[]{:S(2)}) collective-permute-start(bf16[192,640]{1,0:T(8,128)(2,1)S(1)} %collective-permute-done.13.refs_6_), channel_id=1, source_target_pairs={{0,1},{1,0},{2,3},{3,2},{4,5},{5,4},{6,7},{7,6},{8,9},{9,8},{10,11... | collective-permute-start | bytes 737288 | tf_op jit(solution)/shard_map/ppermute | solution.py:238
  40.7 4.9 %collective-permute-start.15 = (bf16[192,640]{1,0:T(8,128)(2,1)S(1)}, bf16[192,640]{1,0:T(8,128)(2,1)S(1)}, u32[]{:S(2)}, u32[]{:S(2)}) collective-permute-start(bf16[192,640]{1,0:T(8,128)(2,1)S(1)} %collective-permute-done.12.refs_10_), channel_id=1, source_target_pairs={{0,1},{1,0},{2,3},{3,2},{4,5},{5,4},{6,7},{7,6},{8,9},{9,8},{10,11... | collective-permute-start | bytes 737288 | tf_op jit(solution)/shard_map/ppermute | solution.py:238
  41.2 4.4 %collective-permute-start.16 = (bf16[192,640]{1,0:T(8,128)(2,1)S(1)}, bf16[192,640]{1,0:T(8,128)(2,1)S(1)}, u32[]{:S(2)}, u32[]{:S(2)}) collective-permute-start(bf16[192,640]{1,0:T(8,128)(2,1)S(1)} %collective-permute-done.7.refs_12_), channel_id=1, source_target_pairs={{0,1},{1,0},{2,3},{3,2},{4,5},{5,4},{6,7},{7,6},{8,9},{9,8},{10,11... | collective-permute-start | bytes 737288 | tf_op jit(solution)/shard_map/ppermute | solution.py:238
  45.5 1.5 %collective-permute-start.18 = (bf16[192,640]{1,0:T(8,128)(2,1)S(1)}, bf16[192,640]{1,0:T(8,128)(2,1)S(1)}, u32[]{:S(2)}, u32[]{:S(2)}) collective-permute-start(bf16[192,640]{1,0:T(8,128)(2,1)S(1)} %collective-permute-done.17.refs_14_), channel_id=1, source_target_pairs={{0,1},{1,0},{2,3},{3,2},{4,5},{5,4},{6,7},{7,6},{8,9},{9,8},{10,11... | collective-permute-start | bytes 737288 | tf_op jit(solution)/shard_map/ppermute | solution.py:238

commit v9 on v8

--- a/solution.py
+++ b/solution.py
@@ -24,6 +24,7 @@
 LOW = -1.0e30
 EXP2_SCALE = 192.0**-0.5 * 1.4426950408889634
 VMEM = 48 * 2**20
+COPY_VMEM = 50 * 2**20
 
 
 def index_tile(iq_ref, weights, keys):
@@ -62,7 +63,15 @@
     )
 
 
-def weights_kernel(iq_ref, w_ref, out_ref):
+def weights_kernel(iq_hbm, w_hbm, iq_ref, out_ref, w_ref, sem):
+    copies = [
+        pltpu.make_async_copy(iq_hbm, iq_ref, sem.at[0]),
+        pltpu.make_async_copy(w_hbm, w_ref, sem.at[1]),
+    ]
+    for copy in copies:
+        copy.start()
+    for copy in copies[::-1]:
+        copy.wait()
     out_ref[...] = w_ref[...].T * IDX**-0.5
 
 
@@ -275,12 +284,16 @@
     line, key_line = [0], jnp.concatenate([prefix_index_keys, window_index_keys], 0)
     (key_line,) = lax.optimization_barrier((key_line,))
     (early_queries, early_weights) = after(rows, index_queries, index_weights.T)
-    weights = pl.pallas_call(
+    index_queries, weights = pl.pallas_call(
         weights_kernel,
-        out_shape=jax.ShapeDtypeStruct((tok, IH), jnp.float32),
-        in_specs=[vmem, vmem],
-        out_specs=vmem,
-        compiler_params=params,
+        out_shape=(
+            jax.ShapeDtypeStruct(index_queries.shape, index_queries.dtype),
+            jax.ShapeDtypeStruct((tok, IH), jnp.float32),
+        ),
+        in_specs=[pl.BlockSpec(memory_space=pl.ANY)] * 2,
+        out_specs=(vmem, vmem),
+        scratch_shapes=[pltpu.VMEM((IH, tok), jnp.float32), pltpu.SemaphoreType.DMA((2,))],
+        compiler_params=pltpu.CompilerParams(vmem_limit_bytes=COPY_VMEM),
     )(early_queries, early_weights)
     for bit in bits:
         other = swap(key_line, bit)
@@ -334,8 +347,8 @@
         compiler_params=params,
         cost_estimate=index_cost(tiles // 2 * TILE),
     )(own, held, weights, key_line, key_side, key_far)
-    send(begun, *[(bit | 2, 1) for bit in bits], *[(rel, 1) for rel in rest])
-    held = settle(index_queries, begun, [rel ^ 1 for rel in bits] + [rel | 2 for rel in bits])
+    send(begun, *[(bit | 2, 1) for bit in high], *[(rel, 1) for rel in rest])
+    held = settle(index_queries, begun, [rel ^ 1 for rel in bits] + [rel | 2 for rel in high])
     prefix_index, window_index = pl.pallas_call(
         functools.partial(index_last_kernel, places, tiles // 2, tiles - tiles // 2),
         out_shape=(
@@ -359,7 +372,7 @@
         far_done,
         begun,
     )
-    send(prefix_index, *[(rel | 2, 1) for rel in rest])
+    send(prefix_index, (low | 2, 1), *[(rel | 2, 1) for rel in rest])
     shards = [shards[rel] for rel in range(devices)]
 
     count = picks.shape[1] * BLK

time: 70.1 us -> 70.5 us (level)
  local copies, waits for them, and re-layouts: 4.27 us -> 1.08 us
  waiting for transfers between devices: 7.51 us -> 9.45 us
  Pallas kernels: 38.4 us -> 39.9 us
    unnamed x10 -> x4, local copies, waits for them, and re-layouts: 3.95 us -> 0.76 us
    ppermute x19, waiting for transfers between devices: 7.51 us -> 9.45 us  [swap(): return lax.ppermute(array, 'ctx', [(i, i ^ rel) for i in range(devices)])]
    pallas_call x1, Pallas kernels: 0.09 us -> 1.71 us  [body(): pl.pallas_call(weights_kernel, out_shape=(jax.ShapeDtypeStruct(index_quer...]
  transfers between devices with their start and end apart: 19 -> 19, of which waited for: 6 -> 7; matrix products, arithmetic and copies ran while one was open for 2% -> 2% of each run, Pallas kernels for 22% -> 25%
where the time goes in v9:
time: 70.5 us; the launch traced here: 70.1 us
  Pallas kernels  39.9 us (57%)
  starting transfers between devices  16.8 us (24%)
  waiting for transfers between devices  9.45 us (13%)
  other arithmetic  2.1 us (3%)
  local copies, waits for them, and re-layouts  1.08 us (2%)
  between operations  0.81 us (1%)
    pallas_call x1, Pallas kernels, body(): pl.pallas_call(functools.partial(attention_kernel, devices), grid_spec=pl...  22.7 us
    ppermute x19, starting transfers between devices, swap(): return lax.ppermute(array, 'ctx', [(i, i ^ rel) for i in range(devices)])  16.8 us
    pallas_call x3, Pallas kernels, index_window(): pl.pallas_call(functools.partial(index_window_kernel, count), out_shape=j...  9.81 us
    ppermute x19, waiting for transfers between devices, swap(): return lax.ppermute(array, 'ctx', [(i, i ^ rel) for i in range(devices)])  9.45 us
    pallas_call x1, Pallas kernels, body(): pl.pallas_call(functools.partial(index_last_kernel, places, tiles // 2, t...  3.33 us
    pallas_call x1, Pallas kernels, body(): pl.pallas_call(functools.partial(index_prefix_kernel, places, 0, tiles //...  2.4 us
    pallas_call x1, Pallas kernels, body(): pl.pallas_call(weights_kernel, out_shape=(jax.ShapeDtypeStruct(index_quer...  1.71 us
  transfers between devices with their start and end apart: 19, of which 7 were waited for; matrix products, arithmetic and copies ran while one was open for 2% of the time, Pallas kernels for 25%

profile of v9, /device:TPU:0, one launch (start us, length us, event | category | flops | bytes accessed | tf_op | source)
XLA Modules:
  0.0 70.1 jit_solution(9321732283173342387)
XLA Ops:
  0.6 0.8 %pad_maximum_fusion.4 = bf16[192,128]{1,0:T(8,128)(2,1)S(1)} fusion(bf16[128,128]{1,0:T(8,128)(2,1)} %param.14, bf16[64,128]{1,0:T(8,128)(2,1)} %param.13), kind=kLoop, calls=%fused_computation.4 | loop fusion | flops 98304 | bytes 98304 | tf_op jit(solution)/shard_map/concatenate | solution.py:284
  1.4 4.0 %collective-permute-start = (bf16[192,128]{1,0:T(8,128)(2,1)S(1)}, bf16[192,128]{1,0:T(8,128)(2,1)S(1)}, u32[]{:S(2)}, u32[]{:S(2)}) collective-permute-start(bf16[192,128]{1,0:T(8,128)(2,1)S(1)} %pad_maximum_fusion.4), channel_id=1, source_target_pairs={{0,8},{1,9},{2,10},{3,11},{4,12},{5,13},{6,14},{7,15},{8,0},{9,1},... | collective-permute-start | bytes 147464 | tf_op jit(solution)/shard_map/ppermute | solution.py:247
  5.4 1.3 %pad_maximum_fusion.1 = bf16[3,36864]{1,0:T(4,128)(2,1)S(1)} fusion(bf16[2,36864]{1,0:T(2,128)(2,1)} %param.10, bf16[1,36864]{1,0:T(2,128)(2,1)} %param.9), kind=kLoop, calls=%fused_computation.1 | loop fusion | flops 442368 | bytes 442368 | tf_op jit(solution)/shard_map/concatenate | solution.py:281
  6.7 0.3 reshape.13
  7.1 0.7 %copy-done = f32[128,64]{0,1:T(8,128)S(1)} copy-done((f32[128,64]{0,1:T(8,128)S(1)}, f32[128,64]{0,1:T(8,128)}, u32[]{:S(2)}) %copy-start) | copy-done | bytes 32792
  7.8 1.7 %shard_map.103 = (bf16[128,8192]{1,0:T(8,128)(2,1)S(1)}, f32[128,64]{1,0:T(8,128)S(1)}) custom-call(bf16[128,8192]{1,0:T(8,128)(2,1)} %iq_hbm, f32[64,128]{1,0:T(8,128)S(1)} %bitcast.2), custom_call_target="tpu_custom_call" | custom-call | tf_op jit(solution)/shard_map/pallas_call | solution.py:287
  9.6 1.6 %collective-permute-start.1 = (bf16[384,128]{1,0:T(8,128)(2,1)S(1)}, bf16[384,128]{1,0:T(8,128)(2,1)S(1)}, u32[]{:S(2)}, u32[]{:S(2)}) collective-permute-start(bf16[384,128]{1,0:T(8,128)(2,1)S(1)} %pad_maximum_fusion.3), channel_id=1, source_target_pairs={{0,4},{1,5},{2,6},{3,7},{4,0},{5,1},{6,2},{7,3},{8,12},{9,13},{10,... | collective-permute-start | bytes 294920 | tf_op jit(solution)/shard_map/ppermute | solution.py:247
  11.2 1.3 %collective-permute-start.6 = (bf16[192,640]{1,0:T(8,128)(2,1)S(1)}, bf16[192,640]{1,0:T(8,128)(2,1)S(1)}, u32[]{:S(2)}, u32[]{:S(2)}) collective-permute-start(bf16[192,640]{1,0:T(8,128)(2,1)S(1)} %pad.4.refs_0_), channel_id=1, source_target_pairs={{0,8},{1,9},{2,10},{3,11},{4,12},{5,13},{6,14},{7,15},{8,0},{9,1},... | collective-permute-start | bytes 737288 | tf_op jit(solution)/shard_map/ppermute | solution.py:247
  12.5 2.0 %collective-permute-done.1 = bf16[384,128]{1,0:T(8,128)(2,1)S(1)} collective-permute-done((bf16[384,128]{1,0:T(8,128)(2,1)S(1)}, bf16[384,128]{1,0:T(8,128)(2,1)S(1)}, u32[]{:S(2)}, u32[]{:S(2)}) %collective-permute-start.1) | collective-permute-done | bytes 98336 | tf_op jit(solution)/shard_map/ppermute | solution.py:247
  14.5 1.6 %collective-permute-start.2 = (bf16[768,128]{1,0:T(8,128)(2,1)S(1)}, bf16[768,128]{1,0:T(8,128)(2,1)S(1)}, u32[]{:S(2)}, u32[]{:S(2)}) collective-permute-start(bf16[768,128]{1,0:T(8,128)(2,1)S(1)} %pad_maximum_fusion.2.keys_ref.refs_0_), channel_id=1, source_target_pairs={{0,2},{1,3},{2,0},{3,1},{4,6},{5,7},{6,4},{7,5},{8,10},{9,11},{10,... | collective-permute-start | bytes 589832 | tf_op jit(solution)/shard_map/ppermute | solution.py:247
  16.1 2.4 %collective-permute-start.8 = (bf16[192,640]{1,0:T(8,128)(2,1)S(1)}, bf16[192,640]{1,0:T(8,128)(2,1)S(1)}, u32[]{:S(2)}, u32[]{:S(2)}) collective-permute-start(bf16[192,640]{1,0:T(8,128)(2,1)S(1)} %pad.4.refs_0_), channel_id=1, source_target_pairs={{0,4},{1,5},{2,6},{3,7},{4,0},{5,1},{6,2},{7,3},{8,12},{9,13},{10,... | collective-permute-start | bytes 737288 | tf_op jit(solution)/shard_map/ppermute | solution.py:247
  18.5 0.5 collective-permute-start.4
  19.0 2.4 %shard_map.105.refs_3_ = f32[4,128,128]{2,1,0:T(8,128)S(1)} custom-call(bf16[128,8192]{1,0:T(8,128)(2,1)S(1)} %get-tuple-element.56.iq_ref, f32[128,64]{1,0:T(8,128)S(1)} %get-tuple-element.39.w_ref, bf16[768,128]{1,0:T(8,128)(2,1)S(1)} %pad_maximum_fusion.2.keys_ref.refs_0_), custom_call_target="tpu_custom_call" | custom-call | flops 4294967296 | bytes 4194304 | tf_op jit(solution)/shard_map/pallas_call | solution.py:262
  21.4 0.1 collective-permute-start.3
  21.5 0.9 %collective-permute-done.2.keys_ref.refs_1_ = bf16[768,128]{1,0:T(8,128)(2,1)S(1)} collective-permute-done((bf16[768,128]{1,0:T(8,128)(2,1)S(1)}, bf16[768,128]{1,0:T(8,128)(2,1)S(1)}, u32[]{:S(2)}, u32[]{:S(2)}) %collective-permute-start.2) | collective-permute-done | bytes 196640 | tf_op jit(solution)/shard_map/ppermute | solution.py:247
  22.4 0.1 collective-permute-start.5
  22.5 2.4 %shard_map.104.refs_4_ = f32[4,128,128]{2,1,0:T(8,128)S(1)} custom-call(bf16[128,8192]{1,0:T(8,128)(2,1)S(1)} %get-tuple-element.56.iq_ref, f32[128,64]{1,0:T(8,128)S(1)} %get-tuple-element.39.w_ref, bf16[768,128]{1,0:T(8,128)(2,1)S(1)} %collective-permute-done.2.keys_ref.refs_1_), custom_call_target="tpu_custom_call" | custom-call | flops 4294967296 | bytes 4194304 | tf_op jit(solution)/shard_map/pallas_call | solution.py:262
  24.9 0.3 collective-permute-done.4.refs_2_
  25.3 1.4 %collective-permute-done.8.refs_4_ = bf16[192,640]{1,0:T(8,128)(2,1)S(1)} collective-permute-done((bf16[192,640]{1,0:T(8,128)(2,1)S(1)}, bf16[192,640]{1,0:T(8,128)(2,1)S(1)}, u32[]{:S(2)}, u32[]{:S(2)}) %collective-permute-start.8) | collective-permute-done | bytes 245792 | tf_op jit(solution)/shard_map/ppermute | solution.py:247
  26.7 1.5 %collective-permute-start.12 = (bf16[192,640]{1,0:T(8,128)(2,1)S(1)}, bf16[192,640]{1,0:T(8,128)(2,1)S(1)}, u32[]{:S(2)}, u32[]{:S(2)}) collective-permute-start(bf16[192,640]{1,0:T(8,128)(2,1)S(1)} %collective-permute-done.6.refs_8_), channel_id=1, source_target_pairs={{0,2},{1,3},{2,0},{3,1},{4,6},{5,7},{6,4},{7,5},{8,10},{9,11},{10,... | collective-permute-start | bytes 737288 | tf_op jit(solution)/shard_map/ppermute | solution.py:247
  28.2 0.5 collective-permute-start.13
  28.7 5.0 %shard_map.106.refs_5_ = f32[8,128,128]{2,1,0:T(8,128)S(1)} custom-call(bf16[128,8192]{1,0:T(8,128)(2,1)S(1)} %get-tuple-element.56.iq_ref, f32[128,64]{1,0:T(8,128)S(1)} %get-tuple-element.39.w_ref, bf16[1536,128]{1,0:T(8,128)(2,1)S(1)} %collective-permute-done.5.keys_ref.refs_2_), custom_call_target="tpu_custom_call" | custom-call | flops 8589934592 | bytes 4194304 | tf_op jit(solution)/shard_map/pallas_call | solution.py:262
  33.8 0.5 collective-permute-start.11
  34.3 1.5 %collective-permute-start.14 = (bf16[192,640]{1,0:T(8,128)(2,1)S(1)}, bf16[192,640]{1,0:T(8,128)(2,1)S(1)}, u32[]{:S(2)}, u32[]{:S(2)}) collective-permute-start(bf16[192,640]{1,0:T(8,128)(2,1)S(1)} %collective-permute-done.7.refs_12_), channel_id=1, source_target_pairs={{0,2},{1,3},{2,0},{3,1},{4,6},{5,7},{6,4},{7,5},{8,10},{9,11},{10,... | collective-permute-start | bytes 737288 | tf_op jit(solution)/shard_map/ppermute | solution.py:247
  35.8 2.4 %shard_map.107.refs_6_ = f32[128,512]{1,0:T(8,128)S(1)} custom-call(s32[1]{0:T(128)} %bitcast.own_ref, bf16[128,8192]{1,0:T(8,128)(2,1)S(1)} %get-tuple-element.56.iq_ref, f32[128,64]{1,0:T(8,128)S(1)} %get-tuple-element.39.w_ref, bf16[768,128]{1,0:T(8,128)(2,1)S(1)} %pad_maximum_fusion.2.keys_ref.refs_0_, ...), custom_call_target="tpu_custom_call" | custom-call | flops 4294967296 | bytes 4194304 | tf_op jit(solution)/shard_map/pallas_call | solution.py:341
  38.3 0.5 collective-permute-start.17
  38.8 3.3 %shard_map.108 = (f32[128,1024]{1,0:T(8,128)}, f32[128,2048]{1,0:T(8,128)}) custom-call(s32[1]{0:T(128)} %bitcast.own_ref, bf16[128,8192]{1,0:T(8,128)(2,1)S(1)} %get-tuple-element.56.iq_ref, f32[128,64]{1,0:T(8,128)S(1)} %get-tuple-element.39.w_ref, bf16[768,128]{1,0:T(8,128)(2,1)S(1)} %pad_maximum_fusion.2.keys_ref.refs_0_, ...), custom_call_target="tpu_custom_call" | custom-call | flops 4294967296 | bytes 4194304 | tf_op jit(solution)/shard_map/pallas_call | solution.py:352
  42.1 3.4 %collective-permute-done.14.refs_14_ = bf16[192,640]{1,0:T(8,128)(2,1)S(1)} collective-permute-done((bf16[192,640]{1,0:T(8,128)(2,1)S(1)}, bf16[192,640]{1,0:T(8,128)(2,1)S(1)}, u32[]{:S(2)}, u32[]{:S(2)}) %collective-permute-start.14) | collective-permute-done | bytes 245792 | tf_op jit(solution)/shard_map/ppermute | solution.py:247
  45.6 0.5 collective-permute-start.18
  46.1 1.0 %collective-permute-done.15.refs_7_ = bf16[192,640]{1,0:T(8,128)(2,1)S(1)} collective-permute-done((bf16[192,640]{1,0:T(8,128)(2,1)S(1)}, bf16[192,640]{1,0:T(8,128)(2,1)S(1)}, u32[]{:S(2)}, u32[]{:S(2)}) %collective-permute-start.15) | collective-permute-done | bytes 245792 | tf_op jit(solution)/shard_map/ppermute | solution.py:247
  47.1 0.4 collective-permute-done.18.refs_15_
  47.4 22.7 %shard_map.109 = bf16[128,32768]{1,0:T(8,128)(2,1)} custom-call(s32[1]{0:T(128)} %bitcast.own_ref, s32[2,12]{1,0:T(2,128)S(1)} %copy-done.1, bf16[128,36864]{1,0:T(8,128)(2,1)} %q_ref.1, bf16[192,640]{1,0:T(8,128)(2,1)S(1)} %pad.4.refs_0_, bf16[192,640]{1,0:T(8,128)(2,1)S(1)} %collective-permute-done.3.refs_1_, ...), custom_call_target="tpu_custom_call" | custom-call | flops 14495514624 | bytes 16777216 | tf_op jit(solution)/shard_map/pallas_call | solution.py:379
  (24 shorter events, 0.3 us)
Async XLA Ops:
  1.4 8.1 %collective-permute-start = (bf16[192,128]{1,0:T(8,128)(2,1)S(1)}, bf16[192,128]{1,0:T(8,128)(2,1)S(1)}, u32[]{:S(2)}, u32[]{:S(2)}) collective-permute-start(bf16[192,128]{1,0:T(8,128)(2,1)S(1)} %pad_maximum_fusion.4), channel_id=1, source_target_pairs={{0,8},{1,9},{2,10},{3,11},{4,12},{5,13},{6,14},{7,15},{8,0},{9,1},... | collective-permute-start | bytes 147464 | tf_op jit(solution)/shard_map/ppermute | solution.py:247
  7.1 0.8 %copy-start = (f32[128,64]{0,1:T(8,128)S(1)}, f32[128,64]{0,1:T(8,128)}, u32[]{:S(2)}) copy-start(f32[128,64]{0,1:T(8,128)} %param.12) | copy-start | bytes 98308
  9.6 5.0 %collective-permute-start.1 = (bf16[384,128]{1,0:T(8,128)(2,1)S(1)}, bf16[384,128]{1,0:T(8,128)(2,1)S(1)}, u32[]{:S(2)}, u32[]{:S(2)}) collective-permute-start(bf16[384,128]{1,0:T(8,128)(2,1)S(1)} %pad_maximum_fusion.3), channel_id=1, source_target_pairs={{0,4},{1,5},{2,6},{3,7},{4,0},{5,1},{6,2},{7,3},{8,12},{9,13},{10,... | collective-permute-start | bytes 294920 | tf_op jit(solution)/shard_map/ppermute | solution.py:247
  11.2 14.0 %collective-permute-start.6 = (bf16[192,640]{1,0:T(8,128)(2,1)S(1)}, bf16[192,640]{1,0:T(8,128)(2,1)S(1)}, u32[]{:S(2)}, u32[]{:S(2)}) collective-permute-start(bf16[192,640]{1,0:T(8,128)(2,1)S(1)} %pad.4.refs_0_), channel_id=1, source_target_pairs={{0,8},{1,9},{2,10},{3,11},{4,12},{5,13},{6,14},{7,15},{8,0},{9,1},... | collective-permute-start | bytes 737288 | tf_op jit(solution)/shard_map/ppermute | solution.py:247
  14.5 7.8 %collective-permute-start.2 = (bf16[768,128]{1,0:T(8,128)(2,1)S(1)}, bf16[768,128]{1,0:T(8,128)(2,1)S(1)}, u32[]{:S(2)}, u32[]{:S(2)}) collective-permute-start(bf16[768,128]{1,0:T(8,128)(2,1)S(1)} %pad_maximum_fusion.2.keys_ref.refs_0_), channel_id=1, source_target_pairs={{0,2},{1,3},{2,0},{3,1},{4,6},{5,7},{6,4},{7,5},{8,10},{9,11},{10,... | collective-permute-start | bytes 589832 | tf_op jit(solution)/shard_map/ppermute | solution.py:247
  16.1 10.5 %collective-permute-start.8 = (bf16[192,640]{1,0:T(8,128)(2,1)S(1)}, bf16[192,640]{1,0:T(8,128)(2,1)S(1)}, u32[]{:S(2)}, u32[]{:S(2)}) collective-permute-start(bf16[192,640]{1,0:T(8,128)(2,1)S(1)} %pad.4.refs_0_), channel_id=1, source_target_pairs={{0,4},{1,5},{2,6},{3,7},{4,0},{5,1},{6,2},{7,3},{8,12},{9,13},{10,... | collective-permute-start | bytes 737288 | tf_op jit(solution)/shard_map/ppermute | solution.py:247
  18.5 6.7 %collective-permute-start.4 = (bf16[192,640]{1,0:T(8,128)(2,1)S(1)}, bf16[192,640]{1,0:T(8,128)(2,1)S(1)}, u32[]{:S(2)}, u32[]{:S(2)}) collective-permute-start(bf16[192,640]{1,0:T(8,128)(2,1)S(1)} %pad.4.refs_0_), channel_id=1, source_target_pairs={{0,2},{1,3},{2,0},{3,1},{4,6},{5,7},{6,4},{7,5},{8,10},{9,11},{10,... | collective-permute-start | bytes 737288 | tf_op jit(solution)/shard_map/ppermute | solution.py:247
  21.4 3.8 %collective-permute-start.3 = (bf16[192,640]{1,0:T(8,128)(2,1)S(1)}, bf16[192,640]{1,0:T(8,128)(2,1)S(1)}, u32[]{:S(2)}, u32[]{:S(2)}) collective-permute-start(bf16[192,640]{1,0:T(8,128)(2,1)S(1)} %pad.4.refs_0_), channel_id=1, source_target_pairs={{0,1},{1,0},{2,3},{3,2},{4,5},{5,4},{6,7},{7,6},{8,9},{9,8},{10,11... | collective-permute-start | bytes 737288 | tf_op jit(solution)/shard_map/ppermute | solution.py:247
  22.4 6.3 %collective-permute-start.5 = (bf16[1536,128]{1,0:T(8,128)(2,1)S(1)}, bf16[1536,128]{1,0:T(8,128)(2,1)S(1)}, u32[]{:S(2)}, u32[]{:S(2)}) collective-permute-start(bf16[1536,128]{1,0:T(8,128)(2,1)S(1)} %pad_maximum_fusion), channel_id=1, source_target_pairs={{0,1},{1,0},{2,3},{3,2},{4,5},{5,4},{6,7},{7,6},{8,9},{9,8},{10,11... | collective-permute-start | bytes 1179656 | tf_op jit(solution)/shard_map/ppermute | solution.py:247
  26.7 7.1 %collective-permute-start.7 = (bf16[192,640]{1,0:T(8,128)(2,1)S(1)}, bf16[192,640]{1,0:T(8,128)(2,1)S(1)}, u32[]{:S(2)}, u32[]{:S(2)}) collective-permute-start(bf16[192,640]{1,0:T(8,128)(2,1)S(1)} %collective-permute-done.6.refs_8_), channel_id=1, source_target_pairs={{0,4},{1,5},{2,6},{3,7},{4,0},{5,1},{6,2},{7,3},{8,12},{9,13},{10,... | collective-permute-start | bytes 737288 | tf_op jit(solution)/shard_map/ppermute | solution.py:247
  26.7 7.1 %collective-permute-start.9 = (bf16[192,640]{1,0:T(8,128)(2,1)S(1)}, bf16[192,640]{1,0:T(8,128)(2,1)S(1)}, u32[]{:S(2)}, u32[]{:S(2)}) collective-permute-start(bf16[192,640]{1,0:T(8,128)(2,1)S(1)} %collective-permute-done.4.refs_2_), channel_id=1, source_target_pairs={{0,1},{1,0},{2,3},{3,2},{4,5},{5,4},{6,7},{7,6},{8,9},{9,8},{10,11... | collective-permute-start | bytes 737288 | tf_op jit(solution)/shard_map/ppermute | solution.py:247
  26.7 11.5 %collective-permute-start.12 = (bf16[192,640]{1,0:T(8,128)(2,1)S(1)}, bf16[192,640]{1,0:T(8,128)(2,1)S(1)}, u32[]{:S(2)}, u32[]{:S(2)}) collective-permute-start(bf16[192,640]{1,0:T(8,128)(2,1)S(1)} %collective-permute-done.6.refs_8_), channel_id=1, source_target_pairs={{0,2},{1,3},{2,0},{3,1},{4,6},{5,7},{6,4},{7,5},{8,10},{9,11},{10,... | collective-permute-start | bytes 737288 | tf_op jit(solution)/shard_map/ppermute | solution.py:247
  28.2 14.0 %collective-permute-start.13 = (bf16[192,640]{1,0:T(8,128)(2,1)S(1)}, bf16[192,640]{1,0:T(8,128)(2,1)S(1)}, u32[]{:S(2)}, u32[]{:S(2)}) collective-permute-start(bf16[192,640]{1,0:T(8,128)(2,1)S(1)} %collective-permute-done.8.refs_4_), channel_id=1, source_target_pairs={{0,2},{1,3},{2,0},{3,1},{4,6},{5,7},{6,4},{7,5},{8,10},{9,11},{10,... | collective-permute-start | bytes 737288 | tf_op jit(solution)/shard_map/ppermute | solution.py:247
  33.7 4.6 %collective-permute-start.10 = (bf16[192,640]{1,0:T(8,128)(2,1)S(1)}, bf16[192,640]{1,0:T(8,128)(2,1)S(1)}, u32[]{:S(2)}, u32[]{:S(2)}) collective-permute-start(bf16[192,640]{1,0:T(8,128)(2,1)S(1)} %collective-permute-done.6.refs_8_), channel_id=1, source_target_pairs={{0,1},{1,0},{2,3},{3,2},{4,5},{5,4},{6,7},{7,6},{8,9},{9,8},{10,11... | collective-permute-start | bytes 737288 | tf_op jit(solution)/shard_map/ppermute | solution.py:247
  33.8 5.0 %collective-permute-start.11 = (bf16[192,640]{1,0:T(8,128)(2,1)S(1)}, bf16[192,640]{1,0:T(8,128)(2,1)S(1)}, u32[]{:S(2)}, u32[]{:S(2)}) collective-permute-start(bf16[192,640]{1,0:T(8,128)(2,1)S(1)} %collective-permute-done.8.refs_4_), channel_id=1, source_target_pairs={{0,1},{1,0},{2,3},{3,2},{4,5},{5,4},{6,7},{7,6},{8,9},{9,8},{10,11... | collective-permute-start | bytes 737288 | tf_op jit(solution)/shard_map/ppermute | solution.py:247
  34.3 11.3 %collective-permute-start.14 = (bf16[192,640]{1,0:T(8,128)(2,1)S(1)}, bf16[192,640]{1,0:T(8,128)(2,1)S(1)}, u32[]{:S(2)}, u32[]{:S(2)}) collective-permute-start(bf16[192,640]{1,0:T(8,128)(2,1)S(1)} %collective-permute-done.7.refs_12_), channel_id=1, source_target_pairs={{0,2},{1,3},{2,0},{3,1},{4,6},{5,7},{6,4},{7,5},{8,10},{9,11},{10,... | collective-permute-start | bytes 737288 | tf_op jit(solution)/shard_map/ppermute | solution.py:247
  38.2 9.2 %copy-start.1 = (s32[2,12]{1,0:T(2,128)S(1)}, s32[2,12]{1,0:T(2,128)}, u32[]{:S(2)}) copy-start(s32[2,12]{1,0:T(2,128)} %pick_ref.1) | copy-start | bytes 292
  38.2 7.9 %collective-permute-start.16 = (bf16[192,640]{1,0:T(8,128)(2,1)S(1)}, bf16[192,640]{1,0:T(8,128)(2,1)S(1)}, u32[]{:S(2)}, u32[]{:S(2)}) collective-permute-start(bf16[192,640]{1,0:T(8,128)(2,1)S(1)} %collective-permute-done.12.refs_10_), channel_id=1, source_target_pairs={{0,1},{1,0},{2,3},{3,2},{4,5},{5,4},{6,7},{7,6},{8,9},{9,8},{10,11... | collective-permute-start | bytes 737288 | tf_op jit(solution)/shard_map/ppermute | solution.py:247
  38.3 7.8 %collective-permute-start.17 = (bf16[192,640]{1,0:T(8,128)(2,1)S(1)}, bf16[192,640]{1,0:T(8,128)(2,1)S(1)}, u32[]{:S(2)}, u32[]{:S(2)}) collective-permute-start(bf16[192,640]{1,0:T(8,128)(2,1)S(1)} %collective-permute-done.7.refs_12_), channel_id=1, source_target_pairs={{0,1},{1,0},{2,3},{3,2},{4,5},{5,4},{6,7},{7,6},{8,9},{9,8},{10,11... | collective-permute-start | bytes 737288 | tf_op jit(solution)/shard_map/ppermute | solution.py:247
  45.6 1.5 %collective-permute-start.15 = (bf16[192,640]{1,0:T(8,128)(2,1)S(1)}, bf16[192,640]{1,0:T(8,128)(2,1)S(1)}, u32[]{:S(2)}, u32[]{:S(2)}) collective-permute-start(bf16[192,640]{1,0:T(8,128)(2,1)S(1)} %collective-permute-done.13.refs_6_), channel_id=1, source_target_pairs={{0,1},{1,0},{2,3},{3,2},{4,5},{5,4},{6,7},{7,6},{8,9},{9,8},{10,11... | collective-permute-start | bytes 737288 | tf_op jit(solution)/shard_map/ppermute | solution.py:247
  45.6 1.9 %collective-permute-start.18 = (bf16[192,640]{1,0:T(8,128)(2,1)S(1)}, bf16[192,640]{1,0:T(8,128)(2,1)S(1)}, u32[]{:S(2)}, u32[]{:S(2)}) collective-permute-start(bf16[192,640]{1,0:T(8,128)(2,1)S(1)} %collective-permute-done.14.refs_14_), channel_id=1, source_target_pairs={{0,1},{1,0},{2,3},{3,2},{4,5},{5,4},{6,7},{7,6},{8,9},{9,8},{10,11... | collective-permute-start | bytes 737288 | tf_op jit(solution)/shard_map/ppermute | solution.py:247

commit v10 on v9

--- a/solution.py
+++ b/solution.py
@@ -299,12 +299,10 @@
         other = swap(key_line, bit)
         if bit != low:
             (other, held, weights) = lax.optimization_barrier((other, rows, weights))
-            shards[bit] = swap(held, bit)
+            for hop in [bit] if bit != high[-1] else [bit, 2, low]:
+                shards[hop] = swap(held, hop)
         key_line = jnp.concatenate([key_line, other], 0)
         line = line + [rel ^ bit for rel in line]
-    (held,) = after(key_line, rows)
-    for bit in (low, 2):
-        shards[bit] = swap(held, bit)
     key_side = swap(key_line, 2)
     side = [rel ^ 2 for rel in line]
     key_far = swap(jnp.concatenate([key_line, key_side], 0), 1)
@@ -317,7 +315,7 @@
             shards[rel ^ bit] = swap(held[rel], bit)
 
     line_done = index_window(key_line)
-    send(line_done, (0, 1))
+    send(line_done, (low, 2), (0, 1))
     def settle(array, done, rels):
         got = lax.optimization_barrier((array, done, *[shards[rel] for rel in rels]))
         shards.update(zip(rels, got[2:]))
@@ -325,7 +323,7 @@
 
     side_done = index_window(key_side)
     side_done = settle(side_done, weights, [1, 2])
-    send(side_done, *[(bit, 2) for bit in high], (low, 2), (2, 1))
+    send(side_done, *[(bit, 2) for bit in high], (2, 1))
     rest = []
     for n, bit in enumerate(high):
         for other in bits[n + 1 :]:
@@ -335,7 +333,7 @@
                 rest.append(rel ^ other)
     far_done = index_window(key_far)
     send(far_done, *[(rel, 2) for rel in rest], *[(rel, 1) for rel in bits])
-    held = settle(index_queries, far_done, rest + [3])
+    held = settle(index_queries, far_done, rest + [3, low | 2])
     places = [line, side, far]
     tiles = devices * BLK // TILE
     begun = pl.pallas_call(
@@ -347,7 +345,7 @@
         compiler_params=params,
         cost_estimate=index_cost(tiles // 2 * TILE),
     )(own, held, weights, key_line, key_side, key_far)
-    send(begun, *[(bit | 2, 1) for bit in high], *[(rel, 1) for rel in rest])
+    send(begun, *[(bit | 2, 1) for bit in bits], *[(rel, 1) for rel in rest])
     held = settle(index_queries, begun, [rel ^ 1 for rel in bits] + [rel | 2 for rel in high])
     prefix_index, window_index = pl.pallas_call(
         functools.partial(index_last_kernel, places, tiles // 2, tiles - tiles // 2),
@@ -372,7 +370,7 @@
         far_done,
         begun,
     )
-    send(prefix_index, (low | 2, 1), *[(rel | 2, 1) for rel in rest])
+    send(prefix_index, *[(rel | 2, 1) for rel in rest])
     shards = [shards[rel] for rel in range(devices)]
 
     count = picks.shape[1] * BLK

time: 70.5 us -> 70.3 us (level)
  transfers between devices with their start and end apart: 19 -> 19, of which waited for: 7 -> 5; matrix products, arithmetic and copies ran while one was open for 2% -> 2% of each run, Pallas kernels for 25% -> 25%
where the time goes in v10:
time: 70.3 us; the launch traced here: 70 us
  Pallas kernels  39.9 us (57%)
  starting transfers between devices  16.7 us (24%)
  waiting for transfers between devices  9.3 us (13%)
  other arithmetic  2.1 us (3%)
  local copies, waits for them, and re-layouts  1.08 us (2%)
  between operations  0.8 us (1%)
    pallas_call x1, Pallas kernels, body(): pl.pallas_call(functools.partial(attention_kernel, devices), grid_spec=pl...  22.7 us
    ppermute x19, starting transfers between devices, swap(): return lax.ppermute(array, 'ctx', [(i, i ^ rel) for i in range(devices)])  16.7 us
    pallas_call x3, Pallas kernels, index_window(): pl.pallas_call(functools.partial(index_window_kernel, count), out_shape=j...  9.81 us
    ppermute x19, waiting for transfers between devices, swap(): return lax.ppermute(array, 'ctx', [(i, i ^ rel) for i in range(devices)])  9.3 us
    pallas_call x1, Pallas kernels, body(): pl.pallas_call(functools.partial(index_last_kernel, places, tiles // 2, t...  3.32 us
    pallas_call x1, Pallas kernels, body(): pl.pallas_call(functools.partial(index_prefix_kernel, places, 0, tiles //...  2.4 us
    pallas_call x1, Pallas kernels, body(): pl.pallas_call(weights_kernel, out_shape=(jax.ShapeDtypeStruct(index_quer...  1.71 us
  transfers between devices with their start and end apart: 19, of which 5 were waited for; matrix products, arithmetic and copies ran while one was open for 2% of the time, Pallas kernels for 25%

profile of v10, /device:TPU:0, one launch (start us, length us, event | category | flops | bytes accessed | tf_op | source)
XLA Modules:
  0.0 70.0 jit_solution(11686384391185502952)
XLA Ops:
  0.6 0.8 %pad_maximum_fusion.4 = bf16[192,128]{1,0:T(8,128)(2,1)S(1)} fusion(bf16[128,128]{1,0:T(8,128)(2,1)} %param.14, bf16[64,128]{1,0:T(8,128)(2,1)} %param.13), kind=kLoop, calls=%fused_computation.4 | loop fusion | flops 98304 | bytes 98304 | tf_op jit(solution)/shard_map/concatenate | solution.py:284
  1.4 4.0 %collective-permute-start = (bf16[192,128]{1,0:T(8,128)(2,1)S(1)}, bf16[192,128]{1,0:T(8,128)(2,1)S(1)}, u32[]{:S(2)}, u32[]{:S(2)}) collective-permute-start(bf16[192,128]{1,0:T(8,128)(2,1)S(1)} %pad_maximum_fusion.4), channel_id=1, source_target_pairs={{0,8},{1,9},{2,10},{3,11},{4,12},{5,13},{6,14},{7,15},{8,0},{9,1},... | collective-permute-start | bytes 147464 | tf_op jit(solution)/shard_map/ppermute | solution.py:247
  5.4 1.3 %pad_maximum_fusion.1 = bf16[3,36864]{1,0:T(4,128)(2,1)S(1)} fusion(bf16[2,36864]{1,0:T(2,128)(2,1)} %param.10, bf16[1,36864]{1,0:T(2,128)(2,1)} %param.9), kind=kLoop, calls=%fused_computation.1 | loop fusion | flops 442368 | bytes 442368 | tf_op jit(solution)/shard_map/concatenate | solution.py:281
  6.7 0.3 reshape.13
  7.1 0.7 %copy-done = f32[128,64]{0,1:T(8,128)S(1)} copy-done((f32[128,64]{0,1:T(8,128)S(1)}, f32[128,64]{0,1:T(8,128)}, u32[]{:S(2)}) %copy-start) | copy-done | bytes 32792
  7.8 1.7 %shard_map.103 = (bf16[128,8192]{1,0:T(8,128)(2,1)S(1)}, f32[128,64]{1,0:T(8,128)S(1)}) custom-call(bf16[128,8192]{1,0:T(8,128)(2,1)} %iq_hbm, f32[64,128]{1,0:T(8,128)S(1)} %bitcast.2), custom_call_target="tpu_custom_call" | custom-call | tf_op jit(solution)/shard_map/pallas_call | solution.py:287
  9.6 1.6 %collective-permute-start.1 = (bf16[384,128]{1,0:T(8,128)(2,1)S(1)}, bf16[384,128]{1,0:T(8,128)(2,1)S(1)}, u32[]{:S(2)}, u32[]{:S(2)}) collective-permute-start(bf16[384,128]{1,0:T(8,128)(2,1)S(1)} %pad_maximum_fusion.3), channel_id=1, source_target_pairs={{0,4},{1,5},{2,6},{3,7},{4,0},{5,1},{6,2},{7,3},{8,12},{9,13},{10,... | collective-permute-start | bytes 294920 | tf_op jit(solution)/shard_map/ppermute | solution.py:247
  11.2 1.3 %collective-permute-start.7 = (bf16[192,640]{1,0:T(8,128)(2,1)S(1)}, bf16[192,640]{1,0:T(8,128)(2,1)S(1)}, u32[]{:S(2)}, u32[]{:S(2)}) collective-permute-start(bf16[192,640]{1,0:T(8,128)(2,1)S(1)} %pad.4.refs_0_), channel_id=1, source_target_pairs={{0,8},{1,9},{2,10},{3,11},{4,12},{5,13},{6,14},{7,15},{8,0},{9,1},... | collective-permute-start | bytes 737288 | tf_op jit(solution)/shard_map/ppermute | solution.py:247
  12.5 1.5 %collective-permute-start.5 = (bf16[192,640]{1,0:T(8,128)(2,1)S(1)}, bf16[192,640]{1,0:T(8,128)(2,1)S(1)}, u32[]{:S(2)}, u32[]{:S(2)}) collective-permute-start(bf16[192,640]{1,0:T(8,128)(2,1)S(1)} %pad.4.refs_0_), channel_id=1, source_target_pairs={{0,2},{1,3},{2,0},{3,1},{4,6},{5,7},{6,4},{7,5},{8,10},{9,11},{10,... | collective-permute-start | bytes 737288 | tf_op jit(solution)/shard_map/ppermute | solution.py:247
  14.0 0.1 collective-permute-start.3
  14.1 0.4 collective-permute-done.1
  14.5 2.9 %collective-permute-start.2 = (bf16[768,128]{1,0:T(8,128)(2,1)S(1)}, bf16[768,128]{1,0:T(8,128)(2,1)S(1)}, u32[]{:S(2)}, u32[]{:S(2)}) collective-permute-start(bf16[768,128]{1,0:T(8,128)(2,1)S(1)} %pad_maximum_fusion.2.keys_ref.refs_0_), channel_id=1, source_target_pairs={{0,2},{1,3},{2,0},{3,1},{4,6},{5,7},{6,4},{7,5},{8,10},{9,11},{10,... | collective-permute-start | bytes 589832 | tf_op jit(solution)/shard_map/ppermute | solution.py:247
  17.4 2.4 %shard_map.105.refs_3_ = f32[4,128,128]{2,1,0:T(8,128)S(1)} custom-call(bf16[128,8192]{1,0:T(8,128)(2,1)S(1)} %get-tuple-element.63.iq_ref, f32[128,64]{1,0:T(8,128)S(1)} %get-tuple-element.39.w_ref, bf16[768,128]{1,0:T(8,128)(2,1)S(1)} %pad_maximum_fusion.2.keys_ref.refs_0_), custom_call_target="tpu_custom_call" | custom-call | flops 4294967296 | bytes 4194304 | tf_op jit(solution)/shard_map/pallas_call | solution.py:262
  19.9 4.9 %collective-permute-done.3.refs_4_ = bf16[192,640]{1,0:T(8,128)(2,1)S(1)} collective-permute-done((bf16[192,640]{1,0:T(8,128)(2,1)S(1)}, bf16[192,640]{1,0:T(8,128)(2,1)S(1)}, u32[]{:S(2)}, u32[]{:S(2)}) %collective-permute-start.3) | collective-permute-done | bytes 245792 | tf_op jit(solution)/shard_map/ppermute | solution.py:247
  24.8 1.5 %collective-permute-start.10 = (bf16[192,640]{1,0:T(8,128)(2,1)S(1)}, bf16[192,640]{1,0:T(8,128)(2,1)S(1)}, u32[]{:S(2)}, u32[]{:S(2)}) collective-permute-start(bf16[192,640]{1,0:T(8,128)(2,1)S(1)} %collective-permute-done.3.refs_4_), channel_id=1, source_target_pairs={{0,2},{1,3},{2,0},{3,1},{4,6},{5,7},{6,4},{7,5},{8,10},{9,11},{10,... | collective-permute-start | bytes 737288 | tf_op jit(solution)/shard_map/ppermute | solution.py:247
  26.3 0.3 collective-permute-start.6
  26.6 2.4 %shard_map.104.refs_4_ = f32[4,128,128]{2,1,0:T(8,128)S(1)} custom-call(bf16[128,8192]{1,0:T(8,128)(2,1)S(1)} %get-tuple-element.63.iq_ref, f32[128,64]{1,0:T(8,128)S(1)} %get-tuple-element.39.w_ref, bf16[768,128]{1,0:T(8,128)(2,1)S(1)} %collective-permute-done.2.keys_ref.refs_1_), custom_call_target="tpu_custom_call" | custom-call | flops 4294967296 | bytes 4194304 | tf_op jit(solution)/shard_map/pallas_call | solution.py:262
  29.1 1.3 %collective-permute-start.8 = (bf16[192,640]{1,0:T(8,128)(2,1)S(1)}, bf16[192,640]{1,0:T(8,128)(2,1)S(1)}, u32[]{:S(2)}, u32[]{:S(2)}) collective-permute-start(bf16[192,640]{1,0:T(8,128)(2,1)S(1)} %collective-permute-done.7.refs_8_), channel_id=1, source_target_pairs={{0,4},{1,5},{2,6},{3,7},{4,0},{5,1},{6,2},{7,3},{8,12},{9,13},{10,... | collective-permute-start | bytes 737288 | tf_op jit(solution)/shard_map/ppermute | solution.py:247
  30.4 0.0 collective-permute-start.9
  30.4 0.5 collective-permute-start.13
  30.9 5.0 %shard_map.106.refs_5_ = f32[8,128,128]{2,1,0:T(8,128)S(1)} custom-call(bf16[128,8192]{1,0:T(8,128)(2,1)S(1)} %get-tuple-element.63.iq_ref, f32[128,64]{1,0:T(8,128)S(1)} %get-tuple-element.39.w_ref, bf16[1536,128]{1,0:T(8,128)(2,1)S(1)} %collective-permute-done.6.keys_ref.refs_2_), custom_call_target="tpu_custom_call" | custom-call | flops 8589934592 | bytes 4194304 | tf_op jit(solution)/shard_map/pallas_call | solution.py:262
  35.9 1.4 %collective-permute-done.8.refs_12_ = bf16[192,640]{1,0:T(8,128)(2,1)S(1)} collective-permute-done((bf16[192,640]{1,0:T(8,128)(2,1)S(1)}, bf16[192,640]{1,0:T(8,128)(2,1)S(1)}, u32[]{:S(2)}, u32[]{:S(2)}) %collective-permute-start.8) | collective-permute-done | bytes 245792 | tf_op jit(solution)/shard_map/ppermute | solution.py:247
  37.3 0.5 collective-permute-start.12
  37.8 0.5 collective-permute-start.17
  38.3 2.4 %shard_map.107.refs_6_ = f32[128,512]{1,0:T(8,128)S(1)} custom-call(s32[1]{0:T(128)} %bitcast.own_ref, bf16[128,8192]{1,0:T(8,128)(2,1)S(1)} %get-tuple-element.63.iq_ref, f32[128,64]{1,0:T(8,128)S(1)} %get-tuple-element.39.w_ref, bf16[768,128]{1,0:T(8,128)(2,1)S(1)} %pad_maximum_fusion.2.keys_ref.refs_0_, ...), custom_call_target="tpu_custom_call" | custom-call | flops 4294967296 | bytes 4194304 | tf_op jit(solution)/shard_map/pallas_call | solution.py:339
  40.7 0.1 collective-permute-start.14
  40.8 0.5 collective-permute-start.15
  41.3 0.1 collective-permute-start.16
  41.4 3.3 %shard_map.108 = (f32[128,1024]{1,0:T(8,128)}, f32[128,2048]{1,0:T(8,128)}) custom-call(s32[1]{0:T(128)} %bitcast.own_ref, bf16[128,8192]{1,0:T(8,128)(2,1)S(1)} %get-tuple-element.63.iq_ref, f32[128,64]{1,0:T(8,128)S(1)} %get-tuple-element.39.w_ref, bf16[768,128]{1,0:T(8,128)(2,1)S(1)} %pad_maximum_fusion.2.keys_ref.refs_0_, ...), custom_call_target="tpu_custom_call" | custom-call | flops 4294967296 | bytes 4194304 | tf_op jit(solution)/shard_map/pallas_call | solution.py:350
  44.7 1.0 %collective-permute-done.17.refs_14_ = bf16[192,640]{1,0:T(8,128)(2,1)S(1)} collective-permute-done((bf16[192,640]{1,0:T(8,128)(2,1)S(1)}, bf16[192,640]{1,0:T(8,128)(2,1)S(1)}, u32[]{:S(2)}, u32[]{:S(2)}) %collective-permute-start.17) | collective-permute-done | bytes 245792 | tf_op jit(solution)/shard_map/ppermute | solution.py:247
  45.8 1.5 %collective-permute-done.18.refs_15_ = bf16[192,640]{1,0:T(8,128)(2,1)S(1)} collective-permute-done((bf16[192,640]{1,0:T(8,128)(2,1)S(1)}, bf16[192,640]{1,0:T(8,128)(2,1)S(1)}, u32[]{:S(2)}, u32[]{:S(2)}) %collective-permute-start.18) | collective-permute-done | bytes 245792 | tf_op jit(solution)/shard_map/ppermute | solution.py:247
  47.3 22.7 %shard_map.109 = bf16[128,32768]{1,0:T(8,128)(2,1)} custom-call(s32[1]{0:T(128)} %bitcast.own_ref, s32[2,12]{1,0:T(2,128)S(1)} %copy-done.1, bf16[128,36864]{1,0:T(8,128)(2,1)} %q_ref.1, bf16[192,640]{1,0:T(8,128)(2,1)S(1)} %pad.4.refs_0_, bf16[192,640]{1,0:T(8,128)(2,1)S(1)} %collective-permute-done.4.refs_1_, ...), custom_call_target="tpu_custom_call" | custom-call | flops 14495514624 | bytes 16777216 | tf_op jit(solution)/shard_map/pallas_call | solution.py:377
  (24 shorter events, 0.1 us)
Async XLA Ops:
  1.4 8.1 %collective-permute-start = (bf16[192,128]{1,0:T(8,128)(2,1)S(1)}, bf16[192,128]{1,0:T(8,128)(2,1)S(1)}, u32[]{:S(2)}, u32[]{:S(2)}) collective-permute-start(bf16[192,128]{1,0:T(8,128)(2,1)S(1)} %pad_maximum_fusion.4), channel_id=1, source_target_pairs={{0,8},{1,9},{2,10},{3,11},{4,12},{5,13},{6,14},{7,15},{8,0},{9,1},... | collective-permute-start | bytes 147464 | tf_op jit(solution)/shard_map/ppermute | solution.py:247
  7.1 0.8 %copy-start = (f32[128,64]{0,1:T(8,128)S(1)}, f32[128,64]{0,1:T(8,128)}, u32[]{:S(2)}) copy-start(f32[128,64]{0,1:T(8,128)} %param.12) | copy-start | bytes 98308
  9.6 5.0 %collective-permute-start.1 = (bf16[384,128]{1,0:T(8,128)(2,1)S(1)}, bf16[384,128]{1,0:T(8,128)(2,1)S(1)}, u32[]{:S(2)}, u32[]{:S(2)}) collective-permute-start(bf16[384,128]{1,0:T(8,128)(2,1)S(1)} %pad_maximum_fusion.3), channel_id=1, source_target_pairs={{0,4},{1,5},{2,6},{3,7},{4,0},{5,1},{6,2},{7,3},{8,12},{9,13},{10,... | collective-permute-start | bytes 294920 | tf_op jit(solution)/shard_map/ppermute | solution.py:247
  11.2 17.9 %collective-permute-start.7 = (bf16[192,640]{1,0:T(8,128)(2,1)S(1)}, bf16[192,640]{1,0:T(8,128)(2,1)S(1)}, u32[]{:S(2)}, u32[]{:S(2)}) collective-permute-start(bf16[192,640]{1,0:T(8,128)(2,1)S(1)} %pad.4.refs_0_), channel_id=1, source_target_pairs={{0,8},{1,9},{2,10},{3,11},{4,12},{5,13},{6,14},{7,15},{8,0},{9,1},... | collective-permute-start | bytes 737288 | tf_op jit(solution)/shard_map/ppermute | solution.py:247
  12.5 16.6 %collective-permute-start.5 = (bf16[192,640]{1,0:T(8,128)(2,1)S(1)}, bf16[192,640]{1,0:T(8,128)(2,1)S(1)}, u32[]{:S(2)}, u32[]{:S(2)}) collective-permute-start(bf16[192,640]{1,0:T(8,128)(2,1)S(1)} %pad.4.refs_0_), channel_id=1, source_target_pairs={{0,2},{1,3},{2,0},{3,1},{4,6},{5,7},{6,4},{7,5},{8,10},{9,11},{10,... | collective-permute-start | bytes 737288 | tf_op jit(solution)/shard_map/ppermute | solution.py:247
  14.0 10.8 %collective-permute-start.3 = (bf16[192,640]{1,0:T(8,128)(2,1)S(1)}, bf16[192,640]{1,0:T(8,128)(2,1)S(1)}, u32[]{:S(2)}, u32[]{:S(2)}) collective-permute-start(bf16[192,640]{1,0:T(8,128)(2,1)S(1)} %pad.4.refs_0_), channel_id=1, source_target_pairs={{0,4},{1,5},{2,6},{3,7},{4,0},{5,1},{6,2},{7,3},{8,12},{9,13},{10,... | collective-permute-start | bytes 737288 | tf_op jit(solution)/shard_map/ppermute | solution.py:247
  14.5 11.8 %collective-permute-start.2 = (bf16[768,128]{1,0:T(8,128)(2,1)S(1)}, bf16[768,128]{1,0:T(8,128)(2,1)S(1)}, u32[]{:S(2)}, u32[]{:S(2)}) collective-permute-start(bf16[768,128]{1,0:T(8,128)(2,1)S(1)} %pad_maximum_fusion.2.keys_ref.refs_0_), channel_id=1, source_target_pairs={{0,2},{1,3},{2,0},{3,1},{4,6},{5,7},{6,4},{7,5},{8,10},{9,11},{10,... | collective-permute-start | bytes 589832 | tf_op jit(solution)/shard_map/ppermute | solution.py:247
  24.8 4.3 %collective-permute-start.4 = (bf16[192,640]{1,0:T(8,128)(2,1)S(1)}, bf16[192,640]{1,0:T(8,128)(2,1)S(1)}, u32[]{:S(2)}, u32[]{:S(2)}) collective-permute-start(bf16[192,640]{1,0:T(8,128)(2,1)S(1)} %pad.4.refs_0_), channel_id=1, source_target_pairs={{0,1},{1,0},{2,3},{3,2},{4,5},{5,4},{6,7},{7,6},{8,9},{9,8},{10,11... | collective-permute-start | bytes 737288 | tf_op jit(solution)/shard_map/ppermute | solution.py:247
  24.8 12.5 %collective-permute-start.10 = (bf16[192,640]{1,0:T(8,128)(2,1)S(1)}, bf16[192,640]{1,0:T(8,128)(2,1)S(1)}, u32[]{:S(2)}, u32[]{:S(2)}) collective-permute-start(bf16[192,640]{1,0:T(8,128)(2,1)S(1)} %collective-permute-done.3.refs_4_), channel_id=1, source_target_pairs={{0,2},{1,3},{2,0},{3,1},{4,6},{5,7},{6,4},{7,5},{8,10},{9,11},{10,... | collective-permute-start | bytes 737288 | tf_op jit(solution)/shard_map/ppermute | solution.py:247
  26.3 4.5 %collective-permute-start.6 = (bf16[1536,128]{1,0:T(8,128)(2,1)S(1)}, bf16[1536,128]{1,0:T(8,128)(2,1)S(1)}, u32[]{:S(2)}, u32[]{:S(2)}) collective-permute-start(bf16[1536,128]{1,0:T(8,128)(2,1)S(1)} %pad_maximum_fusion), channel_id=1, source_target_pairs={{0,1},{1,0},{2,3},{3,2},{4,5},{5,4},{6,7},{7,6},{8,9},{9,8},{10,11... | collective-permute-start | bytes 1179656 | tf_op jit(solution)/shard_map/ppermute | solution.py:247
  29.1 8.2 %collective-permute-start.8 = (bf16[192,640]{1,0:T(8,128)(2,1)S(1)}, bf16[192,640]{1,0:T(8,128)(2,1)S(1)}, u32[]{:S(2)}, u32[]{:S(2)}) collective-permute-start(bf16[192,640]{1,0:T(8,128)(2,1)S(1)} %collective-permute-done.7.refs_8_), channel_id=1, source_target_pairs={{0,4},{1,5},{2,6},{3,7},{4,0},{5,1},{6,2},{7,3},{8,12},{9,13},{10,... | collective-permute-start | bytes 737288 | tf_op jit(solution)/shard_map/ppermute | solution.py:247
  30.4 6.9 %collective-permute-start.9 = (bf16[192,640]{1,0:T(8,128)(2,1)S(1)}, bf16[192,640]{1,0:T(8,128)(2,1)S(1)}, u32[]{:S(2)}, u32[]{:S(2)}) collective-permute-start(bf16[192,640]{1,0:T(8,128)(2,1)S(1)} %collective-permute-done.5.refs_2_), channel_id=1, source_target_pairs={{0,1},{1,0},{2,3},{3,2},{4,5},{5,4},{6,7},{7,6},{8,9},{9,8},{10,11... | collective-permute-start | bytes 737288 | tf_op jit(solution)/shard_map/ppermute | solution.py:247
  30.4 10.4 %collective-permute-start.13 = (bf16[192,640]{1,0:T(8,128)(2,1)S(1)}, bf16[192,640]{1,0:T(8,128)(2,1)S(1)}, u32[]{:S(2)}, u32[]{:S(2)}) collective-permute-start(bf16[192,640]{1,0:T(8,128)(2,1)S(1)} %collective-permute-done.7.refs_8_), channel_id=1, source_target_pairs={{0,2},{1,3},{2,0},{3,1},{4,6},{5,7},{6,4},{7,5},{8,10},{9,11},{10,... | collective-permute-start | bytes 737288 | tf_op jit(solution)/shard_map/ppermute | solution.py:247
  37.3 4.0 %collective-permute-start.11 = (bf16[192,640]{1,0:T(8,128)(2,1)S(1)}, bf16[192,640]{1,0:T(8,128)(2,1)S(1)}, u32[]{:S(2)}, u32[]{:S(2)}) collective-permute-start(bf16[192,640]{1,0:T(8,128)(2,1)S(1)} %collective-permute-done.7.refs_8_), channel_id=1, source_target_pairs={{0,1},{1,0},{2,3},{3,2},{4,5},{5,4},{6,7},{7,6},{8,9},{9,8},{10,11... | collective-permute-start | bytes 737288 | tf_op jit(solution)/shard_map/ppermute | solution.py:247
  37.3 4.1 %collective-permute-start.12 = (bf16[192,640]{1,0:T(8,128)(2,1)S(1)}, bf16[192,640]{1,0:T(8,128)(2,1)S(1)}, u32[]{:S(2)}, u32[]{:S(2)}) collective-permute-start(bf16[192,640]{1,0:T(8,128)(2,1)S(1)} %collective-permute-done.3.refs_4_), channel_id=1, source_target_pairs={{0,1},{1,0},{2,3},{3,2},{4,5},{5,4},{6,7},{7,6},{8,9},{9,8},{10,11... | collective-permute-start | bytes 737288 | tf_op jit(solution)/shard_map/ppermute | solution.py:247
  37.8 7.9 %collective-permute-start.17 = (bf16[192,640]{1,0:T(8,128)(2,1)S(1)}, bf16[192,640]{1,0:T(8,128)(2,1)S(1)}, u32[]{:S(2)}, u32[]{:S(2)}) collective-permute-start(bf16[192,640]{1,0:T(8,128)(2,1)S(1)} %collective-permute-done.8.refs_12_), channel_id=1, source_target_pairs={{0,2},{1,3},{2,0},{3,1},{4,6},{5,7},{6,4},{7,5},{8,10},{9,11},{10,... | collective-permute-start | bytes 737288 | tf_op jit(solution)/shard_map/ppermute | solution.py:247
  40.7 6.5 %copy-start.1 = (s32[2,12]{1,0:T(2,128)S(1)}, s32[2,12]{1,0:T(2,128)}, u32[]{:S(2)}) copy-start(s32[2,12]{1,0:T(2,128)} %pick_ref.1) | copy-start | bytes 292
  40.7 5.0 %collective-permute-start.14 = (bf16[192,640]{1,0:T(8,128)(2,1)S(1)}, bf16[192,640]{1,0:T(8,128)(2,1)S(1)}, u32[]{:S(2)}, u32[]{:S(2)}) collective-permute-start(bf16[192,640]{1,0:T(8,128)(2,1)S(1)} %collective-permute-done.10.refs_6_), channel_id=1, source_target_pairs={{0,1},{1,0},{2,3},{3,2},{4,5},{5,4},{6,7},{7,6},{8,9},{9,8},{10,11... | collective-permute-start | bytes 737288 | tf_op jit(solution)/shard_map/ppermute | solution.py:247
  40.8 4.9 %collective-permute-start.15 = (bf16[192,640]{1,0:T(8,128)(2,1)S(1)}, bf16[192,640]{1,0:T(8,128)(2,1)S(1)}, u32[]{:S(2)}, u32[]{:S(2)}) collective-permute-start(bf16[192,640]{1,0:T(8,128)(2,1)S(1)} %collective-permute-done.13.refs_10_), channel_id=1, source_target_pairs={{0,1},{1,0},{2,3},{3,2},{4,5},{5,4},{6,7},{7,6},{8,9},{9,8},{10,11... | collective-permute-start | bytes 737288 | tf_op jit(solution)/shard_map/ppermute | solution.py:247
  41.3 4.4 %collective-permute-start.16 = (bf16[192,640]{1,0:T(8,128)(2,1)S(1)}, bf16[192,640]{1,0:T(8,128)(2,1)S(1)}, u32[]{:S(2)}, u32[]{:S(2)}) collective-permute-start(bf16[192,640]{1,0:T(8,128)(2,1)S(1)} %collective-permute-done.8.refs_12_), channel_id=1, source_target_pairs={{0,1},{1,0},{2,3},{3,2},{4,5},{5,4},{6,7},{7,6},{8,9},{9,8},{10,11... | collective-permute-start | bytes 737288 | tf_op jit(solution)/shard_map/ppermute | solution.py:247
  45.7 1.5 %collective-permute-start.18 = (bf16[192,640]{1,0:T(8,128)(2,1)S(1)}, bf16[192,640]{1,0:T(8,128)(2,1)S(1)}, u32[]{:S(2)}, u32[]{:S(2)}) collective-permute-start(bf16[192,640]{1,0:T(8,128)(2,1)S(1)} %collective-permute-done.17.refs_14_), channel_id=1, source_target_pairs={{0,1},{1,0},{2,3},{3,2},{4,5},{5,4},{6,7},{7,6},{8,9},{9,8},{10,11... | collective-permute-start | bytes 737288 | tf_op jit(solution)/shard_map/ppermute | solution.py:247
